TPU v7x, 256 devices: a whole 4x4x8 slice. The times are simulated.
256 devices in a mesh: samp: 64 (over x, z_hi, y, core), tok: 4 (over z_lo).
Axes of the slice: x: 4, y: 4, z: 8 (z_hi: 2, z_lo: 4; z = z_hi * 4 + z_lo), core: 2. Of those that a mesh axis runs over, the one named last changes fastest.
Arguments:
- inputs: bfloat16 [64, 512, 768], P('samp', 'tok'), may hold values from -6 to 6
- cotangent: bfloat16 [64, 512, 768], P('samp', 'tok'), may hold values from -6 to 6
- layer_norm_scale: float32 [768], replicated, may hold values from 0.25 to 1.75
- query_weight: bfloat16 [768, 768], P('samp'), may hold values from -0.3125 to 0.3125
- key_weight: bfloat16 [768, 768], P('samp'), may hold values from -0.3125 to 0.3125
- value_weight: bfloat16 [768, 768], P('samp'), may hold values from -0.21875 to 0.21875
- gate_weight: bfloat16 [768, 768], P('samp'), may hold values from -0.21875 to 0.21875
- out_weight: bfloat16 [768, 768], P('samp'), may hold values from -0.21875 to 0.21875
- pair_bias: bfloat16 [16, 512, 512], P(None, 'tok'), may hold values from -2 to 230
- atom_count: int32 [512], replicated, may hold values from 0 to 7
Outputs:
- input_grad: bfloat16 [64, 512, 768], P('samp', 'tok')
- bias_grad: float32 [16, 512, 512], P(None, 'tok', 'samp')
All inputs are finite; a program needn't handle non-finite values.
Results may differ from a plain program's by a relative error of at most 0.019.
Values may be sent and summed in bfloat16 or wider, within the bound.
No kernel may reach another device: no remote copies, remote signals or barrier semaphores. Data moves between devices by JAX's collectives and lax.ppermute only.
A program may use at most 128 MiB of HBM per device.

v0:
```python
import jax
import jax.numpy as jnp
from jax import lax
from jax.sharding import PartitionSpec as P

GROUP = 4


def project(matrix, weight):
    return jnp.einsum("sqd,de->sqe", matrix, weight, preferred_element_type=jnp.float32).astype(
        jnp.bfloat16
    )


def back_project(matrix, weight):
    return jnp.einsum("sqe,de->sqd", matrix, weight, preferred_element_type=jnp.float32)


def on_device(
    inputs,
    cotangent,
    layer_norm_scale,
    query_weight,
    key_weight,
    value_weight,
    gate_weight,
    out_weight,
    pair_bias,
    atom_count,
):
    full_query, full_key, full_value, full_gate, full_out = (
        lax.all_gather(query_weight, "samp", axis=0, tiled=True),
        lax.all_gather(key_weight, "samp", axis=0, tiled=True),
        lax.all_gather(value_weight, "samp", axis=0, tiled=True),
        lax.all_gather(gate_weight, "samp", axis=0, tiled=True),
        lax.all_gather(out_weight, "samp", axis=0, tiled=True),
    )
    samples, rows, width = inputs.shape
    heads = pair_bias.shape[0]
    total = pair_bias.shape[2]
    head_size = width // heads
    scale = float(head_size) ** (-0.5)
    xf = inputs.astype(jnp.float32)
    row_average = jnp.mean(xf, axis=-1, keepdims=True)
    centered_rows = xf - row_average
    inverse_deviation = lax.rsqrt(
        jnp.mean(centered_rows * centered_rows, axis=-1, keepdims=True) + 1e-05
    )
    standardized_input = centered_rows * inverse_deviation
    normed_output = (standardized_input * layer_norm_scale).astype(jnp.bfloat16)
    query = project(normed_output, full_query)
    gate_pre = project(normed_output, full_gate)
    keys, values = (
        lax.all_gather(project(normed_output, full_key), "tok", axis=1, tiled=True),
        lax.all_gather(project(normed_output, full_value), "tok", axis=1, tiled=True),
    )
    d_gated = back_project(cotangent, full_out)
    sigma = jax.nn.sigmoid(gate_pre.astype(jnp.float32))
    d_attn = (d_gated * sigma).astype(jnp.bfloat16)
    valid = (atom_count > 0)[None, None, None, :]
    query_heads = query.reshape(samples, rows, heads, head_size)
    key_heads = keys.reshape(samples, total, heads, head_size)
    value_heads = values.reshape(samples, total, heads, head_size)
    dattn_heads = d_attn.reshape(samples, rows, heads, head_size)
    bias_parts = []
    attended_parts = []
    dquery_parts = []
    dkey_parts = []
    dvalue_parts = []
    for group in range(heads // GROUP):
        lower = group * GROUP
        query_group = query_heads[:, :, lower : lower + GROUP]
        key_group = key_heads[:, :, lower : lower + GROUP]
        value_group = value_heads[:, :, lower : lower + GROUP]
        dattn_group = dattn_heads[:, :, lower : lower + GROUP]
        scores = (
            jnp.einsum(
                "sqhe,skhe->shqk", query_group, key_group, preferred_element_type=jnp.float32
            )
            * scale
        )
        scores = scores + pair_bias[lower : lower + GROUP].astype(jnp.float32)[None]
        scores = jnp.where(valid, scores, -1000000000.0)
        probs = jax.nn.softmax(scores, axis=-1)
        probs_b = probs.astype(jnp.bfloat16)
        attended = jnp.einsum(
            "shqk,skhe->sqhe", probs_b, value_group, preferred_element_type=jnp.float32
        ).astype(jnp.bfloat16)
        delta = jnp.sum(dattn_group.astype(jnp.float32) * attended.astype(jnp.float32), axis=-1)
        d_prob = jnp.einsum(
            "sqhe,skhe->shqk", dattn_group, value_group, preferred_element_type=jnp.float32
        )
        d_score = probs * (d_prob - jnp.transpose(delta, (0, 2, 1))[..., None])
        partial_bias = jnp.sum(d_score, axis=0)
        bias_parts.append(partial_bias)
        d_score_b = d_score.astype(jnp.bfloat16)
        dquery_parts.append(
            (
                jnp.einsum(
                    "shqk,skhe->sqhe", d_score_b, key_group, preferred_element_type=jnp.float32
                )
                * scale
            ).astype(jnp.bfloat16)
        )
        dkey_parts.append(
            jnp.einsum(
                "shqk,sqhe->skhe", d_score_b, query_group, preferred_element_type=jnp.float32
            )
            * scale
        )
        dvalue_parts.append(
            jnp.einsum("shqk,sqhe->skhe", probs_b, dattn_group, preferred_element_type=jnp.float32)
        )
        attended_parts.append(attended)
    attended_all = jnp.concatenate(attended_parts, axis=2).reshape(samples, rows, width)
    d_query = jnp.concatenate(dquery_parts, axis=2).reshape(samples, rows, width)
    d_keys_part = jnp.concatenate(dkey_parts, axis=2).reshape(samples, total, width)
    d_values_part = jnp.concatenate(dvalue_parts, axis=2).reshape(samples, total, width)
    d_gate = (d_gated * attended_all.astype(jnp.float32) * sigma * (1.0 - sigma)).astype(
        jnp.bfloat16
    )
    d_normed = back_project(d_query, full_query) + back_project(d_gate, full_gate)
    d_keys, d_values = (
        lax.psum_scatter(
            d_keys_part.astype(jnp.bfloat16), "tok", scatter_dimension=1, tiled=True
        ).astype(jnp.float32),
        lax.psum_scatter(
            d_values_part.astype(jnp.bfloat16), "tok", scatter_dimension=1, tiled=True
        ).astype(jnp.float32),
    )
    d_normed = (
        d_normed
        + back_project(d_keys.astype(jnp.bfloat16), full_key)
        + back_project(d_values.astype(jnp.bfloat16), full_value)
    )
    upstream_gradient = d_normed * layer_norm_scale
    final_output = inverse_deviation * (
        upstream_gradient
        - jnp.mean(upstream_gradient, axis=-1, keepdims=True)
        - standardized_input
        * jnp.mean(upstream_gradient * standardized_input, axis=-1, keepdims=True)
    )
    bias_grad = lax.psum_scatter(
        jnp.concatenate(bias_parts, axis=0), "samp", scatter_dimension=2, tiled=True
    )
    return (final_output.astype(jnp.bfloat16), bias_grad)


def solution(mesh):
    return jax.shard_map(
        on_device,
        mesh=mesh,
        in_specs=(
            P("samp", "tok", None),
            P("samp", "tok", None),
            P(),
            P("samp", None),
            P("samp", None),
            P("samp", None),
            P("samp", None),
            P("samp", None),
            P(None, "tok", None),
            P(),
        ),
        out_specs=(P("samp", "tok", None), P(None, "tok", "samp")),
        check_vma=False,
    )
```

profile of v0, /device:TPU:1, one launch (start us, length us, event | category | flops | bytes accessed | tf_op | source)
XLA Modules:
  0.0 922.8 jit_solution(9651932414486584392)
XLA Ops:
  11.3 1.0 convert_reduce_fusion
  12.3 1.1 fusion.68
  13.5 82.4 %all-gather.15.cloned.1.call-done = bf16[64,12,768]{2,1,0:T(8,128)(2,1)} async-done(((bf16[1,12,768]{2,1,0:T(8,128)(2,1)}), bf16[64,12,768]{2,1,0:T(8,128)(2,1)}) %all-gather.15.cloned.1.call-update) | async-done | bytes 1179664 | tf_op jit(solution)/shard_map/all_gather | solution.py:32
  95.9 2.2 reshape.438
  98.6 0.8 copy.37
  99.4 74.0 %all-gather.13.cloned.1.call-done = bf16[64,12,768]{2,1,0:T(8,128)(2,1)} async-done(((bf16[1,12,768]{2,1,0:T(8,128)(2,1)}), bf16[64,12,768]{2,1,0:T(8,128)(2,1)}) %all-gather.13.cloned.1.call-update) | async-done | bytes 1179664 | tf_op jit(solution)/shard_map/all_gather | solution.py:33
  173.4 2.2 reshape.436
  176.1 16.9 %all-gather = bf16[512,768]{1,0:T(8,128)(2,1)S(1)} all-gather(bf16[128,768]{1,0:T(8,128)(2,1)S(1)} %convolution_convert_fusion.7), channel_id=2, replica_groups=mesh['samp'=64,'tok'=4] {'tok'}, dimensions={0}, use_global_device_ids=true | all-gather | bytes 983040 | tf_op jit(solution)/shard_map/all_gather | solution.py:54
  193.3 57.6 %all-gather.21.cloned.1.call-done = bf16[64,12,768]{2,1,0:T(8,128)(2,1)} async-done(((bf16[1,12,768]{2,1,0:T(8,128)(2,1)}), bf16[64,12,768]{2,1,0:T(8,128)(2,1)}) %all-gather.21.cloned.1.call-update) | async-done | bytes 1179664 | tf_op jit(solution)/shard_map/all_gather | solution.py:34
  250.9 2.2 reshape.444
  253.2 75.1 %all-gather.19.cloned.1.call-done = bf16[64,12,768]{2,1,0:T(8,128)(2,1)} async-done(((bf16[1,12,768]{2,1,0:T(8,128)(2,1)}), bf16[64,12,768]{2,1,0:T(8,128)(2,1)}) %all-gather.19.cloned.1.call-update) | async-done | bytes 1179664 | tf_op jit(solution)/shard_map/all_gather | solution.py:35
  328.2 3.2 reshape.442
  331.4 1.1 convolution_convert_fusion.4
  332.7 1.2 fusion.29
  333.8 3.1 fusion.119
  337.0 3.2 fusion.118
  340.1 2.5 fusion.117
  342.7 3.1 fusion.116
  345.8 59.8 %all-gather.17.cloned.1.call-done = bf16[64,12,768]{2,1,0:T(8,128)(2,1)} async-done(((bf16[1,12,768]{2,1,0:T(8,128)(2,1)}), bf16[64,12,768]{2,1,0:T(8,128)(2,1)}) %all-gather.17.cloned.1.call-update) | async-done | bytes 1179664 | tf_op jit(solution)/shard_map/all_gather | solution.py:36
  405.5 3.1 reshape.440
  408.7 2.6 multiply_convert_fusion.1
  412.1 16.4 %all-gather.1 = bf16[512,768]{1,0:T(8,128)(2,1)S(1)} all-gather(bf16[128,768]{1,0:T(8,128)(2,1)} %convolution_convert_fusion.4), channel_id=3, replica_groups=mesh['samp'=64,'tok'=4] {'tok'}, dimensions={0}, use_global_device_ids=true | all-gather | bytes 983040 | tf_op jit(solution)/shard_map/all_gather | solution.py:55
  428.4 1.2 copy.39
  429.6 1.5 fusion.62
  431.9 0.9 copy-done.24
  434.2 0.9 multiply_reduce_fusion.3
  438.8 1.0 pad_maximum_fusion.1
  439.8 4.8 copy.43
  444.6 2.4 copy.52
  447.3 1.3 fusion.40
  449.2 3.0 copy.45
  452.2 2.4 copy.51
  454.9 4.8 pad_maximum_fusion
  459.6 5.5 copy.41
  465.1 1.0 pad_maximum_fusion.4
  466.1 0.8 bitcast_convert_fusion
  466.9 1.9 copy.40
  468.9 1.6 fusion.52
  470.5 1.6 fusion.53
  474.9 1.1 reshape_bitcast_fusion.1
  476.0 1.0 copy.44
  477.0 24.6 %reduce-scatter.12.cloned.1.call-done = bf16[128,768]{1,0:T(8,128)(2,1)} async-done(((bf16[512,768]{1,0:T(8,128)(2,1)}), bf16[128,768]{1,0:T(8,128)(2,1)}) %reduce-scatter.12.cloned.1.call-update) | async-done | bytes 196624
  501.6 1.1 reshape_bitcast_fusion
  502.8 1.0 copy.46
  503.8 1.5 convolution_add_fusion.1
  506.0 0.9 fusion.67
  506.9 407.6 %reduce-scatter.8.cloned.1.call-done = f32[16,128,8]{1,0,2:T(8,128)} async-done(((f32[16,128,512]{1,0,2:T(8,128)}), f32[16,128,8]{1,0,2:T(8,128)}) %reduce-scatter.8.cloned.1.call-update) | async-done | bytes 65552 | tf_op jit(solution)/shard_map/reduce_scatter | solution.py:143
  914.5 1.5 copy.42
  (127 shorter events, 16.1 us)
Async XLA Ops:
  7.2 401.5 %copy-start = (bf16[1,128,768]{2,1,0:T(8,128)(2,1)S(1)}, bf16[1,128,768]{2,1,0:T(8,128)(2,1)}, u32[]{:S(2)}) copy-start(bf16[1,128,768]{2,1,0:T(8,128)(2,1)} %param.11) | copy-start | bytes 589828
  7.2 88.8 %all-gather.15.cloned.1.call-start = ((), (), s32[]{:S(2)}) async-start(), calls=%async_computation.5 | async-start | bytes 1597440 | tf_op jit(solution)/shard_map/all_gather | solution.py:32
  7.9 165.5 %all-gather.13.cloned.1.call-start = ((), (), s32[]{:S(2)}) async-start(), calls=%async_computation.4 | async-start | bytes 1597440 | tf_op jit(solution)/shard_map/all_gather | solution.py:33
  8.7 242.2 %all-gather.21.cloned.1.call-start = ((), (), s32[]{:S(2)}) async-start(), calls=%async_computation.8 | async-start | bytes 1597440 | tf_op jit(solution)/shard_map/all_gather | solution.py:34
  9.4 318.8 %all-gather.19.cloned.1.call-start = ((), (), s32[]{:S(2)}) async-start(), calls=%async_computation.7 | async-start | bytes 1597440 | tf_op jit(solution)/shard_map/all_gather | solution.py:35
  10.0 395.6 %all-gather.17.cloned.1.call-start = ((), (), s32[]{:S(2)}) async-start(), calls=%async_computation.6 | async-start | bytes 1597440 | tf_op jit(solution)/shard_map/all_gather | solution.py:36
  10.6 464.3 %reduce-scatter.10.cloned.1.call-start = ((), (), s32[]{:S(2)}) async-start(), calls=%async_computation.9 | async-start | bytes 983040
  11.3 325.7 %copy-start.38 = (pred[512]{0:T(512)(128)(4,1)}, pred[512]{0:T(512)(128)(4,1)S(1)}, u32[]{:S(2)}) copy-start(pred[512]{0:T(512)(128)(4,1)S(1)} %broadcast_compare_fusion) | copy-start | bytes 1540
  13.5 84.7 %copy-start.3 = (bf16[1,128,768]{2,1,0:T(8,128)(2,1)S(1)}, bf16[1,128,768]{2,1,0:T(8,128)(2,1)}, u32[]{:S(2)}) copy-start(bf16[1,128,768]{2,1,0:T(8,128)(2,1)} %param.10) | copy-start | bytes 589828
  13.5 84.7 %copy-start.34 = (f32[768]{0:T(1024)S(1)}, f32[768]{0:T(1024)}, u32[]{:S(2)}) copy-start(f32[768]{0:T(1024)} %param.12) | copy-start | bytes 9220
  98.2 1.2 copy-start.1
  193.3 149.4 %copy-start.15 = (bf16[512,768]{0,1:T(8,128)(2,1)}, bf16[512,768]{0,1:T(8,128)(2,1)S(1)}, u32[]{:S(2)}) copy-start(bf16[512,768]{0,1:T(8,128)(2,1)S(1)} %copy.36) | copy-start | bytes 2359300
  331.4 1.3 copy-start.10
  345.8 62.9 %copy-start.20 = (f32[128,768]{1,0:T(8,128)S(1)}, f32[128,768]{1,0:T(8,128)}, u32[]{:S(2)}) copy-start(f32[128,768]{1,0:T(8,128)} %fusion.29) | copy-start | bytes 1179652
  429.6 1.5 copy-start.17
  429.6 1.8 copy-start.25
  429.6 1.8 copy-start.35
  431.4 2.1 copy-start.31
  431.4 1.5 copy-start.24
  431.6 1.7 copy-start.12
  431.9 1.7 copy-start.32
  431.9 1.4 copy-start.27
  431.9 1.4 copy-start.37
  433.0 2.0 copy-start.13
  433.0 1.1 copy-start.29
  433.3 1.7 copy-start.33
  433.4 1.7 copy-start.26
  433.4 1.7 copy-start.36
  433.5 1.5 copy-start.18
  435.5 3.1 copy-start.4
  435.8 2.0 copy-start.6
  436.2 1.4 copy-start.8
  436.2 1.1 copy-start.28
  437.4 1.0 copy-start.9
  447.0 54.6 %reduce-scatter.12.cloned.1.call-start = ((), (), s32[]{:S(2)}) async-start(), calls=%async_computation.10 | async-start | bytes 983040
  447.1 1.6 copy-start.14
  447.1 1.8 copy-start.19
  454.6 459.9 %reduce-scatter.8.cloned.1.call-start = ((), (), s32[]{:S(2)}) async-start(), calls=%async_computation.3 | async-start | bytes 4259840 | tf_op jit(solution)/shard_map/reduce_scatter | solution.py:143
  465.1 3.7 copy-start.16
  468.9 3.2 copy-start.7
  470.5 1.9 copy-start.5
  472.1 1.3 copy-start.2
  472.4 1.5 copy-start.23
  472.7 1.4 copy-start.11
  472.8 1.5 copy-start.21
  472.8 1.6 copy-start.22
  503.8 1.5 copy-start.30
Sparse Core Ops, SparseCore 0:
  11.7 84.2 all-gather.14
  99.6 73.7 all-gather.12
  177.1 73.7 all-gather.20
  254.4 73.7 all-gather.18
  331.7 73.7 all-gather.16
  447.2 23.5 reduce-scatter.9
  473.3 28.2 reduce-scatter.11
  504.1 410.3 reduce-scatter.7
where the time goes:
time: 932 us; the launch traced here: 923 us
  waiting for transfers between devices  784 us (84%)
  local copies, waits for them, and re-layouts  46.1 us (5%)
  blocking collectives  33.3 us (4%)
  matrix products  30.5 us (3%)
  between operations  14.9 us (2%)
  other arithmetic  13.4 us (1%)
    reduce_scatter x1, waiting for transfers between devices, on_device(): lax.psum_scatter(jnp.concatenate(bias_parts, axis=0), 'samp', scatter_dim...  408 us
    all_gather x1, waiting for transfers between devices, on_device(): lax.all_gather(query_weight, 'samp', axis=0, tiled=True)  82.4 us
    all_gather x1, waiting for transfers between devices, on_device(): lax.all_gather(gate_weight, 'samp', axis=0, tiled=True)  75.1 us
    all_gather x1, waiting for transfers between devices, on_device(): lax.all_gather(key_weight, 'samp', axis=0, tiled=True)  74 us
    all_gather x1, waiting for transfers between devices, on_device(): lax.all_gather(out_weight, 'samp', axis=0, tiled=True)  59.8 us
    all_gather x1, waiting for transfers between devices, on_device(): lax.all_gather(value_weight, 'samp', axis=0, tiled=True)  57.6 us
    unnamed x92, local copies, waits for them, and re-layouts  35.6 us
    unnamed x10, waiting for transfers between devices  27.8 us
  transfers between devices with their start and end apart: 8, of which 7 were waited for; matrix products, arithmetic and copies ran while one was open for 7% of the time, Pallas kernels for 0%

commit v1 on v0

v1 whole, which is shorter than its diff:
```python
import jax
import jax.numpy as jnp
from jax import lax
from jax.experimental import pallas as pl
from jax.experimental.pallas import tpu as pltpu
from jax.sharding import Mesh, PartitionSpec as P

AXES = (("x", 4), ("zh", 2), ("y", 4), ("core", 2))
NX, NZ, NY, NC = 4, 2, 4, 2
NT = 4
BF = jnp.bfloat16
F32 = jnp.float32
NEG = -1000000000.0


def shift(value, axis, count, by):
    return lax.ppermute(value, axis, [(i, (i + by) % count) for i in range(count)])


def nt(a, b):
    return lax.dot_general(a, b, (((1,), (1,)), ((), ())), preferred_element_type=F32)


def nn(a, b):
    return lax.dot_general(a, b, (((1,), (0,)), ((), ())), preferred_element_type=F32)


def attention_kernel(
    pos,
    own0, own1, own2, own3,
    oth0, oth1, oth2, oth3,
    cot_own, cot_oth,
    a0, a1, a2, a3,
    b0, b1, b2, b3,
    bias, valid_row, valid_col,
    out_own, out_oth, out_bias,
    wf, wb, dgt, kk, vv, kt, vt, qt, gt, dx, dq, dg, grad,
):
    heads = bias.shape[0] // NC
    width = own0.shape[1]
    half = width // NC
    size = half // heads
    rows = own0.shape[0]
    scale = float(size) ** (-0.5)
    x, y, core, tok = pos[0], pos[1], pos[2], pos[3]
    rx, rz, ry = width // NX, width // (NX * NZ), width // (NX * NZ * NY)
    piece = NZ * ry

    for m, (a, b) in enumerate(zip((a0, a1, a2, a3), (b0, b1, b2, b3))):
        for k in range(4):
            rows_a = a[k * piece:(k + 1) * piece, :].astype(F32)
            rows_b = b[k * piece:(k + 1) * piece, :half].astype(F32)
            for z in range(NZ):
                at_a = lax.rem(x - k + 4, 4) * rx + z * rz + lax.rem(y - m + 4, 4) * ry
                wf[pl.ds(pl.multiple_of(at_a, 8), ry), : 3 * half] = rows_a[z * ry:(z + 1) * ry]
                at_b = lax.rem(x - m + 4, 4) * rx + z * rz + lax.rem(y - k + 4, 4) * ry
                wf[pl.ds(pl.multiple_of(at_b, 8), ry), 3 * half:] = rows_b[z * ry:(z + 1) * ry]
    wb[...] = wf[...].astype(BF)

    for s, cot in enumerate((cot_own, cot_oth)):
        for m, b in enumerate((b0, b1, b2, b3)):
            part = nt(b[:, half:], cot[...])
            for k in range(4):
                for z in range(NZ):
                    at = lax.rem(x - m + 4, 4) * rx + z * rz + lax.rem(y - k + 4, 4) * ry
                    dgt[s, pl.ds(pl.multiple_of(at, 8), ry), :] = part[k * piece + z * ry:k * piece + (z + 1) * ry]

    for s, blocks in enumerate(((own0, own1, own2, own3), (oth0, oth1, oth2, oth3))):
        for r, block in enumerate(blocks):
            lo = r * rows
            n = block[...]
            k_f = nn(n, wb[:, half:2 * half])
            v_f = nn(n, wb[:, 2 * half:3 * half])
            kt[s, :, lo:lo + rows] = k_f.T.astype(BF)
            vt[s, :, lo:lo + rows] = v_f.T.astype(BF)
            at = pl.multiple_of(lax.rem(tok - r + 4, 4) * rows, rows)
            keep = valid_col[pl.ds(at, rows), :]
            for j in range(half // 128):
                kk[s, lo:lo + rows, j * 128:(j + 1) * 128] = (k_f[:, j * 128:(j + 1) * 128] * keep).astype(BF)
            vv[s, lo:lo + rows, :] = v_f.astype(BF)
        n = blocks[0][...]
        qt[s] = nn(n, wb[:, :half]).T.astype(BF)
        gate = nn(n, wb[:, 3 * half:]).T.astype(BF).astype(F32)
        gt[s] = jax.nn.sigmoid(gate)

    for h in range(heads):
        first = h * size
        w_lo = first // 128 * 128
        w_hi = -(-(first + size) // 128) * 128
        above, below = first - w_lo, w_hi - first - size

        def widen(block):
            parts = [block]
            if above:
                parts = [jnp.zeros((above, rows), BF)] + parts
            if below:
                parts = parts + [jnp.zeros((below, rows), BF)]
            return jnp.concatenate(parts, axis=0) if len(parts) > 1 else block

        masked = jnp.where(valid_row[...] > 0.0, bias[core * heads + h].astype(F32), NEG)
        grad[...] = masked.T
        bias_t = jnp.concatenate(
            [grad[pl.ds(pl.multiple_of(lax.rem(tok - r + 4, 4) * rows, rows), rows), :] for r in range(NT)], axis=0
        )
        total = None
        for s in range(2):
            q_h = qt[s, first:first + size, :]
            dgated = dgt[s, pl.ds(pl.multiple_of(core * half + first, 8), size), :]
            sig = gt[s, first:first + size, :]
            da_h = (dgated * sig).astype(BF)
            scores = nn(kk[s, :, w_lo:w_hi], widen(q_h)) * scale + bias_t
            top = jnp.max(scores, axis=0, keepdims=True)
            e = jnp.exp(scores - top)
            probs = e / jnp.sum(e, axis=0, keepdims=True)
            probs_b = probs.astype(BF)
            att = nn(vt[s, first:first + size, :], probs_b).astype(BF).astype(F32)
            delta = jnp.sum(da_h.astype(F32) * att, axis=0, keepdims=True)
            d_prob = nn(vv[s, :, w_lo:w_hi], widen(da_h))
            d_score = probs * (d_prob - delta)
            total = d_score if total is None else total + d_score
            ds_b = d_score.astype(BF)
            dq[s, first:first + size, :] = (nn(kt[s, first:first + size, :], ds_b) * scale).astype(BF)
            dx[s, first:first + size, :] = (nt(q_h, ds_b) * scale).astype(BF)
            dx[s, half + first:half + first + size, :] = nt(da_h, probs_b).astype(BF)
            dg[s, first:first + size, :] = (dgated * att * sig * (1.0 - sig)).astype(BF)
        for r in range(NT):
            to_x = lax.rem(tok - r + 4, 4)
            for z in range(NZ):
                for to_y in range(NY):
                    lo = r * rows + z * (rows // NZ) + to_y * (rows // (NZ * NY))
                    out_bias[to_x * NY + to_y, h, z] = total[lo:lo + rows // (NZ * NY), :].astype(BF)

    for s, out in enumerate((out_own, out_oth)):
        for r in range(NT):
            lo = r * rows
            d = nn(wb[:, half:3 * half], dx[s, :, lo:lo + rows])
            if r == 0:
                d = d + nn(wb[:, :half], dq[s]) + nn(wb[:, 3 * half:], dg[s])
            out[r] = d.astype(out.dtype)


def final_kernel(inputs, gain, d_own, d_oth, r1, r2, r3, out):
    d = d_own[...] + d_oth[...].astype(F32)
    d = d + r1[...].astype(F32) + r2[...].astype(F32) + r3[...].astype(F32)
    g = d.T * gain[...]
    xf = inputs[...].astype(F32)
    mean = jnp.mean(xf, axis=-1, keepdims=True)
    centered = xf - mean
    inv = lax.rsqrt(jnp.mean(centered * centered, axis=-1, keepdims=True) + 1e-05)
    xhat = centered * inv
    res = inv * (g - jnp.mean(g, axis=-1, keepdims=True) - xhat * jnp.mean(g * xhat, axis=-1, keepdims=True))
    out[...] = res.astype(BF)


def on_device(
    inputs,
    cotangent,
    layer_norm_scale,
    query_weight,
    key_weight,
    value_weight,
    gate_weight,
    out_weight,
    pair_bias,
    atom_count,
):
    x, zh, y, core, tok = (lax.axis_index(a) for a in ("x", "zh", "y", "core", "tok"))
    inputs, cotangent = inputs[0], cotangent[0]
    rows, width = inputs.shape
    half = width // NC
    heads = pair_bias.shape[0] // NC
    total = pair_bias.shape[2]

    four = (query_weight, key_weight, value_weight, gate_weight)
    low = jnp.concatenate([w[:, :half] for w in four] + [out_weight], axis=1)
    high = jnp.concatenate([w[:, half:] for w in four] + [out_weight], axis=1)
    mine = jnp.where(core == 0, low, high)
    his = shift(jnp.where(core == 0, high, low), "core", NC, 1)
    pair = jnp.where(core == 0, jnp.stack([mine, his]), jnp.stack([his, mine]))
    far = shift(pair, "zh", NZ, 1)
    quad = jnp.where(zh == 0, jnp.stack([pair, far]), jnp.stack([far, pair]))
    quad = quad.reshape(-1, quad.shape[-1])
    part_a, part_b = quad[:, : 3 * half], quad[:, 3 * half:]
    row_a = jnp.concatenate([part_a] + [shift(part_a, "x", NX, k) for k in (1, 2, 3)], axis=0)
    row_b = jnp.concatenate([part_b] + [shift(part_b, "y", NY, k) for k in (1, 2, 3)], axis=0)
    all_a = [row_a] + [shift(row_a, "y", NY, k) for k in (1, 2, 3)]
    all_b = [row_b] + [shift(row_b, "x", NX, k) for k in (1, 2, 3)]

    xf = inputs.astype(F32)
    mean = jnp.mean(xf, axis=-1, keepdims=True)
    centered = xf - mean
    inv = lax.rsqrt(jnp.mean(centered * centered, axis=-1, keepdims=True) + 1e-05)
    normed = (centered * inv * layer_norm_scale).astype(BF)
    own = [normed] + [shift(normed, "tok", NT, k) for k in (1, 2, 3)]
    oth = [shift(n, "core", NC, 1) for n in own]
    cot_oth = shift(cotangent, "core", NC, 1)

    valid = (atom_count > 0).astype(F32)
    pos = jnp.stack([x, y, core, tok]).astype(jnp.int32)
    vmem = pl.BlockSpec(memory_space=pltpu.VMEM)
    operands = own + oth + [cotangent, cot_oth] + all_a + all_b
    operands += [pair_bias, valid[None, :], jnp.broadcast_to(valid[:, None], (total, 128))]
    out_own, out_oth, out_bias = pl.pallas_call(
        attention_kernel,
        out_shape=(
            jax.ShapeDtypeStruct((NT, width, rows), F32),
            jax.ShapeDtypeStruct((NT, width, rows), BF),
            jax.ShapeDtypeStruct((NX * NY, heads, NZ, rows // (NZ * NY), rows), BF),
        ),
        in_specs=[pl.BlockSpec(memory_space=pltpu.SMEM)] + [vmem] * len(operands),
        out_specs=(vmem, vmem, vmem),
        scratch_shapes=[
            pltpu.VMEM((width, 4 * half), F32),
            pltpu.VMEM((width, 4 * half), BF),
            pltpu.VMEM((2, width, rows), F32),
            pltpu.VMEM((2, total, half), BF),
            pltpu.VMEM((2, total, half), BF),
            pltpu.VMEM((2, half, total), BF),
            pltpu.VMEM((2, half, total), BF),
            pltpu.VMEM((2, half, rows), BF),
            pltpu.VMEM((2, half, rows), F32),
            pltpu.VMEM((2, 2 * half, total), BF),
            pltpu.VMEM((2, half, rows), BF),
            pltpu.VMEM((2, half, rows), BF),
            pltpu.VMEM((total, rows), F32),
        ],
        compiler_params=pltpu.CompilerParams(vmem_limit_bytes=50 * 1024 * 1024),
        name="attention",
    )(pos, *operands)

    d_oth = shift(out_oth, "core", NC, 1)
    back = [
        lax.ppermute(
            (out_own[k] + d_oth[k].astype(F32)).astype(BF), "tok", [(i, (i - k) % NT) for i in range(NT)]
        )
        for k in (1, 2, 3)
    ]

    parts = lax.all_to_all(out_bias, ("x", "y"), 0, 0, tiled=True)
    plane = jnp.sum(parts.astype(F32), axis=0)
    keep = jnp.where(zh == 0, plane[:, 0], plane[:, 1])
    send = jnp.where(zh == 0, plane[:, 1], plane[:, 0])
    summed = keep + shift(send, "zh", NZ, 1)
    per = summed.shape[1] // NC
    keep = jnp.where(core == 0, summed[:, :per], summed[:, per:])
    got = shift(jnp.where(core == 0, summed[:, per:], summed[:, :per]), "core", NC, 1)
    grads = jnp.where(core == 0, jnp.concatenate([keep, got]), jnp.concatenate([got, keep]))
    bias_grad = jnp.transpose(grads, (0, 2, 1))

    input_grad = pl.pallas_call(
        final_kernel,
        out_shape=jax.ShapeDtypeStruct((rows, width), BF),
        in_specs=[vmem] * 7,
        out_specs=vmem,
        compiler_params=pltpu.CompilerParams(vmem_limit_bytes=50 * 1024 * 1024),
        name="norm_back",
    )(inputs, layer_norm_scale[None, :], out_own[0], d_oth[0], *back)
    return input_grad[None], bias_grad


def solution(mesh):
    names = tuple(name for name, _ in AXES)
    split = Mesh(mesh.devices.reshape(tuple(n for _, n in AXES) + (NT,)), names + ("tok",))
    return jax.shard_map(
        on_device,
        mesh=split,
        in_specs=(
            P(names, "tok", None),
            P(names, "tok", None),
            P(),
            P(names, None),
            P(names, None),
            P(names, None),
            P(names, None),
            P(names, None),
            P(None, "tok", None),
            P(),
        ),
        out_specs=(P(names, "tok", None), P(None, "tok", names)),
        check_vma=False,
    )
```

time: 932 us -> 158 us (0.17)
  waiting for transfers between devices: 784 us -> 53.9 us
  starting transfers between devices: 0.49 us -> 63.8 us
  local copies, waits for them, and re-layouts: 46.1 us -> 11.8 us
  blocking collectives: 33.3 us -> 0 us
  matrix products: 30.5 us -> 0 us
  Pallas kernels: 0 us -> 20.9 us
  between operations: 14.9 us -> 0.85 us
    reduce_scatter x1 -> x0, waiting for transfers between devices: 408 us -> none  [on_device(): lax.psum_scatter(jnp.concatenate(bias_parts, axis=0), 'samp', scatter_dim...]
    all_gather x5 -> x0, waiting for transfers between devices: 349 us -> none  [the longest x1 82.4 us: on_device(): lax.all_gather(query_weight, 'samp', axis=0, tiled=True)]
    ppermute x0 -> x28, starting transfers between devices: none -> 58.1 us  [the longest x25 52 us: shift(): lax.ppermute(value, axis, [(i, (i + by) % count) for i in range(count)])]
    ppermute x0 -> x28, waiting for transfers between devices: none -> 39.4 us  [the longest x25 28.4 us: shift(): lax.ppermute(value, axis, [(i, (i + by) % count) for i in range(count)])]
    all_gather x2 -> x0, blocking collectives: 33.3 us -> none  [the longest x1 16.9 us: on_device(): lax.all_gather(project(normed_output, full_key), 'tok', axis=1, tiled=True)]
    unnamed x10 -> x0, waiting for transfers between devices: 27.8 us -> none
    unnamed x92 -> x26, local copies, waits for them, and re-layouts: 35.6 us -> 9.14 us
    pallas_call x0 -> x2, Pallas kernels: none -> 20.9 us  [the longest x1 19.7 us: on_device(): pl.pallas_call(attention_kernel, out_shape=(jax.ShapeDtypeStruct((NT, wid...]
  transfers between devices with their start and end apart: 8 -> 29, of which waited for: 7 -> 8; matrix products, arithmetic and copies ran while one was open for 7% -> 6% of each run, Pallas kernels for 0% -> 1%
where the time goes in v1:
time: 158 us; the launch traced here: 157 us
  starting transfers between devices  63.8 us (40%)
  waiting for transfers between devices  53.9 us (34%)
  Pallas kernels  20.9 us (13%)
  local copies, waits for them, and re-layouts  11.8 us (7%)
  other arithmetic  5.53 us (4%)
    ppermute x25, starting transfers between devices, shift(): lax.ppermute(value, axis, [(i, (i + by) % count) for i in range(count)])  52 us
    ppermute x25, waiting for transfers between devices, shift(): lax.ppermute(value, axis, [(i, (i + by) % count) for i in range(count)])  28.4 us
    pallas_call x1, Pallas kernels, on_device(): pl.pallas_call(attention_kernel, out_shape=(jax.ShapeDtypeStruct((NT, wid...  19.7 us
    all_to_all x1, waiting for transfers between devices, on_device(): parts = lax.all_to_all(out_bias, ('x', 'y'), 0, 0, tiled=True)  14.5 us
    ppermute x3, waiting for transfers between devices, on_device(): lax.ppermute((out_own[k] + d_oth[k].astype(F32)).astype(BF), 'tok', [(i,...  11.1 us
    unnamed x26, local copies, waits for them, and re-layouts  9.14 us
    ppermute x3, starting transfers between devices, on_device(): lax.ppermute((out_own[k] + d_oth[k].astype(F32)).astype(BF), 'tok', [(i,...  6.15 us
    all_to_all x1, starting transfers between devices, on_device(): parts = lax.all_to_all(out_bias, ('x', 'y'), 0, 0, tiled=True)  5.66 us
  transfers between devices with their start and end apart: 29, of which 8 were waited for; matrix products, arithmetic and copies ran while one was open for 6% of the time, Pallas kernels for 1%

profile of v1, /device:TPU:1, one launch (start us, length us, event | category | flops | bytes accessed | tf_op | source)
XLA Modules:
  0.0 156.7 jit_solution(3903050049556463501)
XLA Ops:
  0.7 0.8 constant_dynamic-update-slice_fusion.19
  1.4 0.7 constant_dynamic-update-slice_fusion.18
  2.2 0.7 constant_dynamic-update-slice_fusion.17
  2.9 0.7 constant_dynamic-update-slice_fusion.16
  3.6 0.7 constant_dynamic-update-slice_fusion.15
  4.4 3.3 %collective-permute-start.8 = (bf16[12,2304]{1,0:T(8,128)(2,1)S(1)}, bf16[12,2304]{1,0:T(8,128)(2,1)S(1)}, u32[]{:S(2)}, u32[]{:S(2)}) collective-permute-start(bf16[12,2304]{1,0:T(8,128)(2,1)S(1)} %broadcast_select_fusion), channel_id=1, source_target_pairs={{0,4},{4,0},{1,5},{5,1},{2,6},{6,2},{3,7},{7,3},{8,12},{12,8},{9,1... | collective-permute-start | bytes 165896 | tf_op jit(solution)/shard_map/ppermute | solution.py:17
  8.4 1.0 convert_reduce_fusion.1
  9.5 1.2 fusion.2
  10.7 0.7 constant_dynamic-update-slice_fusion.8
  12.9 0.7 constant_dynamic-update-slice_fusion.5
  13.7 5.3 %collective-permute-start.9 = (bf16[2,12,2304]{2,1,0:T(8,128)(2,1)S(1)}, bf16[2,12,2304]{2,1,0:T(8,128)(2,1)S(1)}, u32[]{:S(2)}, u32[]{:S(2)}) collective-permute-start(bf16[2,12,2304]{2,1,0:T(8,128)(2,1)S(1)} %maximum_select_fusion.2), channel_id=1, source_target_pairs={{0,32},{32,0},{1,33},{33,1},{2,34},{34,2},{3,35},{35,3},{4,36},{36... | collective-permute-start | bytes 331784 | tf_op jit(solution)/shard_map/ppermute | solution.py:17
  19.0 4.2 %collective-permute-done.9 = bf16[2,12,2304]{2,1,0:T(8,128)(2,1)S(1)} collective-permute-done((bf16[2,12,2304]{2,1,0:T(8,128)(2,1)S(1)}, bf16[2,12,2304]{2,1,0:T(8,128)(2,1)S(1)}, u32[]{:S(2)}, u32[]{:S(2)}) %collective-permute-start.9) | collective-permute-done | bytes 110624 | tf_op jit(solution)/shard_map/ppermute | solution.py:17
  23.3 1.4 collective-permute-start.16
  24.7 2.6 %collective-permute-start.17 = (bf16[48,1152]{1,0:T(8,128)(2,1)S(1)}, bf16[48,1152]{1,0:T(8,128)(2,1)S(1)}, u32[]{:S(2)}, u32[]{:S(2)}) collective-permute-start(bf16[48,1152]{1,0:T(8,128)(2,1)S(1)} %get-tuple-element.12), channel_id=1, source_target_pairs={{0,16},{8,24},{16,0},{24,8},{1,17},{9,25},{17,1},{25,9},{2,18},{10... | collective-permute-start | bytes 331784 | tf_op jit(solution)/shard_map/ppermute | solution.py:17
  27.3 1.1 collective-permute-start.18
  28.6 3.9 %collective-permute-start = (bf16[128,768]{1,0:T(8,128)(2,1)S(1)}, bf16[128,768]{1,0:T(8,128)(2,1)S(1)}, u32[]{:S(2)}, u32[]{:S(2)}) collective-permute-start(bf16[128,768]{1,0:T(8,128)(2,1)S(1)} %fusion.4.own0), channel_id=1, source_target_pairs={{0,1},{1,2},{2,3},{3,0},{4,5},{5,6},{6,7},{7,4},{8,9},{9,10},{10,1... | collective-permute-start | bytes 589832 | tf_op jit(solution)/shard_map/ppermute | solution.py:17
  33.1 2.3 %collective-permute-start.2 = (bf16[128,768]{1,0:T(8,128)(2,1)S(1)}, bf16[128,768]{1,0:T(8,128)(2,1)S(1)}, u32[]{:S(2)}, u32[]{:S(2)}) collective-permute-start(bf16[128,768]{1,0:T(8,128)(2,1)S(1)} %fusion.4.own0), channel_id=1, source_target_pairs={{0,3},{1,0},{2,1},{3,2},{4,7},{5,4},{6,5},{7,6},{8,11},{9,8},{10,9... | collective-permute-start | bytes 589832 | tf_op jit(solution)/shard_map/ppermute | solution.py:17
  35.4 0.8 pad_maximum_fusion.1.b0
  36.2 1.2 collective-permute-start.19
  37.4 2.9 %collective-permute-start.3 = (bf16[128,768]{1,0:T(8,128)(2,1)S(1)}, bf16[128,768]{1,0:T(8,128)(2,1)S(1)}, u32[]{:S(2)}, u32[]{:S(2)}) collective-permute-start(bf16[128,768]{1,0:T(8,128)(2,1)S(1)} %fusion.4.own0), channel_id=1, source_target_pairs={{0,4},{4,0},{1,5},{5,1},{2,6},{6,2},{3,7},{7,3},{8,12},{12,8},{9,1... | collective-permute-start | bytes 589832 | tf_op jit(solution)/shard_map/ppermute | solution.py:17
  40.4 1.2 collective-permute-start.10
  41.6 4.8 %collective-permute-done.1.own2 = bf16[128,768]{1,0:T(8,128)(2,1)S(1)} collective-permute-done((bf16[128,768]{1,0:T(8,128)(2,1)S(1)}, bf16[128,768]{1,0:T(8,128)(2,1)S(1)}, u32[]{:S(2)}, u32[]{:S(2)}) %collective-permute-start.1) | collective-permute-done | bytes 196640 | tf_op jit(solution)/shard_map/ppermute | solution.py:17
  46.4 2.6 %collective-permute-start.11 = (bf16[48,1152]{1,0:T(8,128)(2,1)S(1)}, bf16[48,1152]{1,0:T(8,128)(2,1)S(1)}, u32[]{:S(2)}, u32[]{:S(2)}) collective-permute-start(bf16[48,1152]{1,0:T(8,128)(2,1)S(1)} %get-tuple-element.13), channel_id=1, source_target_pairs={{0,128},{64,192},{128,0},{192,64},{1,129},{65,193},{129,1},{193,65... | collective-permute-start | bytes 331784 | tf_op jit(solution)/shard_map/ppermute | solution.py:17
  49.0 0.9 collective-permute-start.12
  49.9 1.6 %collective-permute-start.7 = (bf16[128,768]{1,0:T(8,128)(2,1)S(1)}, bf16[128,768]{1,0:T(8,128)(2,1)S(1)}, u32[]{:S(2)}, u32[]{:S(2)}) collective-permute-start(bf16[128,768]{1,0:T(8,128)(2,1)S(1)} %bitcast.65), channel_id=1, source_target_pairs={{0,4},{4,0},{1,5},{5,1},{2,6},{6,2},{3,7},{7,3},{8,12},{12,8},{9,1... | collective-permute-start | bytes 589832 | tf_op jit(solution)/shard_map/ppermute | solution.py:17
  51.5 2.2 %collective-permute-start.4 = (bf16[128,768]{1,0:T(8,128)(2,1)S(1)}, bf16[128,768]{1,0:T(8,128)(2,1)S(1)}, u32[]{:S(2)}, u32[]{:S(2)}) collective-permute-start(bf16[128,768]{1,0:T(8,128)(2,1)S(1)} %collective-permute-done.own1), channel_id=1, source_target_pairs={{0,4},{4,0},{1,5},{5,1},{2,6},{6,2},{3,7},{7,3},{8,12},{12,8},{9,1... | collective-permute-start | bytes 589832 | tf_op jit(solution)/shard_map/ppermute | solution.py:17
  53.8 2.2 %collective-permute-start.5 = (bf16[128,768]{1,0:T(8,128)(2,1)S(1)}, bf16[128,768]{1,0:T(8,128)(2,1)S(1)}, u32[]{:S(2)}, u32[]{:S(2)}) collective-permute-start(bf16[128,768]{1,0:T(8,128)(2,1)S(1)} %collective-permute-done.1.own2), channel_id=1, source_target_pairs={{0,4},{4,0},{1,5},{5,1},{2,6},{6,2},{3,7},{7,3},{8,12},{12,8},{9,1... | collective-permute-start | bytes 589832 | tf_op jit(solution)/shard_map/ppermute | solution.py:17
  56.0 1.8 %collective-permute-start.20 = (bf16[192,1152]{1,0:T(8,128)(2,1)}, bf16[192,1152]{1,0:T(8,128)(2,1)}, u32[]{:S(2)}, u32[]{:S(2)}) collective-permute-start(bf16[192,1152]{1,0:T(8,128)(2,1)} %pad_maximum_fusion.1.b0), channel_id=1, source_target_pairs={{0,128},{64,192},{128,0},{192,64},{1,129},{65,193},{129,1},{193,65... | collective-permute-start | bytes 1327112 | tf_op jit(solution)/shard_map/ppermute | solution.py:17
  57.8 1.8 %collective-permute-start.21 = (bf16[192,1152]{1,0:T(8,128)(2,1)}, bf16[192,1152]{1,0:T(8,128)(2,1)}, u32[]{:S(2)}, u32[]{:S(2)}) collective-permute-start(bf16[192,1152]{1,0:T(8,128)(2,1)} %pad_maximum_fusion.1.b0), channel_id=1, source_target_pairs={{0,192},{64,0},{128,64},{192,128},{1,193},{65,1},{129,65},{193,129... | collective-permute-start | bytes 1327112 | tf_op jit(solution)/shard_map/ppermute | solution.py:17
  61.3 1.0 collective-permute-start.14
  62.3 1.4 collective-permute-start.15
  63.8 5.5 %collective-permute-done.20.b2 = bf16[192,1152]{1,0:T(8,128)(2,1)} collective-permute-done((bf16[192,1152]{1,0:T(8,128)(2,1)}, bf16[192,1152]{1,0:T(8,128)(2,1)}, u32[]{:S(2)}, u32[]{:S(2)}) %collective-permute-start.20) | collective-permute-done | bytes 442400 | tf_op jit(solution)/shard_map/ppermute | solution.py:17
  69.3 9.9 %collective-permute-done.21.b3 = bf16[192,1152]{1,0:T(8,128)(2,1)} collective-permute-done((bf16[192,1152]{1,0:T(8,128)(2,1)}, bf16[192,1152]{1,0:T(8,128)(2,1)}, u32[]{:S(2)}, u32[]{:S(2)}) %collective-permute-start.21) | collective-permute-done | bytes 442400 | tf_op jit(solution)/shard_map/ppermute | solution.py:17
  79.2 2.9 %collective-permute-done.13.a1 = bf16[192,1152]{1,0:T(8,128)(2,1)S(1)} collective-permute-done((bf16[192,1152]{1,0:T(8,128)(2,1)S(1)}, bf16[192,1152]{1,0:T(8,128)(2,1)S(1)}, u32[]{:S(2)}, u32[]{:S(2)}) %collective-permute-start.13) | collective-permute-done | bytes 442400 | tf_op jit(solution)/shard_map/ppermute | solution.py:17
  82.1 1.0 collective-permute-done.15.a3
  83.3 0.9 copy-done.3
  84.2 0.9 copy-done.5
  85.1 19.7 %attention.1 = (f32[4,768,128]{2,1,0:T(8,128)}, bf16[4,768,128]{2,1,0:T(8,128)(2,1)}, bf16[16,8,2,16,128]{4,3,2,1,0:T(8,128)(2,1)}) custom-call(s32[4]{0:T(128)S(1)} %pad_add_fusion.pos, bf16[128,768]{1,0:T(8,128)(2,1)S(1)} %fusion.4.own0, bf16[128,768]{1,0:T(8,128)(2,1)S(1)} %collective-permute-done.own1, bf16[128,768]{1,0:T(8,128)(2,1)S(1)} %collective-permute-done.1.own2, ...), custom_call_target="tpu_custom_call" | custom-call | tf_op jit(solution)/shard_map/attention/pallas_call | solution.py:203
  104.8 5.7 %all-to-all-start = ((bf16[16,8,2,16,128]{4,3,2,1,0:T(8,128)(2,1)}), bf16[16,8,2,16,128]{4,3,2,1,0:T(8,128)(2,1)S(1)}, u32[]{:S(2)}, u32[]{:S(2)}) async-start(bf16[16,8,2,16,128]{4,3,2,1,0:T(8,128)(2,1)} %get-tuple-element.7), calls=%async_computation | async-start | bytes 2097152 | tf_op jit(solution)/shard_map/all_to_all | solution.py:239
  110.5 1.0 collective-permute-start.22
  111.6 14.5 %all-to-all-done = bf16[16,8,2,16,128]{4,3,2,1,0:T(8,128)(2,1)S(1)} async-done(((bf16[16,8,2,16,128]{4,3,2,1,0:T(8,128)(2,1)}), bf16[16,8,2,16,128]{4,3,2,1,0:T(8,128)(2,1)S(1)}, u32[]{:S(2)}, u32[]{:S(2)}) %all-to-all-start) | async-done | bytes 1048608 | tf_op jit(solution)/shard_map/all_to_all | solution.py:239
  126.2 5.1 %collective-permute-start.26 = (f32[8,16,128]{2,1,0:T(8,128)S(1)}, f32[8,16,128]{2,1,0:T(8,128)S(1)}, u32[]{:S(2)}, u32[]{:S(2)}) collective-permute-start(f32[8,16,128]{2,1,0:T(8,128)S(1)} %select_bitcast_fusion), channel_id=1, source_target_pairs={{0,32},{32,0},{1,33},{33,1},{2,34},{34,2},{3,35},{35,3},{4,36},{36... | collective-permute-start | bytes 196616 | tf_op jit(solution)/shard_map/ppermute | solution.py:17
  131.3 1.3 fusion.7
  132.6 5.8 %collective-permute-start.23 = (bf16[768,128]{1,0:T(8,128)(2,1)S(1)}, bf16[768,128]{1,0:T(8,128)(2,1)S(1)}, u32[]{:S(2)}, u32[]{:S(2)}) collective-permute-start(bf16[768,128]{1,0:T(8,128)(2,1)S(1)} %get-tuple-element.10), channel_id=1, source_target_pairs={{0,3},{1,0},{2,1},{3,2},{4,7},{5,4},{6,5},{7,6},{8,11},{9,8},{10,9... | collective-permute-start | bytes 589832 | tf_op jit(solution)/shard_map/ppermute | solution.py:233
  138.8 4.1 %collective-permute-start.27 = (f32[8,8,128]{2,1,0:T(8,128)S(1)}, f32[8,8,128]{2,1,0:T(8,128)S(1)}, u32[]{:S(2)}, u32[]{:S(2)}) collective-permute-start(f32[8,8,128]{2,1,0:T(8,128)S(1)} %get-tuple-element.15), channel_id=1, source_target_pairs={{0,4},{4,0},{1,5},{5,1},{2,6},{6,2},{3,7},{7,3},{8,12},{12,8},{9,1... | collective-permute-start | bytes 98312 | tf_op jit(solution)/shard_map/ppermute | solution.py:17
  142.9 0.9 slice_bitcast_fusion.1.d_oth
  143.8 11.1 %collective-permute-done.24.r2 = bf16[768,128]{1,0:T(8,128)(2,1)S(1)} collective-permute-done((bf16[768,128]{1,0:T(8,128)(2,1)S(1)}, bf16[768,128]{1,0:T(8,128)(2,1)S(1)}, u32[]{:S(2)}, u32[]{:S(2)}) %collective-permute-start.24) | collective-permute-done | bytes 196640 | tf_op jit(solution)/shard_map/ppermute | solution.py:233
  154.9 1.2 norm_back.1
  (65 shorter events, 6.5 us)
Async XLA Ops:
  0.6 27.8 %copy-start = (bf16[1,128,768]{2,1,0:T(8,128)(2,1)S(1)}, bf16[1,128,768]{2,1,0:T(8,128)(2,1)}, u32[]{:S(2)}) copy-start(bf16[1,128,768]{2,1,0:T(8,128)(2,1)} %param.10) | copy-start | bytes 589828
  0.6 27.8 %copy-start.7 = (f32[768]{0:T(1024)S(1)}, f32[768]{0:T(1024)}, u32[]{:S(2)}) copy-start(f32[768]{0:T(1024)} %param.12) | copy-start | bytes 9220
  4.4 9.3 %collective-permute-start.8 = (bf16[12,2304]{1,0:T(8,128)(2,1)S(1)}, bf16[12,2304]{1,0:T(8,128)(2,1)S(1)}, u32[]{:S(2)}, u32[]{:S(2)}) collective-permute-start(bf16[12,2304]{1,0:T(8,128)(2,1)S(1)} %broadcast_select_fusion), channel_id=1, source_target_pairs={{0,4},{4,0},{1,5},{5,1},{2,6},{6,2},{3,7},{7,3},{8,12},{12,8},{9,1... | collective-permute-start | bytes 165896 | tf_op jit(solution)/shard_map/ppermute | solution.py:17
  9.5 40.4 %copy-start.1 = (bf16[1,128,768]{2,1,0:T(8,128)(2,1)S(1)}, bf16[1,128,768]{2,1,0:T(8,128)(2,1)}, u32[]{:S(2)}) copy-start(bf16[1,128,768]{2,1,0:T(8,128)(2,1)} %param.11) | copy-start | bytes 589828
  13.7 50.1 %copy-start.8 = (s32[512]{0:T(512)S(1)}, s32[512]{0:T(512)}, u32[]{:S(2)}) copy-start(s32[512]{0:T(512)} %param.19) | copy-start | bytes 6148
  13.7 9.5 %collective-permute-start.9 = (bf16[2,12,2304]{2,1,0:T(8,128)(2,1)S(1)}, bf16[2,12,2304]{2,1,0:T(8,128)(2,1)S(1)}, u32[]{:S(2)}, u32[]{:S(2)}) collective-permute-start(bf16[2,12,2304]{2,1,0:T(8,128)(2,1)S(1)} %maximum_select_fusion.2), channel_id=1, source_target_pairs={{0,32},{32,0},{1,33},{33,1},{2,34},{34,2},{3,35},{35,3},{4,36},{36... | collective-permute-start | bytes 331784 | tf_op jit(solution)/shard_map/ppermute | solution.py:17
  23.3 9.8 %collective-permute-start.16 = (bf16[48,1152]{1,0:T(8,128)(2,1)S(1)}, bf16[48,1152]{1,0:T(8,128)(2,1)S(1)}, u32[]{:S(2)}, u32[]{:S(2)}) collective-permute-start(bf16[48,1152]{1,0:T(8,128)(2,1)S(1)} %get-tuple-element.12), channel_id=1, source_target_pairs={{0,8},{8,16},{16,24},{24,0},{1,9},{9,17},{17,25},{25,1},{2,10},{10... | collective-permute-start | bytes 331784 | tf_op jit(solution)/shard_map/ppermute | solution.py:17
  24.7 10.7 %collective-permute-start.17 = (bf16[48,1152]{1,0:T(8,128)(2,1)S(1)}, bf16[48,1152]{1,0:T(8,128)(2,1)S(1)}, u32[]{:S(2)}, u32[]{:S(2)}) collective-permute-start(bf16[48,1152]{1,0:T(8,128)(2,1)S(1)} %get-tuple-element.12), channel_id=1, source_target_pairs={{0,16},{8,24},{16,0},{24,8},{1,17},{9,25},{17,1},{25,9},{2,18},{10... | collective-permute-start | bytes 331784 | tf_op jit(solution)/shard_map/ppermute | solution.py:17
  27.3 8.1 %collective-permute-start.18 = (bf16[48,1152]{1,0:T(8,128)(2,1)S(1)}, bf16[48,1152]{1,0:T(8,128)(2,1)S(1)}, u32[]{:S(2)}, u32[]{:S(2)}) collective-permute-start(bf16[48,1152]{1,0:T(8,128)(2,1)S(1)} %get-tuple-element.12), channel_id=1, source_target_pairs={{0,24},{8,0},{16,8},{24,16},{1,25},{9,1},{17,9},{25,17},{2,26},{10... | collective-permute-start | bytes 331784 | tf_op jit(solution)/shard_map/ppermute | solution.py:17
  28.6 11.8 %collective-permute-start = (bf16[128,768]{1,0:T(8,128)(2,1)S(1)}, bf16[128,768]{1,0:T(8,128)(2,1)S(1)}, u32[]{:S(2)}, u32[]{:S(2)}) collective-permute-start(bf16[128,768]{1,0:T(8,128)(2,1)S(1)} %fusion.4.own0), channel_id=1, source_target_pairs={{0,1},{1,2},{2,3},{3,0},{4,5},{5,6},{6,7},{7,4},{8,9},{9,10},{10,1... | collective-permute-start | bytes 589832 | tf_op jit(solution)/shard_map/ppermute | solution.py:17
  32.5 13.9 %collective-permute-start.1 = (bf16[128,768]{1,0:T(8,128)(2,1)S(1)}, bf16[128,768]{1,0:T(8,128)(2,1)S(1)}, u32[]{:S(2)}, u32[]{:S(2)}) collective-permute-start(bf16[128,768]{1,0:T(8,128)(2,1)S(1)} %fusion.4.own0), channel_id=1, source_target_pairs={{0,2},{1,3},{2,0},{3,1},{4,6},{5,7},{6,4},{7,5},{8,10},{9,11},{10,... | collective-permute-start | bytes 589832 | tf_op jit(solution)/shard_map/ppermute | solution.py:17
  33.1 15.9 %collective-permute-start.2 = (bf16[128,768]{1,0:T(8,128)(2,1)S(1)}, bf16[128,768]{1,0:T(8,128)(2,1)S(1)}, u32[]{:S(2)}, u32[]{:S(2)}) collective-permute-start(bf16[128,768]{1,0:T(8,128)(2,1)S(1)} %fusion.4.own0), channel_id=1, source_target_pairs={{0,3},{1,0},{2,1},{3,2},{4,7},{5,4},{6,5},{7,6},{8,11},{9,8},{10,9... | collective-permute-start | bytes 589832 | tf_op jit(solution)/shard_map/ppermute | solution.py:17
  36.2 26.1 %collective-permute-start.19 = (bf16[192,1152]{1,0:T(8,128)(2,1)}, bf16[192,1152]{1,0:T(8,128)(2,1)}, u32[]{:S(2)}, u32[]{:S(2)}) collective-permute-start(bf16[192,1152]{1,0:T(8,128)(2,1)} %pad_maximum_fusion.1.b0), channel_id=1, source_target_pairs={{0,64},{64,128},{128,192},{192,0},{1,65},{65,129},{129,193},{193,1... | collective-permute-start | bytes 1327112 | tf_op jit(solution)/shard_map/ppermute | solution.py:17
  37.4 12.5 %collective-permute-start.3 = (bf16[128,768]{1,0:T(8,128)(2,1)S(1)}, bf16[128,768]{1,0:T(8,128)(2,1)S(1)}, u32[]{:S(2)}, u32[]{:S(2)}) collective-permute-start(bf16[128,768]{1,0:T(8,128)(2,1)S(1)} %fusion.4.own0), channel_id=1, source_target_pairs={{0,4},{4,0},{1,5},{5,1},{2,6},{6,2},{3,7},{7,3},{8,12},{12,8},{9,1... | collective-permute-start | bytes 589832 | tf_op jit(solution)/shard_map/ppermute | solution.py:17
  40.4 11.2 %collective-permute-start.10 = (bf16[48,1152]{1,0:T(8,128)(2,1)S(1)}, bf16[48,1152]{1,0:T(8,128)(2,1)S(1)}, u32[]{:S(2)}, u32[]{:S(2)}) collective-permute-start(bf16[48,1152]{1,0:T(8,128)(2,1)S(1)} %get-tuple-element.13), channel_id=1, source_target_pairs={{0,64},{64,128},{128,192},{192,0},{1,65},{65,129},{129,193},{193,1... | collective-permute-start | bytes 331784 | tf_op jit(solution)/shard_map/ppermute | solution.py:17
  46.4 7.4 %collective-permute-start.11 = (bf16[48,1152]{1,0:T(8,128)(2,1)S(1)}, bf16[48,1152]{1,0:T(8,128)(2,1)S(1)}, u32[]{:S(2)}, u32[]{:S(2)}) collective-permute-start(bf16[48,1152]{1,0:T(8,128)(2,1)S(1)} %get-tuple-element.13), channel_id=1, source_target_pairs={{0,128},{64,192},{128,0},{192,64},{1,129},{65,193},{129,1},{193,65... | collective-permute-start | bytes 331784 | tf_op jit(solution)/shard_map/ppermute | solution.py:17
  49.0 6.9 %collective-permute-start.12 = (bf16[48,1152]{1,0:T(8,128)(2,1)S(1)}, bf16[48,1152]{1,0:T(8,128)(2,1)S(1)}, u32[]{:S(2)}, u32[]{:S(2)}) collective-permute-start(bf16[48,1152]{1,0:T(8,128)(2,1)S(1)} %get-tuple-element.13), channel_id=1, source_target_pairs={{0,192},{64,0},{128,64},{192,128},{1,193},{65,1},{129,65},{193,129... | collective-permute-start | bytes 331784 | tf_op jit(solution)/shard_map/ppermute | solution.py:17
  49.9 6.1 %collective-permute-start.7 = (bf16[128,768]{1,0:T(8,128)(2,1)S(1)}, bf16[128,768]{1,0:T(8,128)(2,1)S(1)}, u32[]{:S(2)}, u32[]{:S(2)}) collective-permute-start(bf16[128,768]{1,0:T(8,128)(2,1)S(1)} %bitcast.65), channel_id=1, source_target_pairs={{0,4},{4,0},{1,5},{5,1},{2,6},{6,2},{3,7},{7,3},{8,12},{12,8},{9,1... | collective-permute-start | bytes 589832 | tf_op jit(solution)/shard_map/ppermute | solution.py:17
  51.5 6.2 %collective-permute-start.4 = (bf16[128,768]{1,0:T(8,128)(2,1)S(1)}, bf16[128,768]{1,0:T(8,128)(2,1)S(1)}, u32[]{:S(2)}, u32[]{:S(2)}) collective-permute-start(bf16[128,768]{1,0:T(8,128)(2,1)S(1)} %collective-permute-done.own1), channel_id=1, source_target_pairs={{0,4},{4,0},{1,5},{5,1},{2,6},{6,2},{3,7},{7,3},{8,12},{12,8},{9,1... | collective-permute-start | bytes 589832 | tf_op jit(solution)/shard_map/ppermute | solution.py:17
  53.8 5.8 %collective-permute-start.5 = (bf16[128,768]{1,0:T(8,128)(2,1)S(1)}, bf16[128,768]{1,0:T(8,128)(2,1)S(1)}, u32[]{:S(2)}, u32[]{:S(2)}) collective-permute-start(bf16[128,768]{1,0:T(8,128)(2,1)S(1)} %collective-permute-done.1.own2), channel_id=1, source_target_pairs={{0,4},{4,0},{1,5},{5,1},{2,6},{6,2},{3,7},{7,3},{8,12},{12,8},{9,1... | collective-permute-start | bytes 589832 | tf_op jit(solution)/shard_map/ppermute | solution.py:17
  56.0 4.7 %collective-permute-start.6 = (bf16[128,768]{1,0:T(8,128)(2,1)S(1)}, bf16[128,768]{1,0:T(8,128)(2,1)S(1)}, u32[]{:S(2)}, u32[]{:S(2)}) collective-permute-start(bf16[128,768]{1,0:T(8,128)(2,1)S(1)} %collective-permute-done.2.own3), channel_id=1, source_target_pairs={{0,4},{4,0},{1,5},{5,1},{2,6},{6,2},{3,7},{7,3},{8,12},{12,8},{9,1... | collective-permute-start | bytes 589832 | tf_op jit(solution)/shard_map/ppermute | solution.py:17
  56.0 13.3 %collective-permute-start.20 = (bf16[192,1152]{1,0:T(8,128)(2,1)}, bf16[192,1152]{1,0:T(8,128)(2,1)}, u32[]{:S(2)}, u32[]{:S(2)}) collective-permute-start(bf16[192,1152]{1,0:T(8,128)(2,1)} %pad_maximum_fusion.1.b0), channel_id=1, source_target_pairs={{0,128},{64,192},{128,0},{192,64},{1,129},{65,193},{129,1},{193,65... | collective-permute-start | bytes 1327112 | tf_op jit(solution)/shard_map/ppermute | solution.py:17
  57.8 21.4 %collective-permute-start.21 = (bf16[192,1152]{1,0:T(8,128)(2,1)}, bf16[192,1152]{1,0:T(8,128)(2,1)}, u32[]{:S(2)}, u32[]{:S(2)}) collective-permute-start(bf16[192,1152]{1,0:T(8,128)(2,1)} %pad_maximum_fusion.1.b0), channel_id=1, source_target_pairs={{0,192},{64,0},{128,64},{192,128},{1,193},{65,1},{129,65},{193,129... | collective-permute-start | bytes 1327112 | tf_op jit(solution)/shard_map/ppermute | solution.py:17
  59.6 0.7 copy-start.2
  60.3 21.9 %collective-permute-start.13 = (bf16[192,1152]{1,0:T(8,128)(2,1)S(1)}, bf16[192,1152]{1,0:T(8,128)(2,1)S(1)}, u32[]{:S(2)}, u32[]{:S(2)}) collective-permute-start(bf16[192,1152]{1,0:T(8,128)(2,1)S(1)} %pad_maximum_fusion.a0), channel_id=1, source_target_pairs={{0,8},{8,16},{16,24},{24,0},{1,9},{9,17},{17,25},{25,1},{2,10},{10... | collective-permute-start | bytes 1327112 | tf_op jit(solution)/shard_map/ppermute | solution.py:17
  60.7 0.7 copy-start.4
  61.3 20.8 %collective-permute-start.14 = (bf16[192,1152]{1,0:T(8,128)(2,1)S(1)}, bf16[192,1152]{1,0:T(8,128)(2,1)S(1)}, u32[]{:S(2)}, u32[]{:S(2)}) collective-permute-start(bf16[192,1152]{1,0:T(8,128)(2,1)S(1)} %pad_maximum_fusion.a0), channel_id=1, source_target_pairs={{0,16},{8,24},{16,0},{24,8},{1,17},{9,25},{17,1},{25,9},{2,18},{10... | collective-permute-start | bytes 1327112 | tf_op jit(solution)/shard_map/ppermute | solution.py:17
  62.3 20.8 %collective-permute-start.15 = (bf16[192,1152]{1,0:T(8,128)(2,1)S(1)}, bf16[192,1152]{1,0:T(8,128)(2,1)S(1)}, u32[]{:S(2)}, u32[]{:S(2)}) collective-permute-start(bf16[192,1152]{1,0:T(8,128)(2,1)S(1)} %pad_maximum_fusion.a0), channel_id=1, source_target_pairs={{0,24},{8,0},{16,8},{24,16},{1,25},{9,1},{17,9},{25,17},{2,26},{10... | collective-permute-start | bytes 1327112 | tf_op jit(solution)/shard_map/ppermute | solution.py:17
  83.3 0.9 copy-start.3
  84.2 0.9 copy-start.5
  104.8 26.5 %copy-start.6 = (f32[4,768,128]{2,1,0:T(8,128)S(1)}, f32[4,768,128]{2,1,0:T(8,128)}, u32[]{:S(2)}) copy-start(f32[4,768,128]{2,1,0:T(8,128)} %get-tuple-element.5) | copy-start | bytes 4718596
  104.8 21.2 %all-to-all-start = ((bf16[16,8,2,16,128]{4,3,2,1,0:T(8,128)(2,1)}), bf16[16,8,2,16,128]{4,3,2,1,0:T(8,128)(2,1)S(1)}, u32[]{:S(2)}, u32[]{:S(2)}) async-start(bf16[16,8,2,16,128]{4,3,2,1,0:T(8,128)(2,1)} %get-tuple-element.7), calls=%async_computation | async-start | bytes 2097152 | tf_op jit(solution)/shard_map/all_to_all | solution.py:239
  110.5 20.8 %collective-permute-start.22 = (bf16[4,768,128]{2,1,0:T(8,128)(2,1)}, bf16[4,768,128]{2,1,0:T(8,128)(2,1)}, u32[]{:S(2)}, u32[]{:S(2)}) collective-permute-start(bf16[4,768,128]{2,1,0:T(8,128)(2,1)} %get-tuple-element.6), channel_id=1, source_target_pairs={{0,4},{4,0},{1,5},{5,1},{2,6},{6,2},{3,7},{7,3},{8,12},{12,8},{9,1... | collective-permute-start | bytes 2359304 | tf_op jit(solution)/shard_map/ppermute | solution.py:17
  126.2 12.6 %collective-permute-start.26 = (f32[8,16,128]{2,1,0:T(8,128)S(1)}, f32[8,16,128]{2,1,0:T(8,128)S(1)}, u32[]{:S(2)}, u32[]{:S(2)}) collective-permute-start(f32[8,16,128]{2,1,0:T(8,128)S(1)} %select_bitcast_fusion), channel_id=1, source_target_pairs={{0,32},{32,0},{1,33},{33,1},{2,34},{34,2},{3,35},{35,3},{4,36},{36... | collective-permute-start | bytes 196616 | tf_op jit(solution)/shard_map/ppermute | solution.py:17
  132.6 11.2 %collective-permute-start.23 = (bf16[768,128]{1,0:T(8,128)(2,1)S(1)}, bf16[768,128]{1,0:T(8,128)(2,1)S(1)}, u32[]{:S(2)}, u32[]{:S(2)}) collective-permute-start(bf16[768,128]{1,0:T(8,128)(2,1)S(1)} %get-tuple-element.10), channel_id=1, source_target_pairs={{0,3},{1,0},{2,1},{3,2},{4,7},{5,4},{6,5},{7,6},{8,11},{9,8},{10,9... | collective-permute-start | bytes 589832 | tf_op jit(solution)/shard_map/ppermute | solution.py:233
  138.4 16.5 %collective-permute-start.24 = (bf16[768,128]{1,0:T(8,128)(2,1)S(1)}, bf16[768,128]{1,0:T(8,128)(2,1)S(1)}, u32[]{:S(2)}, u32[]{:S(2)}) collective-permute-start(bf16[768,128]{1,0:T(8,128)(2,1)S(1)} %get-tuple-element.9), channel_id=1, source_target_pairs={{0,2},{1,3},{2,0},{3,1},{4,6},{5,7},{6,4},{7,5},{8,10},{9,11},{10,... | collective-permute-start | bytes 589832 | tf_op jit(solution)/shard_map/ppermute | solution.py:233
  138.4 16.5 %collective-permute-start.25 = (bf16[768,128]{1,0:T(8,128)(2,1)S(1)}, bf16[768,128]{1,0:T(8,128)(2,1)S(1)}, u32[]{:S(2)}, u32[]{:S(2)}) collective-permute-start(bf16[768,128]{1,0:T(8,128)(2,1)S(1)} %get-tuple-element.8), channel_id=1, source_target_pairs={{0,1},{1,2},{2,3},{3,0},{4,5},{5,6},{6,7},{7,4},{8,9},{9,10},{10,1... | collective-permute-start | bytes 589832 | tf_op jit(solution)/shard_map/ppermute | solution.py:233
  138.8 17.3 %collective-permute-start.27 = (f32[8,8,128]{2,1,0:T(8,128)S(1)}, f32[8,8,128]{2,1,0:T(8,128)S(1)}, u32[]{:S(2)}, u32[]{:S(2)}) collective-permute-start(f32[8,8,128]{2,1,0:T(8,128)S(1)} %get-tuple-element.15), channel_id=1, source_target_pairs={{0,4},{4,0},{1,5},{5,1},{2,6},{6,2},{3,7},{7,3},{8,12},{12,8},{9,1... | collective-permute-start | bytes 98312 | tf_op jit(solution)/shard_map/ppermute | solution.py:17

commit v2 on v1

v2 whole, which is shorter than its diff:
```python
import jax
import jax.numpy as jnp
from jax import lax
from jax.experimental import pallas as pl
from jax.experimental.pallas import tpu as pltpu
from jax.sharding import Mesh, PartitionSpec as P

AXES = (("x", 4), ("zh", 2), ("y", 4), ("core", 2))
TOK = (("th", 2), ("tl", 2))
NX, NZ, NY, NC = 4, 2, 4, 2
NT = 4
BF = jnp.bfloat16
F32 = jnp.float32
NEG = -1000000000.0


def shift(value, axis, count, by):
    return lax.ppermute(value, axis, [(i, (i + by) % count) for i in range(count)])


def swap(value, by):
    return lax.ppermute(value, ("th", "tl"), [(i, i ^ by) for i in range(NT)])


def nt(a, b):
    return lax.dot_general(a, b, (((1,), (1,)), ((), ())), preferred_element_type=F32)


def nn(a, b):
    return lax.dot_general(a, b, (((1,), (0,)), ((), ())), preferred_element_type=F32)


def attention_kernel(
    pos,
    own_near, own_far, oth_near, oth_far,
    cot_own0, cot_own1, cot_oth0, cot_oth1,
    weights,
    bias, bias_pair, valid_row, valid_col,
    out_first, out_own, out_oth, out_bias,
    wf, wo, wb, dgt, kv, km, kvt, qt, gt, dx, dqg,
):
    heads = bias_pair.shape[0]
    width = own_near.shape[1]
    part = width // 4
    size = part // heads
    rows = bias.shape[1]
    scale = float(size) ** (-0.5)
    core, tok, pair = pos[2], pos[3], pos[5]
    rx, rz, ry = width // NX, width // (NX * NZ), width // (NX * NZ * NY)
    tail = weights.shape[2] - width

    for block in range(NX * NY):
        to_x, to_y = divmod(block, NY)
        rows_of = weights[block].astype(F32)
        for z in range(NZ):
            at = to_x * rx + z * rz + to_y * ry
            wf[at:at + ry, :] = rows_of[z * ry:(z + 1) * ry, :width]
            at = to_x * rz + to_y * ry
            wo[at:at + ry, z * tail:(z + 1) * tail] = rows_of[z * ry:(z + 1) * ry, width:]
    wb[...] = wf[...].astype(BF)

    mine = jnp.concatenate(
        [wo[pl.ds(pl.multiple_of(j * rz + pair * size, 8), size), :] for j in range(heads)], axis=0
    ).astype(BF)
    for s, cots in enumerate(((cot_own0, cot_own1), (cot_oth0, cot_oth1))):
        for u, cot in enumerate(cots):
            dgt[s, :, u * rows:(u + 1) * rows] = nt(mine, cot[...])

    for s, tokens in enumerate(((own_near, own_far), (oth_near, oth_far))):
        for r in range(NT):
            n = tokens[r // 2][r % 2 * rows:(r % 2 + 1) * rows, :]
            lo = pl.multiple_of((tok ^ r) * rows, rows)
            both = nn(n, wb[:, : 2 * part])
            kvt[s, :, pl.ds(lo, rows)] = both.T.astype(BF)
            kv[s, pl.ds(lo, rows), :] = both.astype(BF)
            keep = valid_col[pl.ds(lo, rows), :]
            for j in range(2):
                km[s, pl.ds(lo, rows), j * 128:(j + 1) * 128] = (both[:, j * 128:(j + 1) * 128] * keep).astype(BF)
        both = nn(tokens[0][...], wb[:, 2 * part:]).T
        qt[s] = both[:part].astype(BF)
        gt[s] = jax.nn.sigmoid(both[part:].astype(BF).astype(F32))

    def widen(block, first):
        low = first // 128 * 128
        high = -(-(first + size) // 128) * 128
        parts = [block]
        if first > low:
            parts = [jnp.zeros((first - low, block.shape[1]), BF)] + parts
        if high > first + size:
            parts = parts + [jnp.zeros((high - first - size, block.shape[1]), BF)]
        return low, high, jnp.concatenate(parts, axis=0)

    for h in range(heads):
        first = h * size
        at = slice(first, first + size)
        biases = (bias[4 * h + 2 * core + pair], bias_pair[h])
        bias_t = jnp.concatenate(
            [jnp.where(valid_row[...] > 0.0, b.astype(F32), NEG).T for b in biases], axis=1
        )
        total = None
        for s in range(2):
            q_h = qt[s, at, :]
            dgated = dgt[s, at, :]
            sig = gt[s, at, :]
            da_h = (dgated * sig).astype(BF)
            low, high, q_wide = widen(q_h, first)
            scores = nn(km[s, :, low:high], q_wide) * scale + bias_t
            top = jnp.max(scores, axis=0, keepdims=True)
            e = jnp.exp(scores - top)
            probs = e * (1.0 / jnp.sum(e, axis=0, keepdims=True))
            probs_b = probs.astype(BF)
            att = nn(kvt[s, part + first:part + first + size, :], probs_b).astype(BF).astype(F32)
            delta = jnp.sum(da_h.astype(F32) * att, axis=0, keepdims=True)
            low, high, da_wide = widen(da_h, part + first)
            d_prob = nn(kv[s, :, low:high], da_wide)
            d_score = probs * (d_prob - delta)
            total = d_score if total is None else total + d_score
            ds_b = d_score.astype(BF)
            dqg[s, at, :] = (nn(kvt[s, at, :], ds_b) * scale).astype(BF)
            dqg[s, part + first:part + first + size, :] = (dgated * att * sig * (1.0 - sig)).astype(BF)
            dx[s, at, :] = (nt(q_h, ds_b) * scale).astype(BF)
            dx[s, part + first:part + first + size, :] = nt(da_h, probs_b).astype(BF)
        each = rows // (NZ * NY)
        for to_x in range(NX):
            for z in range(NZ):
                for to_y in range(NY):
                    lo = to_x * rows + z * (rows // NZ) + to_y * each
                    out_bias[to_x * NY + to_y, h, z] = total[lo:lo + each, :].astype(BF)

    for s in range(2):
        for r in range(NT):
            at = pl.multiple_of((tok ^ r) * rows, rows)
            d = nn(wb[:, : 2 * part], dx[s, :, pl.ds(at, rows)])
            if r < 2:
                d = d + nn(wb[:, 2 * part:], dqg[s, :, r * rows:(r + 1) * rows])
            if s == 1:
                out_oth[r] = d.astype(BF)
            elif r == 0:
                out_first[...] = d
            else:
                out_own[r - 1] = d.astype(BF)


def pack_kernel(pos, query, key, value, gate, out, mine, send):
    width = query.shape[1]
    part = width // 4
    size = part // NX
    row = lax.broadcasted_iota(jnp.int32, (width, part), 0)
    lane = lax.broadcasted_iota(jnp.int32, (width, part), 1)
    col = lane + pos[5] * size
    for k in range(1, NX):
        col = col + jnp.where(lane >= k * size, width // NX - size, 0)
    low = jnp.where(row == col, 1.0, 0.0).astype(BF)
    high = jnp.where(row == col + 2 * size, 1.0, 0.0).astype(BF)
    first = pos[2] == 0
    lows = jnp.concatenate([nn(w[...], low) for w in (key, value, query, gate)], axis=1)
    highs = jnp.concatenate([nn(w[...], high) for w in (key, value, query, gate)], axis=1)
    mine[:, :width] = jnp.where(first, lows, highs).astype(BF)
    send[:, :width] = jnp.where(first, highs, lows).astype(BF)
    mine[:, width:] = out[...]
    send[:, width:] = out[...]


def norm_kernel(inputs, gain, normed):
    xf = inputs[...].astype(F32)
    centered = xf - jnp.mean(xf, axis=-1, keepdims=True)
    inv = lax.rsqrt(jnp.mean(centered * centered, axis=-1, keepdims=True) + 1e-05)
    normed[...] = (centered * inv * gain[...][None, :]).astype(BF)


def assemble_kernel(pos, mine, beside, above, across, normed, beyond, part, near):
    rows = normed.shape[0]
    near[:rows, :] = normed[...]
    near[rows:, :] = beyond[...]
    first, below = pos[2] == 0, pos[4] == 0
    m, b, u, d = (ref[...].astype(F32) for ref in (mine, beside, above, across))
    near_lo, near_hi = jnp.where(first, m, b), jnp.where(first, b, m)
    far_lo, far_hi = jnp.where(first, u, d), jnp.where(first, d, u)
    cols = normed.shape[1]
    half = part.shape[2] - cols
    quad = jnp.concatenate(
        [
            jnp.where(below, near_lo, far_lo)[:, :cols],
            jnp.where(below, near_hi, far_hi)[:, :cols],
            jnp.where(below, far_lo, near_lo)[:, :cols],
            jnp.where(below, far_hi, near_hi)[:, :cols],
        ],
        axis=0,
    ).astype(BF)
    same = pos[4] == pos[2]
    out_lo, out_hi = jnp.where(same, near_lo, far_lo), jnp.where(same, near_hi, far_hi)
    tail = jnp.concatenate(
        [out_lo[:, cols:cols + half], out_hi[:, cols:cols + half], out_lo[:, cols + half:], out_hi[:, cols + half:]], axis=0
    ).astype(BF)
    for k in range(part.shape[0]):
        part[k, :, :cols] = quad
        part[k, :, cols:] = tail


def sum_kernel(first, own, oth, s0, s1, s2, s3):
    s0[...] = first[...] + oth[0].astype(F32)
    for k, out in enumerate((s1, s2, s3)):
        out[...] = (own[k].astype(F32) + oth[k + 1].astype(F32)).astype(BF)


def plane_kernel(pos, parts, r1, r2, r3, out):
    rows = out.shape[-1]
    each = out.shape[-2]
    total = jnp.sum(parts[...].astype(F32), axis=0)
    for z in range(NZ):
        for c in range(NC):
            for u in range(2):
                out[z, c, pos[5] ^ u] = total[:, z, c * each:(c + 1) * each, u * rows:(u + 1) * rows]


def final_kernel(inputs, gain, r0, r1, r2, r3, out):
    d = r0[...] + r1[...].astype(F32) + r2[...].astype(F32) + r3[...].astype(F32)
    g = d.T * gain[...][None, :]
    xf = inputs[...].astype(F32)
    mean = jnp.mean(xf, axis=-1, keepdims=True)
    centered = xf - mean
    inv = lax.rsqrt(jnp.mean(centered * centered, axis=-1, keepdims=True) + 1e-05)
    xhat = centered * inv
    res = inv * (g - jnp.mean(g, axis=-1, keepdims=True) - xhat * jnp.mean(g * xhat, axis=-1, keepdims=True))
    out[...] = res.astype(BF)


def on_device(
    inputs,
    cotangent,
    layer_norm_scale,
    query_weight,
    key_weight,
    value_weight,
    gate_weight,
    out_weight,
    pair_bias,
    atom_count,
):
    x, zh, y, core, th, tl = (lax.axis_index(a) for a in ("x", "zh", "y", "core", "th", "tl"))
    inputs, cotangent = inputs[0], cotangent[0]
    rows, width = inputs.shape
    part = width // 4
    heads = pair_bias.shape[0] // 4
    total = pair_bias.shape[2]

    pos = jnp.stack([x, y, core, 2 * th + tl, zh, tl]).astype(jnp.int32)
    vmem = pl.BlockSpec(memory_space=pltpu.VMEM)
    smem = pl.BlockSpec(memory_space=pltpu.SMEM)
    anywhere = pl.BlockSpec(memory_space=pl.ANY)
    gain = layer_norm_scale

    packed = jax.ShapeDtypeStruct((query_weight.shape[0], 2 * width), BF)
    mine, send = pl.pallas_call(
        pack_kernel,
        out_shape=(packed, packed),
        in_specs=[smem] + [vmem] * 5,
        out_specs=(vmem, vmem),
        name="pack",
    )(pos, query_weight, key_weight, value_weight, gate_weight, out_weight)
    beside = shift(send, "core", NC, 1)
    above = shift(mine, "zh", NZ, 1)
    across = lax.ppermute(send, ("zh", "core"), [(0, 3), (3, 0), (1, 2), (2, 1)])

    normed = pl.pallas_call(
        norm_kernel,
        out_shape=jax.ShapeDtypeStruct((rows, width), BF),
        in_specs=[vmem, vmem],
        out_specs=vmem,
        name="norm",
    )(inputs, gain)
    beyond = swap(normed, 1)

    pieces, own_near = pl.pallas_call(
        assemble_kernel,
        out_shape=(
            jax.ShapeDtypeStruct((NX * NY, NC * NZ * mine.shape[0], width + width // 2), BF),
            jax.ShapeDtypeStruct((2 * rows, width), BF),
        ),
        in_specs=[smem] + [vmem] * 6,
        out_specs=(vmem, vmem),
        compiler_params=pltpu.CompilerParams(vmem_limit_bytes=30 * 1024 * 1024),
        name="assemble",
    )(pos, mine, beside, above, across, normed, beyond)
    own_far = swap(own_near, 2)
    weights = lax.all_to_all(pieces, ("x", "y"), 0, 0, tiled=True)
    oth_near, oth_far = shift(own_near, "core", NC, 1), shift(own_far, "core", NC, 1)
    cot_pair = swap(cotangent, 1)
    cots = [cotangent, cot_pair, shift(cotangent, "core", NC, 1), shift(cot_pair, "core", NC, 1)]
    groups = pair_bias.reshape((heads, NC, 2) + pair_bias.shape[1:])
    theirs = lax.dynamic_index_in_dim(lax.dynamic_index_in_dim(groups, core, 1, False), 1 - tl, 1, False)
    bias_pair = swap(theirs, 1)

    valid = (atom_count > 0).astype(F32)
    operands = [own_near, own_far, oth_near, oth_far] + cots + [weights]
    operands += [pair_bias, bias_pair, valid[None, :], jnp.broadcast_to(valid[:, None], (total, 128))]
    out_first, out_own, out_oth, out_bias = pl.pallas_call(
        attention_kernel,
        out_shape=(
            jax.ShapeDtypeStruct((width, rows), F32),
            jax.ShapeDtypeStruct((NT - 1, width, rows), BF),
            jax.ShapeDtypeStruct((NT, width, rows), BF),
            jax.ShapeDtypeStruct((NX * NY, heads, NZ, rows // (NZ * NY), 2 * rows), BF),
        ),
        in_specs=[smem] + [vmem] * len(operands),
        out_specs=(vmem,) * 4,
        scratch_shapes=[
            pltpu.VMEM((width, width), F32),
            pltpu.VMEM((width // 2, width), F32),
            pltpu.VMEM((width, width), BF),
            pltpu.VMEM((2, part, 2 * rows), F32),
            pltpu.VMEM((2, total, 2 * part), BF),
            pltpu.VMEM((2, total, 256), BF),
            pltpu.VMEM((2, 2 * part, total), BF),
            pltpu.VMEM((2, part, 2 * rows), BF),
            pltpu.VMEM((2, part, 2 * rows), F32),
            pltpu.VMEM((2, 2 * part, total), BF),
            pltpu.VMEM((2, 2 * part, 2 * rows), BF),
        ],
        compiler_params=pltpu.CompilerParams(vmem_limit_bytes=50 * 1024 * 1024),
        name="attention",
    )(pos, *operands)

    d_oth = shift(out_oth, "core", NC, 1)
    block = jax.ShapeDtypeStruct((width, rows), BF)
    sums = pl.pallas_call(
        sum_kernel,
        out_shape=(jax.ShapeDtypeStruct((width, rows), F32), block, block, block),
        in_specs=[vmem] * 3,
        out_specs=(vmem,) * 4,
        name="sum_cores",
    )(out_first, out_own, d_oth)
    back = [swap(sums[k], k) for k in (1, 2, 3)]

    parts = lax.all_to_all(out_bias, ("x", "y"), 0, 0, tiled=True)
    planes = pl.pallas_call(
        plane_kernel,
        out_shape=jax.ShapeDtypeStruct((NZ, NC, 2, heads, rows // (NZ * NY) // NC, rows), F32),
        in_specs=[smem, vmem, anywhere, anywhere, anywhere],
        out_specs=vmem,
        name="sum_plane",
    )(pos, parts, *back)
    shape = planes.shape
    planes = lax.all_to_all(planes.reshape((-1,) + shape[3:]), ("zh", "core", "tl"), 0, 0, tiled=True)
    planes = jnp.sum(planes.reshape(shape), axis=0)
    bias_grad = jnp.transpose(planes, (2, 0, 1, 4, 3)).reshape(4 * heads, rows, shape[4])

    input_grad = pl.pallas_call(
        final_kernel,
        out_shape=jax.ShapeDtypeStruct((rows, width), BF),
        in_specs=[vmem] * 6,
        out_specs=vmem,
        compiler_params=pltpu.CompilerParams(vmem_limit_bytes=50 * 1024 * 1024),
        name="norm_back",
    )(inputs, gain, sums[0], *back)
    return input_grad[None], bias_grad


def solution(mesh):
    names, toks = tuple(name for name, _ in AXES), tuple(name for name, _ in TOK)
    split = Mesh(mesh.devices.reshape(tuple(n for _, n in AXES + TOK)), names + toks)
    return jax.shard_map(
        on_device,
        mesh=split,
        in_specs=(
            P(names, toks, None),
            P(names, toks, None),
            P(),
            P(names, None),
            P(names, None),
            P(names, None),
            P(names, None),
            P(names, None),
            P(None, toks, None),
            P(),
        ),
        out_specs=(P(names, toks, None), P(None, toks, names)),
        check_vma=False,
    )
```

time: 158 us -> 124 us (0.78)
  starting transfers between devices: 63.8 us -> 40.7 us
  waiting for transfers between devices: 53.9 us -> 46.6 us
  other arithmetic: 5.53 us -> 0.01 us
  Pallas kernels: 20.9 us -> 24.9 us
    ppermute x25 -> x7, starting transfers between devices: 52 us -> 10.5 us  [shift(): lax.ppermute(value, axis, [(i, (i + by) % count) for i in range(count)])]
    ppermute x25 -> x7, waiting for transfers between devices: 28.4 us -> 2.38 us  [shift(): lax.ppermute(value, axis, [(i, (i + by) % count) for i in range(count)])]
    ppermute x3 -> x8, waiting for transfers between devices: 11.1 us -> 31 us  [the longest x7 24.5 us: swap(): return lax.ppermute(value, ('th', 'tl'), [(i, i ^ by) for i in range(NT)])]
    all_to_all x0 -> x2, starting transfers between devices: none -> 14.2 us  [the longest x1 7.22 us: on_device(): lax.all_to_all(planes.reshape((-1,) + shape[3:]), ('zh', 'core', 'tl'), 0...]
    all_to_all x1, waiting for transfers between devices: 14.5 us -> 9.13 us  [on_device(): parts = lax.all_to_all(out_bias, ('x', 'y'), 0, 0, tiled=True)]
    all_to_all x0 -> x2, waiting for transfers between devices: none -> 4.08 us  [the longest x1 4.08 us: on_device(): lax.all_to_all(planes.reshape((-1,) + shape[3:]), ('zh', 'core', 'tl'), 0...]
    pallas_call x1 -> x6, Pallas kernels: 19.7 us -> 23.8 us  [the longest x1 13.5 us: on_device(): pl.pallas_call(attention_kernel, out_shape=(jax.ShapeDtypeStruct((width,...]
    ppermute x3 -> x8, starting transfers between devices: 6.15 us -> 9.5 us  [the longest x7 8.62 us: swap(): return lax.ppermute(value, ('th', 'tl'), [(i, i ^ by) for i in range(NT)])]
  transfers between devices with their start and end apart: 29 -> 18, of which waited for: 8 -> 8; matrix products, arithmetic and copies ran while one was open for 6% -> 1% of each run, Pallas kernels for 1% -> 5%
where the time goes in v2:
time: 124 us
  waiting for transfers between devices  46.6 us (38%)
  starting transfers between devices  40.7 us (33%)
  Pallas kernels  24.9 us (20%)
  local copies, waits for them, and re-layouts  10.7 us (9%)
    ppermute x7, waiting for transfers between devices, swap(): return lax.ppermute(value, ('th', 'tl'), [(i, i ^ by) for i in range(NT)])  24.5 us
    pallas_call x1, Pallas kernels, on_device(): pl.pallas_call(attention_kernel, out_shape=(jax.ShapeDtypeStruct((width,...  13.5 us
    ppermute x7, starting transfers between devices, shift(): lax.ppermute(value, axis, [(i, (i + by) % count) for i in range(count)])  10.5 us
    all_to_all x1, waiting for transfers between devices, on_device(): parts = lax.all_to_all(out_bias, ('x', 'y'), 0, 0, tiled=True)  9.13 us
    ppermute x7, starting transfers between devices, swap(): return lax.ppermute(value, ('th', 'tl'), [(i, i ^ by) for i in range(NT)])  8.62 us
    unnamed x36, local copies, waits for them, and re-layouts  8.22 us
    all_to_all x1, starting transfers between devices, on_device(): lax.all_to_all(planes.reshape((-1,) + shape[3:]), ('zh', 'core', 'tl'), 0...  7.22 us
    all_to_all x1, starting transfers between devices, on_device(): weights = lax.all_to_all(pieces, ('x', 'y'), 0, 0, tiled=True)  6.93 us
  transfers between devices with their start and end apart: 18, of which 8 were waited for; matrix products, arithmetic and copies ran while one was open for 1% of the time, Pallas kernels for 5%

profile of v2, /device:TPU:1, one launch (start us, length us, event | category | flops | bytes accessed | tf_op | source)
XLA Modules:
  0.0 123.7 jit_solution(17781382011022615026)
XLA Ops:
  0.6 1.8 %norm.1.normed = bf16[128,768]{1,0:T(8,128)(2,1)} custom-call(bf16[128,768]{1,0:T(8,128)(2,1)} %bitcast.19, f32[768]{0:T(1024)} %gain.3), custom_call_target="tpu_custom_call" | custom-call | tf_op jit(solution)/shard_map/norm/pallas_call | solution.py:265
  2.5 2.5 %collective-permute-start.3 = (bf16[128,768]{1,0:T(8,128)(2,1)}, bf16[128,768]{1,0:T(8,128)(2,1)S(1)}, u32[]{:S(2)}, u32[]{:S(2)}) collective-permute-start(bf16[128,768]{1,0:T(8,128)(2,1)} %norm.1.normed), channel_id=1, source_target_pairs={{0,1},{1,0},{2,3},{3,2},{4,5},{5,4},{6,7},{7,6},{8,9},{9,8},{10,11... | collective-permute-start | bytes 589832 | tf_op jit(solution)/shard_map/ppermute | solution.py:22
  4.9 0.7 stack.27.pos
  5.6 2.1 %pack.1 = (bf16[12,1536]{1,0:T(8,128)(2,1)}, bf16[12,1536]{1,0:T(8,128)(2,1)}) custom-call(s32[6]{0:T(128)} %stack.27.pos, bf16[12,768]{1,0:T(8,128)(2,1)} %query.1, bf16[12,768]{1,0:T(8,128)(2,1)} %key.1, bf16[12,768]{1,0:T(8,128)(2,1)} %value.1, bf16[12,768]{1,0:T(8,128)(2,1)} %gate.1, bf16[12,768]{1,0:T(8,128)(2,1)} %out.1), custom_call_target="tpu_custom_call" | custom-call | tf_op jit(solution)/shard_map/pack/pallas_call | solution.py:254
  7.7 6.0 %collective-permute-start.1 = (bf16[12,1536]{1,0:T(8,128)(2,1)}, bf16[12,1536]{1,0:T(8,128)(2,1)S(1)}, u32[]{:S(2)}, u32[]{:S(2)}) collective-permute-start(bf16[12,1536]{1,0:T(8,128)(2,1)} %get-tuple-element.14.mine), channel_id=1, source_target_pairs={{0,32},{32,0},{1,33},{33,1},{2,34},{34,2},{3,35},{35,3},{4,36},{36... | collective-permute-start | bytes 110600 | tf_op jit(solution)/shard_map/ppermute | solution.py:18
  13.7 0.9 collective-permute-start.2
  14.5 0.4 collective-permute-start
  14.9 1.3 %collective-permute-done.1.above = bf16[12,1536]{1,0:T(8,128)(2,1)S(1)} collective-permute-done((bf16[12,1536]{1,0:T(8,128)(2,1)}, bf16[12,1536]{1,0:T(8,128)(2,1)S(1)}, u32[]{:S(2)}, u32[]{:S(2)}) %collective-permute-start.1) | collective-permute-done | bytes 36896 | tf_op jit(solution)/shard_map/ppermute | solution.py:18
  16.2 6.5 %collective-permute-done.2.across = bf16[12,1536]{1,0:T(8,128)(2,1)S(1)} collective-permute-done((bf16[12,1536]{1,0:T(8,128)(2,1)}, bf16[12,1536]{1,0:T(8,128)(2,1)S(1)}, u32[]{:S(2)}, u32[]{:S(2)}) %collective-permute-start.2) | collective-permute-done | bytes 36896 | tf_op jit(solution)/shard_map/ppermute | solution.py:263
  22.7 0.9 copy-done
  23.6 0.8 copy-done.11
  24.4 0.7 copy-done.13
  25.1 1.9 %assemble.1 = (bf16[16,48,1152]{2,1,0:T(8,128)(2,1)}, bf16[256,768]{1,0:T(8,128)(2,1)S(1)}) custom-call(s32[6]{0:T(128)S(1)} %copy-done.13, bf16[12,1536]{1,0:T(8,128)(2,1)S(1)} %copy-done.11, bf16[12,1536]{1,0:T(8,128)(2,1)S(1)} %collective-permute-done.beside, bf16[12,1536]{1,0:T(8,128)(2,1)S(1)} %collective-permute-done.1.above, ...), custom_call_target="tpu_custom_call" | custom-call | tf_op jit(solution)/shard_map/assemble/pallas_call | solution.py:274
  27.0 6.9 %all-to-all-start = ((bf16[16,48,1152]{2,1,0:T(8,128)(2,1)}), bf16[16,48,1152]{2,1,0:T(8,128)(2,1)}, u32[]{:S(2)}, u32[]{:S(2)}) async-start(bf16[16,48,1152]{2,1,0:T(8,128)(2,1)} %get-tuple-element.17), calls=%async_computation | async-start | bytes 3538944 | tf_op jit(solution)/shard_map/all_to_all | solution.py:286
  34.0 0.1 collective-permute-start.4
  34.1 1.1 dynamic-slice_bitcast_fusion
  35.2 2.4 %collective-permute-start.10 = (bf16[4,128,512]{2,1,0:T(8,128)(2,1)S(1)}, bf16[4,128,512]{2,1,0:T(8,128)(2,1)S(1)}, u32[]{:S(2)}, u32[]{:S(2)}) collective-permute-start(bf16[4,128,512]{2,1,0:T(8,128)(2,1)S(1)} %dynamic-slice_bitcast_fusion), channel_id=1, source_target_pairs={{0,1},{1,0},{2,3},{3,2},{4,5},{5,4},{6,7},{7,6},{8,9},{9,8},{10,11... | collective-permute-start | bytes 1572872 | tf_op jit(solution)/shard_map/ppermute | solution.py:22
  37.6 0.1 collective-permute-start.7
  37.7 1.4 %collective-permute-start.5 = (bf16[256,768]{1,0:T(8,128)(2,1)S(1)}, bf16[256,768]{1,0:T(8,128)(2,1)S(1)}, u32[]{:S(2)}, u32[]{:S(2)}) collective-permute-start(bf16[256,768]{1,0:T(8,128)(2,1)S(1)} %get-tuple-element.16.own_near), channel_id=1, source_target_pairs={{0,4},{4,0},{1,5},{5,1},{2,6},{6,2},{3,7},{7,3},{8,12},{12,8},{9,1... | collective-permute-start | bytes 1179656 | tf_op jit(solution)/shard_map/ppermute | solution.py:18
  39.1 15.2 %collective-permute-done.4.own_far = bf16[256,768]{1,0:T(8,128)(2,1)S(1)} collective-permute-done((bf16[256,768]{1,0:T(8,128)(2,1)S(1)}, bf16[256,768]{1,0:T(8,128)(2,1)S(1)}, u32[]{:S(2)}, u32[]{:S(2)}) %collective-permute-start.4) | collective-permute-done | bytes 393248 | tf_op jit(solution)/shard_map/ppermute | solution.py:22
  54.3 0.4 collective-permute-start.6
  54.7 0.1 collective-permute-start.8
  54.8 6.3 %collective-permute-done.7.cot_own1 = bf16[128,768]{1,0:T(8,128)(2,1)S(1)} collective-permute-done((bf16[128,768]{1,0:T(8,128)(2,1)S(1)}, bf16[128,768]{1,0:T(8,128)(2,1)S(1)}, u32[]{:S(2)}, u32[]{:S(2)}) %collective-permute-start.7) | collective-permute-done | bytes 196640 | tf_op jit(solution)/shard_map/ppermute | solution.py:22
  61.1 1.9 %collective-permute-start.9 = (bf16[128,768]{1,0:T(8,128)(2,1)S(1)}, bf16[128,768]{1,0:T(8,128)(2,1)S(1)}, u32[]{:S(2)}, u32[]{:S(2)}) collective-permute-start(bf16[128,768]{1,0:T(8,128)(2,1)S(1)} %collective-permute-done.7.cot_own1), channel_id=1, source_target_pairs={{0,4},{4,0},{1,5},{5,1},{2,6},{6,2},{3,7},{7,3},{8,12},{12,8},{9,1... | collective-permute-start | bytes 589832 | tf_op jit(solution)/shard_map/ppermute | solution.py:18
  63.0 1.1 collective-permute-done.9.cot_oth1
  64.1 0.1 broadcast_in_dim.13.valid_col
  64.2 13.5 %attention.1 = (f32[768,128]{1,0:T(8,128)S(1)}, bf16[3,768,128]{2,1,0:T(8,128)(2,1)}, bf16[4,768,128]{2,1,0:T(8,128)(2,1)}, bf16[16,4,2,16,256]{4,3,2,1,0:T(8,128)(2,1)}) custom-call(s32[6]{0:T(128)S(1)} %copy-done.14, bf16[256,768]{1,0:T(8,128)(2,1)S(1)} %get-tuple-element.16.own_near, bf16[256,768]{1,0:T(8,128)(2,1)S(1)} %collective-permute-done.4.own_far, ...), custom_call_target="tpu_custom_call" | custom-call | tf_op jit(solution)/shard_map/attention/pallas_call | solution.py:297
  77.7 0.8 copy-done.8
  78.5 0.4 collective-permute-start.11
  78.9 6.5 %all-to-all-start.1 = ((bf16[16,4,2,16,256]{4,3,2,1,0:T(8,128)(2,1)}), bf16[16,4,2,16,256]{4,3,2,1,0:T(8,128)(2,1)S(1)}, u32[]{:S(2)}, u32[]{:S(2)}) async-start(bf16[16,4,2,16,256]{4,3,2,1,0:T(8,128)(2,1)} %get-tuple-element.25), calls=%async_computation.1 | async-start | bytes 2097152 | tf_op jit(solution)/shard_map/all_to_all | solution.py:335
  85.4 0.0 copy-start.1
  85.4 0.0 copy-start.12
  85.4 0.9 copy-done.16
  86.3 2.4 %sum_cores.1 = (f32[768,128]{1,0:T(8,128)}, bf16[768,128]{1,0:T(8,128)(2,1)}, bf16[768,128]{1,0:T(8,128)(2,1)}, bf16[768,128]{1,0:T(8,128)(2,1)}) custom-call(f32[768,128]{1,0:T(8,128)} %copy-done.8, bf16[3,768,128]{2,1,0:T(8,128)(2,1)} %get-tuple-element.19.own, bf16[4,768,128]{2,1,0:T(8,128)(2,1)} %copy-done.16), custom_call_target="tpu_custom_call" | custom-call | tf_op jit(solution)/shard_map/sum_cores/pallas_call | solution.py:326
  88.7 1.6 %collective-permute-start.13 = (bf16[768,128]{1,0:T(8,128)(2,1)}, bf16[768,128]{1,0:T(8,128)(2,1)S(1)}, u32[]{:S(2)}, u32[]{:S(2)}) collective-permute-start(bf16[768,128]{1,0:T(8,128)(2,1)} %get-tuple-element.23), channel_id=1, source_target_pairs={{0,2},{1,3},{2,0},{3,1},{4,6},{5,7},{6,4},{7,5},{8,10},{9,11},{10,... | collective-permute-start | bytes 589832 | tf_op jit(solution)/shard_map/ppermute | solution.py:22
  90.3 2.0 %collective-permute-start.14 = (bf16[768,128]{1,0:T(8,128)(2,1)}, bf16[768,128]{1,0:T(8,128)(2,1)S(1)}, u32[]{:S(2)}, u32[]{:S(2)}) collective-permute-start(bf16[768,128]{1,0:T(8,128)(2,1)} %get-tuple-element.24), channel_id=1, source_target_pairs={{0,3},{1,2},{2,1},{3,0},{4,7},{5,6},{6,5},{7,4},{8,11},{9,10},{10,... | collective-permute-start | bytes 589832 | tf_op jit(solution)/shard_map/ppermute | solution.py:22
  92.3 9.1 %all-to-all-done.1.parts = bf16[16,4,2,16,256]{4,3,2,1,0:T(8,128)(2,1)S(1)} async-done(((bf16[16,4,2,16,256]{4,3,2,1,0:T(8,128)(2,1)}), bf16[16,4,2,16,256]{4,3,2,1,0:T(8,128)(2,1)S(1)}, u32[]{:S(2)}, u32[]{:S(2)}) %all-to-all-start.1) | async-done | bytes 1048608 | tf_op jit(solution)/shard_map/all_to_all | solution.py:335
  101.4 3.0 %collective-permute-done.13.r2 = bf16[768,128]{1,0:T(8,128)(2,1)S(1)} collective-permute-done((bf16[768,128]{1,0:T(8,128)(2,1)}, bf16[768,128]{1,0:T(8,128)(2,1)S(1)}, u32[]{:S(2)}, u32[]{:S(2)}) %collective-permute-start.13) | collective-permute-done | bytes 196640 | tf_op jit(solution)/shard_map/ppermute | solution.py:22
  104.5 0.7 copy-done.4
  105.1 0.7 copy-done.6
  105.8 2.0 %sum_plane.1 = f32[2,2,2,4,8,128]{5,4,3,2,1,0:T(8,128)} custom-call(s32[6]{0:T(128)} %stack.27.pos, bf16[16,4,2,16,256]{4,3,2,1,0:T(8,128)(2,1)} %copy-done.15, bf16[768,128]{1,0:T(8,128)(2,1)} %copy-done.2, bf16[768,128]{1,0:T(8,128)(2,1)} %copy-done.4, bf16[768,128]{1,0:T(8,128)(2,1)} %copy-done.6), custom_call_target="tpu_custom_call" | custom-call | tf_op jit(solution)/shard_map/sum_plane/pallas_call | solution.py:336
  107.8 7.2 %all-to-all-start.2 = ((f32[8,4,8,128]{3,2,1,0:T(8,128)}), f32[8,4,8,128]{3,2,1,0:T(8,128)S(1)}, u32[]{:S(2)}, u32[]{:S(2)}) async-start(f32[8,4,8,128]{3,2,1,0:T(8,128)} %bitcast.27), calls=%async_computation.2 | async-start | bytes 262144 | tf_op jit(solution)/shard_map/all_to_all | solution.py:344
  115.1 0.9 copy-done.3
  116.0 0.9 copy-done.5
  116.9 0.9 copy-done.7
  117.9 1.1 norm_back.1
  119.0 4.1 %all-to-all-done.2 = f32[8,4,8,128]{3,2,1,0:T(8,128)S(1)} async-done(((f32[8,4,8,128]{3,2,1,0:T(8,128)}), f32[8,4,8,128]{3,2,1,0:T(8,128)S(1)}, u32[]{:S(2)}, u32[]{:S(2)}) %all-to-all-start.2) | async-done | bytes 131104 | tf_op jit(solution)/shard_map/all_to_all | solution.py:344
  123.1 0.6 copy.15
  (37 shorter events, 0.1 us)
Async XLA Ops:
  2.5 20.3 %collective-permute-start.3 = (bf16[128,768]{1,0:T(8,128)(2,1)}, bf16[128,768]{1,0:T(8,128)(2,1)S(1)}, u32[]{:S(2)}, u32[]{:S(2)}) collective-permute-start(bf16[128,768]{1,0:T(8,128)(2,1)} %norm.1.normed), channel_id=1, source_target_pairs={{0,1},{1,0},{2,3},{3,2},{4,5},{5,4},{6,7},{7,6},{8,9},{9,8},{10,11... | collective-permute-start | bytes 589832 | tf_op jit(solution)/shard_map/ppermute | solution.py:22
  7.7 8.6 %collective-permute-start.1 = (bf16[12,1536]{1,0:T(8,128)(2,1)}, bf16[12,1536]{1,0:T(8,128)(2,1)S(1)}, u32[]{:S(2)}, u32[]{:S(2)}) collective-permute-start(bf16[12,1536]{1,0:T(8,128)(2,1)} %get-tuple-element.14.mine), channel_id=1, source_target_pairs={{0,32},{32,0},{1,33},{33,1},{2,34},{34,2},{3,35},{35,3},{4,36},{36... | collective-permute-start | bytes 110600 | tf_op jit(solution)/shard_map/ppermute | solution.py:18
  13.7 9.0 %collective-permute-start.2 = (bf16[12,1536]{1,0:T(8,128)(2,1)}, bf16[12,1536]{1,0:T(8,128)(2,1)S(1)}, u32[]{:S(2)}, u32[]{:S(2)}) collective-permute-start(bf16[12,1536]{1,0:T(8,128)(2,1)} %get-tuple-element.15), channel_id=1, source_target_pairs={{0,36},{36,0},{4,32},{32,4},{1,37},{37,1},{5,33},{33,5},{2,38},{38... | collective-permute-start | bytes 110600 | tf_op jit(solution)/shard_map/ppermute | solution.py:263
  14.5 8.2 %collective-permute-start = (bf16[12,1536]{1,0:T(8,128)(2,1)}, bf16[12,1536]{1,0:T(8,128)(2,1)S(1)}, u32[]{:S(2)}, u32[]{:S(2)}) collective-permute-start(bf16[12,1536]{1,0:T(8,128)(2,1)} %get-tuple-element.15), channel_id=1, source_target_pairs={{0,4},{4,0},{1,5},{5,1},{2,6},{6,2},{3,7},{7,3},{8,12},{12,8},{9,1... | collective-permute-start | bytes 110600 | tf_op jit(solution)/shard_map/ppermute | solution.py:18
  22.7 0.9 copy-start
  23.6 0.8 copy-start.11
  24.4 0.7 copy-start.13
  27.0 10.6 %copy-start.10 = (bf16[1,128,768]{2,1,0:T(8,128)(2,1)S(1)}, bf16[1,128,768]{2,1,0:T(8,128)(2,1)}, u32[]{:S(2)}) copy-start(bf16[1,128,768]{2,1,0:T(8,128)(2,1)} %param.11) | copy-start | bytes 589828
  27.0 36.0 %copy-start.17 = (s32[512]{0:T(512)S(1)}, s32[512]{0:T(512)}, u32[]{:S(2)}) copy-start(s32[512]{0:T(512)} %param.19) | copy-start | bytes 6148
  27.0 37.2 %copy-start.14 = (s32[6]{0:T(128)S(1)}, s32[6]{0:T(128)}, u32[]{:S(2)}) copy-start(s32[6]{0:T(128)} %stack.27.pos) | copy-start | bytes 76
  27.0 37.1 %all-to-all-start = ((bf16[16,48,1152]{2,1,0:T(8,128)(2,1)}), bf16[16,48,1152]{2,1,0:T(8,128)(2,1)}, u32[]{:S(2)}, u32[]{:S(2)}) async-start(bf16[16,48,1152]{2,1,0:T(8,128)(2,1)} %get-tuple-element.17), calls=%async_computation | async-start | bytes 3538944 | tf_op jit(solution)/shard_map/all_to_all | solution.py:286
  34.0 20.3 %collective-permute-start.4 = (bf16[256,768]{1,0:T(8,128)(2,1)S(1)}, bf16[256,768]{1,0:T(8,128)(2,1)S(1)}, u32[]{:S(2)}, u32[]{:S(2)}) collective-permute-start(bf16[256,768]{1,0:T(8,128)(2,1)S(1)} %get-tuple-element.16.own_near), channel_id=1, source_target_pairs={{0,2},{1,3},{2,0},{3,1},{4,6},{5,7},{6,4},{7,5},{8,10},{9,11},{10,... | collective-permute-start | bytes 1179656 | tf_op jit(solution)/shard_map/ppermute | solution.py:22
  35.2 28.9 %collective-permute-start.10 = (bf16[4,128,512]{2,1,0:T(8,128)(2,1)S(1)}, bf16[4,128,512]{2,1,0:T(8,128)(2,1)S(1)}, u32[]{:S(2)}, u32[]{:S(2)}) collective-permute-start(bf16[4,128,512]{2,1,0:T(8,128)(2,1)S(1)} %dynamic-slice_bitcast_fusion), channel_id=1, source_target_pairs={{0,1},{1,0},{2,3},{3,2},{4,5},{5,4},{6,7},{7,6},{8,9},{9,8},{10,11... | collective-permute-start | bytes 1572872 | tf_op jit(solution)/shard_map/ppermute | solution.py:22
  37.6 23.5 %collective-permute-start.7 = (bf16[128,768]{1,0:T(8,128)(2,1)S(1)}, bf16[128,768]{1,0:T(8,128)(2,1)S(1)}, u32[]{:S(2)}, u32[]{:S(2)}) collective-permute-start(bf16[128,768]{1,0:T(8,128)(2,1)S(1)} %bitcast.21), channel_id=1, source_target_pairs={{0,1},{1,0},{2,3},{3,2},{4,5},{5,4},{6,7},{7,6},{8,9},{9,8},{10,11... | collective-permute-start | bytes 589832 | tf_op jit(solution)/shard_map/ppermute | solution.py:22
  37.7 26.4 %collective-permute-start.5 = (bf16[256,768]{1,0:T(8,128)(2,1)S(1)}, bf16[256,768]{1,0:T(8,128)(2,1)S(1)}, u32[]{:S(2)}, u32[]{:S(2)}) collective-permute-start(bf16[256,768]{1,0:T(8,128)(2,1)S(1)} %get-tuple-element.16.own_near), channel_id=1, source_target_pairs={{0,4},{4,0},{1,5},{5,1},{2,6},{6,2},{3,7},{7,3},{8,12},{12,8},{9,1... | collective-permute-start | bytes 1179656 | tf_op jit(solution)/shard_map/ppermute | solution.py:18
  54.3 9.8 %collective-permute-start.6 = (bf16[256,768]{1,0:T(8,128)(2,1)S(1)}, bf16[256,768]{1,0:T(8,128)(2,1)S(1)}, u32[]{:S(2)}, u32[]{:S(2)}) collective-permute-start(bf16[256,768]{1,0:T(8,128)(2,1)S(1)} %collective-permute-done.4.own_far), channel_id=1, source_target_pairs={{0,4},{4,0},{1,5},{5,1},{2,6},{6,2},{3,7},{7,3},{8,12},{12,8},{9,1... | collective-permute-start | bytes 1179656 | tf_op jit(solution)/shard_map/ppermute | solution.py:18
  54.7 8.3 %collective-permute-start.8 = (bf16[128,768]{1,0:T(8,128)(2,1)S(1)}, bf16[128,768]{1,0:T(8,128)(2,1)S(1)}, u32[]{:S(2)}, u32[]{:S(2)}) collective-permute-start(bf16[128,768]{1,0:T(8,128)(2,1)S(1)} %bitcast.22), channel_id=1, source_target_pairs={{0,4},{4,0},{1,5},{5,1},{2,6},{6,2},{3,7},{7,3},{8,12},{12,8},{9,1... | collective-permute-start | bytes 589832 | tf_op jit(solution)/shard_map/ppermute | solution.py:18
  61.1 2.9 %collective-permute-start.9 = (bf16[128,768]{1,0:T(8,128)(2,1)S(1)}, bf16[128,768]{1,0:T(8,128)(2,1)S(1)}, u32[]{:S(2)}, u32[]{:S(2)}) collective-permute-start(bf16[128,768]{1,0:T(8,128)(2,1)S(1)} %collective-permute-done.7.cot_own1), channel_id=1, source_target_pairs={{0,4},{4,0},{1,5},{5,1},{2,6},{6,2},{3,7},{7,3},{8,12},{12,8},{9,1... | collective-permute-start | bytes 589832 | tf_op jit(solution)/shard_map/ppermute | solution.py:18
  77.7 0.8 copy-start.8
  78.5 6.9 %collective-permute-start.11 = (bf16[4,768,128]{2,1,0:T(8,128)(2,1)}, bf16[4,768,128]{2,1,0:T(8,128)(2,1)S(1)}, u32[]{:S(2)}, u32[]{:S(2)}) collective-permute-start(bf16[4,768,128]{2,1,0:T(8,128)(2,1)} %get-tuple-element.20), channel_id=1, source_target_pairs={{0,4},{4,0},{1,5},{5,1},{2,6},{6,2},{3,7},{7,3},{8,12},{12,8},{9,1... | collective-permute-start | bytes 2359304 | tf_op jit(solution)/shard_map/ppermute | solution.py:18
  78.9 22.6 %all-to-all-start.1 = ((bf16[16,4,2,16,256]{4,3,2,1,0:T(8,128)(2,1)}), bf16[16,4,2,16,256]{4,3,2,1,0:T(8,128)(2,1)S(1)}, u32[]{:S(2)}, u32[]{:S(2)}) async-start(bf16[16,4,2,16,256]{4,3,2,1,0:T(8,128)(2,1)} %get-tuple-element.25), calls=%async_computation.1 | async-start | bytes 2097152 | tf_op jit(solution)/shard_map/all_to_all | solution.py:335
  85.4 29.7 %copy-start.1 = (bf16[1,128,768]{2,1,0:T(8,128)(2,1)S(1)}, bf16[1,128,768]{2,1,0:T(8,128)(2,1)}, u32[]{:S(2)}) copy-start(bf16[1,128,768]{2,1,0:T(8,128)(2,1)} %param.10) | copy-start | bytes 589828
  85.4 29.7 %copy-start.12 = (f32[768]{0:T(1024)S(1)}, f32[768]{0:T(1024)}, u32[]{:S(2)}) copy-start(f32[768]{0:T(1024)} %gain.3) | copy-start | bytes 9220
  85.4 0.9 copy-start.16
  88.7 26.3 %copy-start.9 = (f32[768,128]{1,0:T(8,128)S(1)}, f32[768,128]{1,0:T(8,128)}, u32[]{:S(2)}) copy-start(f32[768,128]{1,0:T(8,128)} %get-tuple-element.21.r0) | copy-start | bytes 1179652
  88.7 12.7 %collective-permute-start.12 = (bf16[768,128]{1,0:T(8,128)(2,1)}, bf16[768,128]{1,0:T(8,128)(2,1)S(1)}, u32[]{:S(2)}, u32[]{:S(2)}) collective-permute-start(bf16[768,128]{1,0:T(8,128)(2,1)} %get-tuple-element.22), channel_id=1, source_target_pairs={{0,1},{1,0},{2,3},{3,2},{4,5},{5,4},{6,7},{7,6},{8,9},{9,8},{10,11... | collective-permute-start | bytes 589832 | tf_op jit(solution)/shard_map/ppermute | solution.py:22
  88.7 15.7 %collective-permute-start.13 = (bf16[768,128]{1,0:T(8,128)(2,1)}, bf16[768,128]{1,0:T(8,128)(2,1)S(1)}, u32[]{:S(2)}, u32[]{:S(2)}) collective-permute-start(bf16[768,128]{1,0:T(8,128)(2,1)} %get-tuple-element.23), channel_id=1, source_target_pairs={{0,2},{1,3},{2,0},{3,1},{4,6},{5,7},{6,4},{7,5},{8,10},{9,11},{10,... | collective-permute-start | bytes 589832 | tf_op jit(solution)/shard_map/ppermute | solution.py:22
  90.3 14.1 %collective-permute-start.14 = (bf16[768,128]{1,0:T(8,128)(2,1)}, bf16[768,128]{1,0:T(8,128)(2,1)S(1)}, u32[]{:S(2)}, u32[]{:S(2)}) collective-permute-start(bf16[768,128]{1,0:T(8,128)(2,1)} %get-tuple-element.24), channel_id=1, source_target_pairs={{0,3},{1,2},{2,1},{3,0},{4,7},{5,6},{6,5},{7,4},{8,11},{9,10},{10,... | collective-permute-start | bytes 589832 | tf_op jit(solution)/shard_map/ppermute | solution.py:22
  101.4 3.0 %copy-start.15 = (bf16[16,4,2,16,256]{4,3,2,1,0:T(8,128)(2,1)}, bf16[16,4,2,16,256]{4,3,2,1,0:T(8,128)(2,1)S(1)}, u32[]{:S(2)}) copy-start(bf16[16,4,2,16,256]{4,3,2,1,0:T(8,128)(2,1)S(1)} %all-to-all-done.1.parts) | copy-start | bytes 3145732
  101.4 3.0 %copy-start.2 = (bf16[768,128]{1,0:T(8,128)(2,1)}, bf16[768,128]{1,0:T(8,128)(2,1)S(1)}, u32[]{:S(2)}) copy-start(bf16[768,128]{1,0:T(8,128)(2,1)S(1)} %collective-permute-done.12.r1) | copy-start | bytes 589828
  104.4 0.7 copy-start.4
  105.1 0.7 copy-start.6
  107.8 15.2 %all-to-all-start.2 = ((f32[8,4,8,128]{3,2,1,0:T(8,128)}), f32[8,4,8,128]{3,2,1,0:T(8,128)S(1)}, u32[]{:S(2)}, u32[]{:S(2)}) async-start(f32[8,4,8,128]{3,2,1,0:T(8,128)} %bitcast.27), calls=%async_computation.2 | async-start | bytes 262144 | tf_op jit(solution)/shard_map/all_to_all | solution.py:344
  115.1 0.9 copy-start.3
  116.0 0.9 copy-start.5
  116.9 0.9 copy-start.7

commit v3 on v2

--- a/solution.py
+++ b/solution.py
@@ -35,8 +35,8 @@
     own_near, own_far, oth_near, oth_far,
     cot_own0, cot_own1, cot_oth0, cot_oth1,
     weights,
-    bias, bias_pair, valid_row, valid_col,
-    out_first, out_own, out_oth, out_bias,
+    bias, bias_pair, valid_row,
+    own_near_out, own_far_out, own_go, oth_keep, oth_go, out_bias,
     wf, wo, wb, dgt, kv, km, kvt, qt, gt, dx, dqg,
 ):
     heads = bias_pair.shape[0]
@@ -62,23 +62,28 @@
     mine = jnp.concatenate(
         [wo[pl.ds(pl.multiple_of(j * rz + pair * size, 8), size), :] for j in range(heads)], axis=0
     ).astype(BF)
-    for s, cots in enumerate(((cot_own0, cot_own1), (cot_oth0, cot_oth1))):
-        for u, cot in enumerate(cots):
-            dgt[s, :, u * rows:(u + 1) * rows] = nt(mine, cot[...])
-
-    for s, tokens in enumerate(((own_near, own_far), (oth_near, oth_far))):
-        for r in range(NT):
-            n = tokens[r // 2][r % 2 * rows:(r % 2 + 1) * rows, :]
-            lo = pl.multiple_of((tok ^ r) * rows, rows)
-            both = nn(n, wb[:, : 2 * part])
-            kvt[s, :, pl.ds(lo, rows)] = both.T.astype(BF)
-            kv[s, pl.ds(lo, rows), :] = both.astype(BF)
-            keep = valid_col[pl.ds(lo, rows), :]
-            for j in range(2):
-                km[s, pl.ds(lo, rows), j * 128:(j + 1) * 128] = (both[:, j * 128:(j + 1) * 128] * keep).astype(BF)
-        both = nn(tokens[0][...], wb[:, 2 * part:]).T
-        qt[s] = both[:part].astype(BF)
-        gt[s] = jax.nn.sigmoid(both[part:].astype(BF).astype(F32))
+    cots = jnp.concatenate([cot_own0[...], cot_own1[...], cot_oth0[...], cot_oth1[...]], axis=0)
+    both = nt(mine, cots)
+    for s in range(2):
+        dgt[s] = both[:, 2 * s * rows:2 * (s + 1) * rows]
+
+    starts = [pl.multiple_of((tok ^ r) * rows, rows) for r in range(NT)]
+    tokens = jnp.concatenate([own_near[...], own_far[...], oth_near[...], oth_far[...]], axis=0)
+    both = nn(tokens, wb[:, : 2 * part])
+    keep = jnp.concatenate(
+        [jnp.broadcast_to(valid_row[:, pl.ds(at, rows)], (rows, rows)).T for at in starts], axis=0
+    )
+    for s in range(2):
+        one = both[s * NT * rows:(s + 1) * NT * rows]
+        kv[s] = one.astype(BF)
+        kvt[s] = one.T.astype(BF)
+        for j in range(2):
+            km[s, :, j * 128:(j + 1) * 128] = (one[:, j * 128:(j + 1) * 128] * keep).astype(BF)
+    both = nn(jnp.concatenate([own_near[...], oth_near[...]], axis=0), wb[:, 2 * part:]).T
+    for s in range(2):
+        one = both[:, 2 * s * rows:2 * (s + 1) * rows]
+        qt[s] = one[:part].astype(BF)
+        gt[s] = jax.nn.sigmoid(one[part:].astype(BF).astype(F32))
 
     def widen(block, first):
         low = first // 128 * 128
@@ -93,10 +98,12 @@
     for h in range(heads):
         first = h * size
         at = slice(first, first + size)
-        biases = (bias[4 * h + 2 * core + pair], bias_pair[h])
-        bias_t = jnp.concatenate(
-            [jnp.where(valid_row[...] > 0.0, b.astype(F32), NEG).T for b in biases], axis=1
-        )
+        blocks = []
+        for start in starts:
+            keys = pl.ds(start, rows)
+            both = jnp.concatenate([bias[h, :, keys], bias_pair[h, :, keys]], axis=0)
+            blocks.append(jnp.where(valid_row[:, keys] > 0.0, both.astype(F32), NEG).T)
+        bias_t = jnp.concatenate(blocks, axis=0)
         total = None
         for s in range(2):
             q_h = qt[s, at, :]
@@ -121,24 +128,25 @@
             dx[s, at, :] = (nt(q_h, ds_b) * scale).astype(BF)
             dx[s, part + first:part + first + size, :] = nt(da_h, probs_b).astype(BF)
         each = rows // (NZ * NY)
-        for to_x in range(NX):
+        for r in range(NT):
             for z in range(NZ):
                 for to_y in range(NY):
-                    lo = to_x * rows + z * (rows // NZ) + to_y * each
-                    out_bias[to_x * NY + to_y, h, z] = total[lo:lo + each, :].astype(BF)
+                    lo = r * rows + z * (rows // NZ) + to_y * each
+                    out_bias[(tok ^ r) * NY + to_y, h, z] = total[lo:lo + each, :].astype(BF)
 
     for s in range(2):
-        for r in range(NT):
-            at = pl.multiple_of((tok ^ r) * rows, rows)
-            d = nn(wb[:, : 2 * part], dx[s, :, pl.ds(at, rows)])
-            if r < 2:
-                d = d + nn(wb[:, 2 * part:], dqg[s, :, r * rows:(r + 1) * rows])
-            if s == 1:
-                out_oth[r] = d.astype(BF)
-            elif r == 0:
-                out_first[...] = d
-            else:
-                out_own[r - 1] = d.astype(BF)
+        wide = 2 * rows
+        near = nn(wb[...], jnp.concatenate([dx[s, :, :wide], dqg[s]], axis=0))
+        far = nn(wb[:, : 2 * part], dx[s, :, wide:])
+        go = own_go if s == 0 else oth_go
+        go[0] = near[:, rows:].astype(BF)
+        go[1] = far[:, rows:].astype(BF)
+        if s == 0:
+            own_near_out[...] = near[:, :rows]
+            own_far_out[...] = far[:, :rows]
+        else:
+            oth_keep[0] = near[:, :rows].astype(BF)
+            oth_keep[1] = far[:, :rows].astype(BF)
 
 
 def pack_kernel(pos, query, key, value, gate, out, mine, send):
@@ -197,24 +205,28 @@
         part[k, :, cols:] = tail
 
 
-def sum_kernel(first, own, oth, s0, s1, s2, s3):
-    s0[...] = first[...] + oth[0].astype(F32)
-    for k, out in enumerate((s1, s2, s3)):
-        out[...] = (own[k].astype(F32) + oth[k + 1].astype(F32)).astype(BF)
-
-
-def plane_kernel(pos, parts, r1, r2, r3, out):
+def sum_kernel(own, oth, out):
+    out[...] = (own[...].astype(F32) + oth[...].astype(F32)).astype(BF)
+
+
+def halve_kernel(own_near, own_far, oth, got, near, far):
+    near[...] = own_near[...] + oth[0].astype(F32) + got[0].astype(F32)
+    far[...] = (own_far[...] + oth[1].astype(F32) + got[1].astype(F32)).astype(BF)
+
+
+def plane_kernel(pos, parts, after, out):
     rows = out.shape[-1]
     each = out.shape[-2]
     total = jnp.sum(parts[...].astype(F32), axis=0)
     for z in range(NZ):
         for c in range(NC):
             for u in range(2):
-                out[z, c, pos[5] ^ u] = total[:, z, c * each:(c + 1) * each, u * rows:(u + 1) * rows]
-
-
-def final_kernel(inputs, gain, r0, r1, r2, r3, out):
-    d = r0[...] + r1[...].astype(F32) + r2[...].astype(F32) + r3[...].astype(F32)
+                block = total[:, z, c * each:(c + 1) * each, u * rows:(u + 1) * rows]
+                out[z, c, pos[5] ^ u] = block.astype(BF)
+
+
+def final_kernel(inputs, gain, near, back, out):
+    d = near[...] + back[...].astype(F32)
     g = d.T * gain[...][None, :]
     xf = inputs[...].astype(F32)
     mean = jnp.mean(xf, axis=-1, keepdims=True)
@@ -249,6 +261,7 @@
     smem = pl.BlockSpec(memory_space=pltpu.SMEM)
     anywhere = pl.BlockSpec(memory_space=pl.ANY)
     gain = layer_norm_scale
+    room = pltpu.CompilerParams(vmem_limit_bytes=58 * 1024 * 1024)
 
     packed = jax.ShapeDtypeStruct((query_weight.shape[0], 2 * width), BF)
     mine, send = pl.pallas_call(
@@ -279,7 +292,7 @@
         ),
         in_specs=[smem] + [vmem] * 6,
         out_specs=(vmem, vmem),
-        compiler_params=pltpu.CompilerParams(vmem_limit_bytes=30 * 1024 * 1024),
+        compiler_params=room,
         name="assemble",
     )(pos, mine, beside, above, across, normed, beyond)
     own_far = swap(own_near, 2)
@@ -288,22 +301,26 @@
     cot_pair = swap(cotangent, 1)
     cots = [cotangent, cot_pair, shift(cotangent, "core", NC, 1), shift(cot_pair, "core", NC, 1)]
     groups = pair_bias.reshape((heads, NC, 2) + pair_bias.shape[1:])
-    theirs = lax.dynamic_index_in_dim(lax.dynamic_index_in_dim(groups, core, 1, False), 1 - tl, 1, False)
+    groups = lax.dynamic_index_in_dim(groups, core, 1, False)
+    theirs = lax.dynamic_index_in_dim(groups, 1 - tl, 1, False)
+    bias_mine = lax.dynamic_index_in_dim(groups, tl, 1, False)
     bias_pair = swap(theirs, 1)
 
     valid = (atom_count > 0).astype(F32)
     operands = [own_near, own_far, oth_near, oth_far] + cots + [weights]
-    operands += [pair_bias, bias_pair, valid[None, :], jnp.broadcast_to(valid[:, None], (total, 128))]
-    out_first, out_own, out_oth, out_bias = pl.pallas_call(
+    operands += [bias_mine, bias_pair, valid[None, :]]
+    own_near_out, own_far_out, own_go, oth_keep, oth_go, out_bias = pl.pallas_call(
         attention_kernel,
         out_shape=(
             jax.ShapeDtypeStruct((width, rows), F32),
-            jax.ShapeDtypeStruct((NT - 1, width, rows), BF),
-            jax.ShapeDtypeStruct((NT, width, rows), BF),
+            jax.ShapeDtypeStruct((width, rows), F32),
+            jax.ShapeDtypeStruct((2, width, rows), BF),
+            jax.ShapeDtypeStruct((2, width, rows), BF),
+            jax.ShapeDtypeStruct((2, width, rows), BF),
             jax.ShapeDtypeStruct((NX * NY, heads, NZ, rows // (NZ * NY), 2 * rows), BF),
         ),
         in_specs=[smem] + [vmem] * len(operands),
-        out_specs=(vmem,) * 4,
+        out_specs=(vmem,) * 6,
         scratch_shapes=[
             pltpu.VMEM((width, width), F32),
             pltpu.VMEM((width // 2, width), F32),
@@ -317,42 +334,50 @@
             pltpu.VMEM((2, 2 * part, total), BF),
             pltpu.VMEM((2, 2 * part, 2 * rows), BF),
         ],
-        compiler_params=pltpu.CompilerParams(vmem_limit_bytes=50 * 1024 * 1024),
+        compiler_params=room,
         name="attention",
     )(pos, *operands)
 
-    d_oth = shift(out_oth, "core", NC, 1)
-    block = jax.ShapeDtypeStruct((width, rows), BF)
-    sums = pl.pallas_call(
+    go = pl.pallas_call(
         sum_kernel,
-        out_shape=(jax.ShapeDtypeStruct((width, rows), F32), block, block, block),
-        in_specs=[vmem] * 3,
-        out_specs=(vmem,) * 4,
+        out_shape=jax.ShapeDtypeStruct((2, width, rows), BF),
+        in_specs=[vmem, vmem],
+        out_specs=vmem,
+        compiler_params=room,
         name="sum_cores",
-    )(out_first, out_own, d_oth)
-    back = [swap(sums[k], k) for k in (1, 2, 3)]
+    )(own_go, shift(oth_go, "core", NC, 1))
+    near, far = pl.pallas_call(
+        halve_kernel,
+        out_shape=(jax.ShapeDtypeStruct((width, rows), F32), jax.ShapeDtypeStruct((width, rows), BF)),
+        in_specs=[vmem] * 4,
+        out_specs=(vmem, vmem),
+        compiler_params=room,
+        name="sum_pair",
+    )(own_near_out, own_far_out, shift(oth_keep, "core", NC, 1), swap(go, 1))
+    back = swap(far, 2)
 
     parts = lax.all_to_all(out_bias, ("x", "y"), 0, 0, tiled=True)
     planes = pl.pallas_call(
         plane_kernel,
-        out_shape=jax.ShapeDtypeStruct((NZ, NC, 2, heads, rows // (NZ * NY) // NC, rows), F32),
-        in_specs=[smem, vmem, anywhere, anywhere, anywhere],
+        out_shape=jax.ShapeDtypeStruct((NZ, NC, 2, heads, rows // (NZ * NY) // NC, rows), BF),
+        in_specs=[smem, vmem, anywhere],
         out_specs=vmem,
+        compiler_params=room,
         name="sum_plane",
-    )(pos, parts, *back)
+    )(pos, parts, far)
     shape = planes.shape
     planes = lax.all_to_all(planes.reshape((-1,) + shape[3:]), ("zh", "core", "tl"), 0, 0, tiled=True)
-    planes = jnp.sum(planes.reshape(shape), axis=0)
+    planes = jnp.sum(planes.reshape(shape).astype(F32), axis=0)
     bias_grad = jnp.transpose(planes, (2, 0, 1, 4, 3)).reshape(4 * heads, rows, shape[4])
 
     input_grad = pl.pallas_call(
         final_kernel,
         out_shape=jax.ShapeDtypeStruct((rows, width), BF),
-        in_specs=[vmem] * 6,
+        in_specs=[vmem] * 4,
         out_specs=vmem,
-        compiler_params=pltpu.CompilerParams(vmem_limit_bytes=50 * 1024 * 1024),
+        compiler_params=room,
         name="norm_back",
-    )(inputs, gain, sums[0], *back)
+    )(inputs, gain, near, back)
     return input_grad[None], bias_grad
 
 

time: 124 us -> 121 us (0.976)
  starting transfers between devices: 40.7 us -> 35.4 us
  Pallas kernels: 24.9 us -> 27.5 us
    ppermute x7 -> x6, waiting for transfers between devices: 24.5 us -> 36.3 us  [swap(): return lax.ppermute(value, ('th', 'tl'), [(i, i ^ by) for i in range(NT)])]
    all_to_all x1, waiting for transfers between devices: 9.13 us -> 0.01 us  [on_device(): parts = lax.all_to_all(out_bias, ('x', 'y'), 0, 0, tiled=True)]
    all_to_all x1, waiting for transfers between devices: 4.08 us -> 0.01 us  [on_device(): lax.all_to_all(planes.reshape((-1,) + shape[3:]), ('zh', 'core', 'tl'), 0...]
    ppermute x7 -> x6, starting transfers between devices: 8.62 us -> 5.28 us  [swap(): return lax.ppermute(value, ('th', 'tl'), [(i, i ^ by) for i in range(NT)])]
    all_to_all x1, starting transfers between devices: 7.22 us -> 4.42 us  [on_device(): lax.all_to_all(planes.reshape((-1,) + shape[3:]), ('zh', 'core', 'tl'), 0...]
    unnamed x36 -> x40, local copies, waits for them, and re-layouts: 8.22 us -> 6.48 us
    pallas_call x1 -> x2, Pallas kernels: 2.44 us -> 4.17 us  [the longest x1 2.21 us: on_device(): pl.pallas_call(halve_kernel, out_shape=(jax.ShapeDtypeStruct((width, rows...]
    ppermute x7 -> x8, waiting for transfers between devices: 2.38 us -> 3.05 us  [shift(): lax.ppermute(value, axis, [(i, (i + by) % count) for i in range(count)])]
  transfers between devices with their start and end apart: 18 -> 18, of which waited for: 8 -> 8; matrix products, arithmetic and copies ran while one was open for 1% -> 3% of each run, Pallas kernels for 5% -> 9%
where the time goes in v3:
time: 121 us; the launch traced here: 120 us
  waiting for transfers between devices  45.9 us (38%)
  starting transfers between devices  35.4 us (29%)
  Pallas kernels  27.5 us (23%)
  local copies, waits for them, and re-layouts  9.86 us (8%)
    ppermute x6, waiting for transfers between devices, swap(): return lax.ppermute(value, ('th', 'tl'), [(i, i ^ by) for i in range(NT)])  36.3 us
    pallas_call x1, Pallas kernels, on_device(): pl.pallas_call(attention_kernel, out_shape=(jax.ShapeDtypeStruct((width,...  12.6 us
    ppermute x8, starting transfers between devices, shift(): lax.ppermute(value, axis, [(i, (i + by) % count) for i in range(count)])  11.1 us
    all_to_all x1, starting transfers between devices, on_device(): weights = lax.all_to_all(pieces, ('x', 'y'), 0, 0, tiled=True)  6.9 us
    all_to_all x1, starting transfers between devices, on_device(): parts = lax.all_to_all(out_bias, ('x', 'y'), 0, 0, tiled=True)  6.8 us
    ppermute x1, waiting for transfers between devices, on_device(): lax.ppermute(send, ('zh', 'core'), [(0, 3), (3, 0), (1, 2), (2, 1)])  6.49 us
    unnamed x40, local copies, waits for them, and re-layouts  6.48 us
    ppermute x6, starting transfers between devices, swap(): return lax.ppermute(value, ('th', 'tl'), [(i, i ^ by) for i in range(NT)])  5.28 us
  transfers between devices with their start and end apart: 18, of which 8 were waited for; matrix products, arithmetic and copies ran while one was open for 3% of the time, Pallas kernels for 9%

profile of v3, /device:TPU:1, one launch (start us, length us, event | category | flops | bytes accessed | tf_op | source)
XLA Modules:
  0.0 120.0 jit_solution(14274061245120965627)
XLA Ops:
  0.6 1.8 %norm.1.normed = bf16[128,768]{1,0:T(8,128)(2,1)} custom-call(bf16[128,768]{1,0:T(8,128)(2,1)} %bitcast.24, f32[768]{0:T(1024)} %gain.3), custom_call_target="tpu_custom_call" | custom-call | tf_op jit(solution)/shard_map/norm/pallas_call | solution.py:278
  2.5 2.5 %collective-permute-start.3 = (bf16[128,768]{1,0:T(8,128)(2,1)}, bf16[128,768]{1,0:T(8,128)(2,1)S(1)}, u32[]{:S(2)}, u32[]{:S(2)}) collective-permute-start(bf16[128,768]{1,0:T(8,128)(2,1)} %norm.1.normed), channel_id=1, source_target_pairs={{0,1},{1,0},{2,3},{3,2},{4,5},{5,4},{6,7},{7,6},{8,9},{9,8},{10,11... | collective-permute-start | bytes 589832 | tf_op jit(solution)/shard_map/ppermute | solution.py:22
  4.9 0.7 stack.27.pos
  5.6 2.1 %pack.1 = (bf16[12,1536]{1,0:T(8,128)(2,1)}, bf16[12,1536]{1,0:T(8,128)(2,1)}) custom-call(s32[6]{0:T(128)} %stack.27.pos, bf16[12,768]{1,0:T(8,128)(2,1)} %query.1, bf16[12,768]{1,0:T(8,128)(2,1)} %key.1, bf16[12,768]{1,0:T(8,128)(2,1)} %value.1, bf16[12,768]{1,0:T(8,128)(2,1)} %gate.1, bf16[12,768]{1,0:T(8,128)(2,1)} %out.1), custom_call_target="tpu_custom_call" | custom-call | tf_op jit(solution)/shard_map/pack/pallas_call | solution.py:267
  7.7 6.0 %collective-permute-start.1 = (bf16[12,1536]{1,0:T(8,128)(2,1)}, bf16[12,1536]{1,0:T(8,128)(2,1)S(1)}, u32[]{:S(2)}, u32[]{:S(2)}) collective-permute-start(bf16[12,1536]{1,0:T(8,128)(2,1)} %get-tuple-element.14.mine), channel_id=1, source_target_pairs={{0,32},{32,0},{1,33},{33,1},{2,34},{34,2},{3,35},{35,3},{4,36},{36... | collective-permute-start | bytes 110600 | tf_op jit(solution)/shard_map/ppermute | solution.py:18
  13.7 0.9 collective-permute-start.2
  14.5 0.4 collective-permute-start
  14.9 1.3 %collective-permute-done.1.above = bf16[12,1536]{1,0:T(8,128)(2,1)S(1)} collective-permute-done((bf16[12,1536]{1,0:T(8,128)(2,1)}, bf16[12,1536]{1,0:T(8,128)(2,1)S(1)}, u32[]{:S(2)}, u32[]{:S(2)}) %collective-permute-start.1) | collective-permute-done | bytes 36896 | tf_op jit(solution)/shard_map/ppermute | solution.py:18
  16.2 6.5 %collective-permute-done.2.across = bf16[12,1536]{1,0:T(8,128)(2,1)S(1)} collective-permute-done((bf16[12,1536]{1,0:T(8,128)(2,1)}, bf16[12,1536]{1,0:T(8,128)(2,1)S(1)}, u32[]{:S(2)}, u32[]{:S(2)}) %collective-permute-start.2) | collective-permute-done | bytes 36896 | tf_op jit(solution)/shard_map/ppermute | solution.py:276
  22.7 0.6 copy-done.15
  23.3 0.0 copy-done.16
  23.4 0.7 copy-done.12
  24.0 2.5 %assemble.1 = (bf16[16,48,1152]{2,1,0:T(8,128)(2,1)}, bf16[256,768]{1,0:T(8,128)(2,1)}) custom-call(s32[6]{0:T(128)} %stack.27.pos, bf16[12,1536]{1,0:T(8,128)(2,1)} %get-tuple-element.14.mine, bf16[12,1536]{1,0:T(8,128)(2,1)} %copy-done.16, bf16[12,1536]{1,0:T(8,128)(2,1)} %copy-done.14, bf16[12,1536]{1,0:T(8,128)(2,1)} %copy-done.15, ...), custom_call_target="tpu_custom_call" | custom-call | tf_op jit(solution)/shard_map/assemble/pallas_call | solution.py:287
  26.6 6.9 %all-to-all-start = ((bf16[16,48,1152]{2,1,0:T(8,128)(2,1)}), bf16[16,48,1152]{2,1,0:T(8,128)(2,1)S(1)}, u32[]{:S(2)}, u32[]{:S(2)}) async-start(bf16[16,48,1152]{2,1,0:T(8,128)(2,1)} %get-tuple-element.17), calls=%async_computation | async-start | bytes 3538944 | tf_op jit(solution)/shard_map/all_to_all | solution.py:299
  33.5 0.1 collective-permute-start.4
  33.6 2.1 %dynamic-slice_bitcast_fusion = (bf16[4,128,512]{2,1,0:T(8,128)(2,1)S(1)}, bf16[4,128,512]{2,1,0:T(8,128)(2,1)}) fusion(bf16[4,2,2,128,512]{4,3,2,1,0:T(8,128)(2,1)} %bitcast.26, s32[]{:T(128)S(6)} %select_n.18, s32[]{:T(128)S(6)} %select_n.22, s32[]{:T(128)S(6)} %select_n.20), kind=kLoop, calls=%fused_computation | loop fusion | bytes 2097164 | tf_op jit(solution)/shard_map/jit(dynamic_index_in_dim)/squeeze | solution.py:305
  35.7 2.3 %collective-permute-start.10 = (bf16[4,128,512]{2,1,0:T(8,128)(2,1)S(1)}, bf16[4,128,512]{2,1,0:T(8,128)(2,1)S(1)}, u32[]{:S(2)}, u32[]{:S(2)}) collective-permute-start(bf16[4,128,512]{2,1,0:T(8,128)(2,1)S(1)} %get-tuple-element.26), channel_id=1, source_target_pairs={{0,1},{1,0},{2,3},{3,2},{4,5},{5,4},{6,7},{7,6},{8,9},{9,8},{10,11... | collective-permute-start | bytes 1572872 | tf_op jit(solution)/shard_map/ppermute | solution.py:22
  38.0 0.0 collective-permute-start.7
  38.0 1.5 %collective-permute-start.5 = (bf16[256,768]{1,0:T(8,128)(2,1)S(1)}, bf16[256,768]{1,0:T(8,128)(2,1)S(1)}, u32[]{:S(2)}, u32[]{:S(2)}) collective-permute-start(bf16[256,768]{1,0:T(8,128)(2,1)S(1)} %copy-done.3), channel_id=1, source_target_pairs={{0,4},{4,0},{1,5},{5,1},{2,6},{6,2},{3,7},{7,3},{8,12},{12,8},{9,1... | collective-permute-start | bytes 1179656 | tf_op jit(solution)/shard_map/ppermute | solution.py:18
  39.5 14.2 %collective-permute-done.4.own_far = bf16[256,768]{1,0:T(8,128)(2,1)S(1)} collective-permute-done((bf16[256,768]{1,0:T(8,128)(2,1)S(1)}, bf16[256,768]{1,0:T(8,128)(2,1)S(1)}, u32[]{:S(2)}, u32[]{:S(2)}) %collective-permute-start.4) | collective-permute-done | bytes 393248 | tf_op jit(solution)/shard_map/ppermute | solution.py:22
  53.7 0.6 collective-permute-start.6
  54.3 7.3 %collective-permute-done.7.cot_own1 = bf16[128,768]{1,0:T(8,128)(2,1)S(1)} collective-permute-done((bf16[128,768]{1,0:T(8,128)(2,1)}, bf16[128,768]{1,0:T(8,128)(2,1)S(1)}, u32[]{:S(2)}, u32[]{:S(2)}) %collective-permute-start.7) | collective-permute-done | bytes 196640 | tf_op jit(solution)/shard_map/ppermute | solution.py:22
  61.5 1.9 %collective-permute-start.9 = (bf16[128,768]{1,0:T(8,128)(2,1)S(1)}, bf16[128,768]{1,0:T(8,128)(2,1)S(1)}, u32[]{:S(2)}, u32[]{:S(2)}) collective-permute-start(bf16[128,768]{1,0:T(8,128)(2,1)S(1)} %collective-permute-done.7.cot_own1), channel_id=1, source_target_pairs={{0,4},{4,0},{1,5},{5,1},{2,6},{6,2},{3,7},{7,3},{8,12},{12,8},{9,1... | collective-permute-start | bytes 589832 | tf_op jit(solution)/shard_map/ppermute | solution.py:18
  63.4 0.6 compare_convert_fusion
  64.0 0.5 collective-permute-done.9.cot_oth1
  64.5 0.2 copy-done.10
  64.7 0.5 copy-done.11
  65.2 0.1 copy-done.2
  65.3 0.6 copy-done.5
  66.0 0.6 copy-done
  66.5 12.6 %attention.1 = (f32[768,128]{1,0:T(8,128)}, f32[768,128]{1,0:T(8,128)}, bf16[2,768,128]{2,1,0:T(8,128)(2,1)}, bf16[2,768,128]{2,1,0:T(8,128)(2,1)}, bf16[2,768,1...) custom-call(s32[6]{0:T(128)} %stack.27.pos, bf16[256,768]{1,0:T(8,128)(2,1)} %get-tuple-element.16.own_near, ...), custom_call_target="tpu_custom_call" | custom-call | tf_op jit(solution)/shard_map/attention/pallas_call | solution.py:312
  79.1 6.8 %all-to-all-start.1 = ((bf16[16,4,2,16,256]{4,3,2,1,0:T(8,128)(2,1)}), bf16[16,4,2,16,256]{4,3,2,1,0:T(8,128)(2,1)S(1)}, u32[]{:S(2)}, u32[]{:S(2)}) async-start(bf16[16,4,2,16,256]{4,3,2,1,0:T(8,128)(2,1)} %get-tuple-element.25), calls=%async_computation.1 | async-start | bytes 2097152 | tf_op jit(solution)/shard_map/all_to_all | solution.py:359
  86.0 0.7 collective-permute-start.12
  86.7 0.1 collective-permute-start.11
  86.8 1.2 %collective-permute-done.12.oth = bf16[2,768,128]{2,1,0:T(8,128)(2,1)S(1)} collective-permute-done((bf16[2,768,128]{2,1,0:T(8,128)(2,1)S(1)}, bf16[2,768,128]{2,1,0:T(8,128)(2,1)S(1)}, u32[]{:S(2)}, u32[]{:S(2)}) %collective-permute-start.12) | collective-permute-done | bytes 393248 | tf_op jit(solution)/shard_map/ppermute | solution.py:18
  88.0 0.7 copy-done.8
  88.8 2.0 %sum_cores.1 = bf16[2,768,128]{2,1,0:T(8,128)(2,1)} custom-call(bf16[2,768,128]{2,1,0:T(8,128)(2,1)} %get-tuple-element.21.own, bf16[2,768,128]{2,1,0:T(8,128)(2,1)} %copy-done.8), custom_call_target="tpu_custom_call" | custom-call | tf_op jit(solution)/shard_map/sum_cores/pallas_call | solution.py:341
  90.8 10.5 %collective-permute-done.13.got = bf16[2,768,128]{2,1,0:T(8,128)(2,1)S(1)} collective-permute-done((bf16[2,768,128]{2,1,0:T(8,128)(2,1)}, bf16[2,768,128]{2,1,0:T(8,128)(2,1)S(1)}, u32[]{:S(2)}, u32[]{:S(2)}) %collective-permute-start.13) | collective-permute-done | bytes 393248 | tf_op jit(solution)/shard_map/ppermute | solution.py:22
  101.3 0.8 copy-done.7
  102.0 2.2 %sum_pair.1 = (f32[768,128]{1,0:T(8,128)}, bf16[768,128]{1,0:T(8,128)(2,1)}) custom-call(f32[768,128]{1,0:T(8,128)} %get-tuple-element.18.own_near, f32[768,128]{1,0:T(8,128)} %get-tuple-element.19.own_far, bf16[2,768,128]{2,1,0:T(8,128)(2,1)} %copy-done.6, bf16[2,768,128]{2,1,0:T(8,128)(2,1)} %copy-done.7), custom_call_target="tpu_custom_call" | custom-call | tf_op jit(solution)/shard_map/sum_pair/pallas_call | solution.py:349
  104.3 0.4 collective-permute-start.14
  104.6 1.0 copy-done.1
  105.6 2.0 %sum_plane.1 = bf16[2,2,2,4,8,128]{5,4,3,2,1,0:T(8,128)(2,1)} custom-call(s32[6]{0:T(128)} %stack.27.pos, bf16[16,4,2,16,256]{4,3,2,1,0:T(8,128)(2,1)} %copy-done.1, bf16[768,128]{1,0:T(8,128)(2,1)} %get-tuple-element.24.after), custom_call_target="tpu_custom_call" | custom-call | tf_op jit(solution)/shard_map/sum_plane/pallas_call | solution.py:360
  107.6 4.4 %all-to-all-start.2 = ((bf16[8,4,8,128]{3,2,1,0:T(8,128)(2,1)}), bf16[8,4,8,128]{3,2,1,0:T(8,128)(2,1)S(1)}, u32[]{:S(2)}, u32[]{:S(2)}) async-start(bf16[8,4,8,128]{3,2,1,0:T(8,128)(2,1)} %bitcast.27), calls=%async_computation.2 | async-start | bytes 131072 | tf_op jit(solution)/shard_map/all_to_all | solution.py:369
  112.0 4.3 %collective-permute-done.14.back = bf16[768,128]{1,0:T(8,128)(2,1)S(1)} collective-permute-done((bf16[768,128]{1,0:T(8,128)(2,1)}, bf16[768,128]{1,0:T(8,128)(2,1)S(1)}, u32[]{:S(2)}, u32[]{:S(2)}) %collective-permute-start.14) | collective-permute-done | bytes 196640 | tf_op jit(solution)/shard_map/ppermute | solution.py:22
  116.4 0.7 copy-done.13
  117.0 2.3 %norm_back.1 = bf16[128,768]{1,0:T(8,128)(2,1)} custom-call(bf16[128,768]{1,0:T(8,128)(2,1)} %bitcast.25, f32[768]{0:T(1024)} %gain.3, f32[768,128]{1,0:T(8,128)} %get-tuple-element.23.near, bf16[768,128]{1,0:T(8,128)(2,1)} %copy-done.13), custom_call_target="tpu_custom_call" | custom-call | tf_op jit(solution)/shard_map/norm_back/pallas_call | solution.py:373
  119.3 0.6 copy.18
  (41 shorter events, 0.1 us)
Async XLA Ops:
  2.5 20.3 %collective-permute-start.3 = (bf16[128,768]{1,0:T(8,128)(2,1)}, bf16[128,768]{1,0:T(8,128)(2,1)S(1)}, u32[]{:S(2)}, u32[]{:S(2)}) collective-permute-start(bf16[128,768]{1,0:T(8,128)(2,1)} %norm.1.normed), channel_id=1, source_target_pairs={{0,1},{1,0},{2,3},{3,2},{4,5},{5,4},{6,7},{7,6},{8,9},{9,8},{10,11... | collective-permute-start | bytes 589832 | tf_op jit(solution)/shard_map/ppermute | solution.py:22
  7.7 8.6 %collective-permute-start.1 = (bf16[12,1536]{1,0:T(8,128)(2,1)}, bf16[12,1536]{1,0:T(8,128)(2,1)S(1)}, u32[]{:S(2)}, u32[]{:S(2)}) collective-permute-start(bf16[12,1536]{1,0:T(8,128)(2,1)} %get-tuple-element.14.mine), channel_id=1, source_target_pairs={{0,32},{32,0},{1,33},{33,1},{2,34},{34,2},{3,35},{35,3},{4,36},{36... | collective-permute-start | bytes 110600 | tf_op jit(solution)/shard_map/ppermute | solution.py:18
  13.7 9.0 %collective-permute-start.2 = (bf16[12,1536]{1,0:T(8,128)(2,1)}, bf16[12,1536]{1,0:T(8,128)(2,1)S(1)}, u32[]{:S(2)}, u32[]{:S(2)}) collective-permute-start(bf16[12,1536]{1,0:T(8,128)(2,1)} %get-tuple-element.15), channel_id=1, source_target_pairs={{0,36},{36,0},{4,32},{32,4},{1,37},{37,1},{5,33},{33,5},{2,38},{38... | collective-permute-start | bytes 110600 | tf_op jit(solution)/shard_map/ppermute | solution.py:276
  14.5 8.2 %collective-permute-start = (bf16[12,1536]{1,0:T(8,128)(2,1)}, bf16[12,1536]{1,0:T(8,128)(2,1)S(1)}, u32[]{:S(2)}, u32[]{:S(2)}) collective-permute-start(bf16[12,1536]{1,0:T(8,128)(2,1)} %get-tuple-element.15), channel_id=1, source_target_pairs={{0,4},{4,0},{1,5},{5,1},{2,6},{6,2},{3,7},{7,3},{8,12},{12,8},{9,1... | collective-permute-start | bytes 110600 | tf_op jit(solution)/shard_map/ppermute | solution.py:18
  16.2 6.5 %copy-start.14 = (bf16[12,1536]{1,0:T(8,128)(2,1)}, bf16[12,1536]{1,0:T(8,128)(2,1)S(1)}, u32[]{:S(2)}) copy-start(bf16[12,1536]{1,0:T(8,128)(2,1)S(1)} %collective-permute-done.1.above) | copy-start | bytes 110596
  22.7 0.6 copy-start.15
  22.7 0.6 copy-start.16
  23.4 0.7 copy-start.12
  26.6 6.9 %copy-start.3 = (bf16[256,768]{1,0:T(8,128)(2,1)S(1)}, bf16[256,768]{1,0:T(8,128)(2,1)}, u32[]{:S(2)}) copy-start(bf16[256,768]{1,0:T(8,128)(2,1)} %get-tuple-element.16.own_near) | copy-start | bytes 1179652
  26.6 36.9 %copy-start.17 = (s32[512]{0:T(512)S(1)}, s32[512]{0:T(512)}, u32[]{:S(2)}) copy-start(s32[512]{0:T(512)} %param.19) | copy-start | bytes 6148
  26.6 38.6 %all-to-all-start = ((bf16[16,48,1152]{2,1,0:T(8,128)(2,1)}), bf16[16,48,1152]{2,1,0:T(8,128)(2,1)S(1)}, u32[]{:S(2)}, u32[]{:S(2)}) async-start(bf16[16,48,1152]{2,1,0:T(8,128)(2,1)} %get-tuple-element.17), calls=%async_computation | async-start | bytes 3538944 | tf_op jit(solution)/shard_map/all_to_all | solution.py:299
  33.5 20.2 %collective-permute-start.4 = (bf16[256,768]{1,0:T(8,128)(2,1)S(1)}, bf16[256,768]{1,0:T(8,128)(2,1)S(1)}, u32[]{:S(2)}, u32[]{:S(2)}) collective-permute-start(bf16[256,768]{1,0:T(8,128)(2,1)S(1)} %copy-done.3), channel_id=1, source_target_pairs={{0,2},{1,3},{2,0},{3,1},{4,6},{5,7},{6,4},{7,5},{8,10},{9,11},{10,... | collective-permute-start | bytes 1179656 | tf_op jit(solution)/shard_map/ppermute | solution.py:22
  35.7 28.8 %collective-permute-start.10 = (bf16[4,128,512]{2,1,0:T(8,128)(2,1)S(1)}, bf16[4,128,512]{2,1,0:T(8,128)(2,1)S(1)}, u32[]{:S(2)}, u32[]{:S(2)}) collective-permute-start(bf16[4,128,512]{2,1,0:T(8,128)(2,1)S(1)} %get-tuple-element.26), channel_id=1, source_target_pairs={{0,1},{1,0},{2,3},{3,2},{4,5},{5,4},{6,7},{7,6},{8,9},{9,8},{10,11... | collective-permute-start | bytes 1572872 | tf_op jit(solution)/shard_map/ppermute | solution.py:22
  38.0 23.5 %collective-permute-start.7 = (bf16[128,768]{1,0:T(8,128)(2,1)}, bf16[128,768]{1,0:T(8,128)(2,1)S(1)}, u32[]{:S(2)}, u32[]{:S(2)}) collective-permute-start(bf16[128,768]{1,0:T(8,128)(2,1)} %bitcast.7.cot_own0), channel_id=1, source_target_pairs={{0,1},{1,0},{2,3},{3,2},{4,5},{5,4},{6,7},{7,6},{8,9},{9,8},{10,11... | collective-permute-start | bytes 589832 | tf_op jit(solution)/shard_map/ppermute | solution.py:22
  38.0 26.5 %collective-permute-start.5 = (bf16[256,768]{1,0:T(8,128)(2,1)S(1)}, bf16[256,768]{1,0:T(8,128)(2,1)S(1)}, u32[]{:S(2)}, u32[]{:S(2)}) collective-permute-start(bf16[256,768]{1,0:T(8,128)(2,1)S(1)} %copy-done.3), channel_id=1, source_target_pairs={{0,4},{4,0},{1,5},{5,1},{2,6},{6,2},{3,7},{7,3},{8,12},{12,8},{9,1... | collective-permute-start | bytes 1179656 | tf_op jit(solution)/shard_map/ppermute | solution.py:18
  53.7 11.5 %copy-start.4 = (bf16[256,768]{1,0:T(8,128)(2,1)}, bf16[256,768]{1,0:T(8,128)(2,1)S(1)}, u32[]{:S(2)}) copy-start(bf16[256,768]{1,0:T(8,128)(2,1)S(1)} %collective-permute-done.4.own_far) | copy-start | bytes 1179652
  53.7 11.5 %collective-permute-start.6 = (bf16[256,768]{1,0:T(8,128)(2,1)S(1)}, bf16[256,768]{1,0:T(8,128)(2,1)}, u32[]{:S(2)}, u32[]{:S(2)}) collective-permute-start(bf16[256,768]{1,0:T(8,128)(2,1)S(1)} %collective-permute-done.4.own_far), channel_id=1, source_target_pairs={{0,4},{4,0},{1,5},{5,1},{2,6},{6,2},{3,7},{7,3},{8,12},{12,8},{9,1... | collective-permute-start | bytes 1179656 | tf_op jit(solution)/shard_map/ppermute | solution.py:18
  54.2 9.8 %collective-permute-start.8 = (bf16[128,768]{1,0:T(8,128)(2,1)}, bf16[128,768]{1,0:T(8,128)(2,1)S(1)}, u32[]{:S(2)}, u32[]{:S(2)}) collective-permute-start(bf16[128,768]{1,0:T(8,128)(2,1)} %bitcast.7.cot_own0), channel_id=1, source_target_pairs={{0,4},{4,0},{1,5},{5,1},{2,6},{6,2},{3,7},{7,3},{8,12},{12,8},{9,1... | collective-permute-start | bytes 589832 | tf_op jit(solution)/shard_map/ppermute | solution.py:18
  61.5 3.0 %copy-start.9 = (bf16[128,768]{1,0:T(8,128)(2,1)}, bf16[128,768]{1,0:T(8,128)(2,1)S(1)}, u32[]{:S(2)}) copy-start(bf16[128,768]{1,0:T(8,128)(2,1)S(1)} %collective-permute-done.7.cot_own1) | copy-start | bytes 589828
  61.5 2.9 %collective-permute-start.9 = (bf16[128,768]{1,0:T(8,128)(2,1)S(1)}, bf16[128,768]{1,0:T(8,128)(2,1)S(1)}, u32[]{:S(2)}, u32[]{:S(2)}) collective-permute-start(bf16[128,768]{1,0:T(8,128)(2,1)S(1)} %collective-permute-done.7.cot_own1), channel_id=1, source_target_pairs={{0,4},{4,0},{1,5},{5,1},{2,6},{6,2},{3,7},{7,3},{8,12},{12,8},{9,1... | collective-permute-start | bytes 589832 | tf_op jit(solution)/shard_map/ppermute | solution.py:18
  64.0 0.7 copy-start.10
  64.5 0.7 copy-start.11
  64.5 0.8 copy-start.2
  65.2 0.8 copy-start.5
  65.2 1.3 %copy-start = (bf16[16,48,1152]{2,1,0:T(8,128)(2,1)}, bf16[16,48,1152]{2,1,0:T(8,128)(2,1)S(1)}, u32[]{:S(2)}) copy-start(bf16[16,48,1152]{2,1,0:T(8,128)(2,1)S(1)} %all-to-all-done.weights) | copy-start | bytes 5308420
  79.1 6.8 %copy-start.19 = (bf16[2,768,128]{2,1,0:T(8,128)(2,1)S(1)}, bf16[2,768,128]{2,1,0:T(8,128)(2,1)}, u32[]{:S(2)}) copy-start(bf16[2,768,128]{2,1,0:T(8,128)(2,1)} %get-tuple-element.22) | copy-start | bytes 1179652
  79.1 7.6 %copy-start.18 = (bf16[2,768,128]{2,1,0:T(8,128)(2,1)S(1)}, bf16[2,768,128]{2,1,0:T(8,128)(2,1)}, u32[]{:S(2)}) copy-start(bf16[2,768,128]{2,1,0:T(8,128)(2,1)} %get-tuple-element.20) | copy-start | bytes 1179652
  79.1 25.5 %all-to-all-start.1 = ((bf16[16,4,2,16,256]{4,3,2,1,0:T(8,128)(2,1)}), bf16[16,4,2,16,256]{4,3,2,1,0:T(8,128)(2,1)S(1)}, u32[]{:S(2)}, u32[]{:S(2)}) async-start(bf16[16,4,2,16,256]{4,3,2,1,0:T(8,128)(2,1)} %get-tuple-element.25), calls=%async_computation.1 | async-start | bytes 2097152 | tf_op jit(solution)/shard_map/all_to_all | solution.py:359
  86.0 2.1 %collective-permute-start.12 = (bf16[2,768,128]{2,1,0:T(8,128)(2,1)S(1)}, bf16[2,768,128]{2,1,0:T(8,128)(2,1)S(1)}, u32[]{:S(2)}, u32[]{:S(2)}) collective-permute-start(bf16[2,768,128]{2,1,0:T(8,128)(2,1)S(1)} %copy-done.19), channel_id=1, source_target_pairs={{0,4},{4,0},{1,5},{5,1},{2,6},{6,2},{3,7},{7,3},{8,12},{12,8},{9,1... | collective-permute-start | bytes 1179656 | tf_op jit(solution)/shard_map/ppermute | solution.py:18
  86.7 4.1 %collective-permute-start.11 = (bf16[2,768,128]{2,1,0:T(8,128)(2,1)S(1)}, bf16[2,768,128]{2,1,0:T(8,128)(2,1)S(1)}, u32[]{:S(2)}, u32[]{:S(2)}) collective-permute-start(bf16[2,768,128]{2,1,0:T(8,128)(2,1)S(1)} %copy-done.18), channel_id=1, source_target_pairs={{0,4},{4,0},{1,5},{5,1},{2,6},{6,2},{3,7},{7,3},{8,12},{12,8},{9,1... | collective-permute-start | bytes 1179656 | tf_op jit(solution)/shard_map/ppermute | solution.py:18
  88.0 0.7 copy-start.8
  90.7 10.5 %collective-permute-start.13 = (bf16[2,768,128]{2,1,0:T(8,128)(2,1)}, bf16[2,768,128]{2,1,0:T(8,128)(2,1)S(1)}, u32[]{:S(2)}, u32[]{:S(2)}) collective-permute-start(bf16[2,768,128]{2,1,0:T(8,128)(2,1)} %sum_cores.1), channel_id=1, source_target_pairs={{0,1},{1,0},{2,3},{3,2},{4,5},{5,4},{6,7},{7,6},{8,9},{9,8},{10,11... | collective-permute-start | bytes 1179656 | tf_op jit(solution)/shard_map/ppermute | solution.py:22
  90.8 10.5 %copy-start.6 = (bf16[2,768,128]{2,1,0:T(8,128)(2,1)}, bf16[2,768,128]{2,1,0:T(8,128)(2,1)S(1)}, u32[]{:S(2)}) copy-start(bf16[2,768,128]{2,1,0:T(8,128)(2,1)S(1)} %collective-permute-done.11.oth) | copy-start | bytes 1179652
  101.3 0.8 copy-start.7
  104.3 12.1 %collective-permute-start.14 = (bf16[768,128]{1,0:T(8,128)(2,1)}, bf16[768,128]{1,0:T(8,128)(2,1)S(1)}, u32[]{:S(2)}, u32[]{:S(2)}) collective-permute-start(bf16[768,128]{1,0:T(8,128)(2,1)} %get-tuple-element.24.after), channel_id=1, source_target_pairs={{0,2},{1,3},{2,0},{3,1},{4,6},{5,7},{6,4},{7,5},{8,10},{9,11},{10,... | collective-permute-start | bytes 589832 | tf_op jit(solution)/shard_map/ppermute | solution.py:22
  104.6 1.0 copy-start.1
  107.6 11.7 %all-to-all-start.2 = ((bf16[8,4,8,128]{3,2,1,0:T(8,128)(2,1)}), bf16[8,4,8,128]{3,2,1,0:T(8,128)(2,1)S(1)}, u32[]{:S(2)}, u32[]{:S(2)}) async-start(bf16[8,4,8,128]{3,2,1,0:T(8,128)(2,1)} %bitcast.27), calls=%async_computation.2 | async-start | bytes 131072 | tf_op jit(solution)/shard_map/all_to_all | solution.py:369
  116.4 0.7 copy-start.13

commit v4 on v3

--- a/solution.py
+++ b/solution.py
@@ -176,7 +176,7 @@
     normed[...] = (centered * inv * gain[...][None, :]).astype(BF)
 
 
-def assemble_kernel(pos, mine, beside, above, across, normed, beyond, part, near):
+def assemble_kernel(pos, mine, beside, above, across, normed, beyond, after, ready, part, near):
     rows = normed.shape[0]
     near[:rows, :] = normed[...]
     near[rows:, :] = beyond[...]
@@ -263,6 +263,11 @@
     gain = layer_norm_scale
     room = pltpu.CompilerParams(vmem_limit_bytes=58 * 1024 * 1024)
 
+    groups = pair_bias.reshape((heads, NC, 2) + pair_bias.shape[1:])
+    groups = lax.dynamic_index_in_dim(groups, core, 1, False)
+    theirs = lax.dynamic_index_in_dim(groups, 1 - tl, 1, False)
+    bias_mine = lax.dynamic_index_in_dim(groups, tl, 1, False)
+
     packed = jax.ShapeDtypeStruct((query_weight.shape[0], 2 * width), BF)
     mine, send = pl.pallas_call(
         pack_kernel,
@@ -283,6 +288,7 @@
         name="norm",
     )(inputs, gain)
     beyond = swap(normed, 1)
+    cot_pair = swap(cotangent, 1)
 
     pieces, own_near = pl.pallas_call(
         assemble_kernel,
@@ -290,20 +296,15 @@
             jax.ShapeDtypeStruct((NX * NY, NC * NZ * mine.shape[0], width + width // 2), BF),
             jax.ShapeDtypeStruct((2 * rows, width), BF),
         ),
-        in_specs=[smem] + [vmem] * 6,
+        in_specs=[smem] + [vmem] * 6 + [anywhere] * 2,
         out_specs=(vmem, vmem),
         compiler_params=room,
         name="assemble",
-    )(pos, mine, beside, above, across, normed, beyond)
+    )(pos, mine, beside, above, across, normed, beyond, cot_pair, theirs)
     own_far = swap(own_near, 2)
     weights = lax.all_to_all(pieces, ("x", "y"), 0, 0, tiled=True)
     oth_near, oth_far = shift(own_near, "core", NC, 1), shift(own_far, "core", NC, 1)
-    cot_pair = swap(cotangent, 1)
     cots = [cotangent, cot_pair, shift(cotangent, "core", NC, 1), shift(cot_pair, "core", NC, 1)]
-    groups = pair_bias.reshape((heads, NC, 2) + pair_bias.shape[1:])
-    groups = lax.dynamic_index_in_dim(groups, core, 1, False)
-    theirs = lax.dynamic_index_in_dim(groups, 1 - tl, 1, False)
-    bias_mine = lax.dynamic_index_in_dim(groups, tl, 1, False)
     bias_pair = swap(theirs, 1)
 
     valid = (atom_count > 0).astype(F32)

time: 121 us -> 115 us (0.950)
  waiting for transfers between devices: 45.9 us -> 36.2 us
  starting transfers between devices: 35.4 us -> 38.7 us
    ppermute x6, waiting for transfers between devices: 36.3 us -> 27.4 us  [swap(): return lax.ppermute(value, ('th', 'tl'), [(i, i ^ by) for i in range(NT)])]
    ppermute x1, starting transfers between devices: 0.87 us -> 7.82 us  [on_device(): lax.ppermute(send, ('zh', 'core'), [(0, 3), (3, 0), (1, 2), (2, 1)])]
    ppermute x1, waiting for transfers between devices: 6.49 us -> 0.01 us  [on_device(): lax.ppermute(send, ('zh', 'core'), [(0, 3), (3, 0), (1, 2), (2, 1)])]
    ppermute x8, starting transfers between devices: 11.1 us -> 4.67 us  [shift(): lax.ppermute(value, axis, [(i, (i + by) % count) for i in range(count)])]
    ppermute x8, waiting for transfers between devices: 3.05 us -> 7.19 us  [shift(): lax.ppermute(value, axis, [(i, (i + by) % count) for i in range(count)])]
    ppermute x6, starting transfers between devices: 5.28 us -> 7.51 us  [swap(): return lax.ppermute(value, ('th', 'tl'), [(i, i ^ by) for i in range(NT)])]
    all_to_all x1, waiting for transfers between devices: 0.01 us -> 1.56 us  [on_device(): lax.all_to_all(planes.reshape((-1,) + shape[3:]), ('zh', 'core', 'tl'), 0...]
    unnamed x40 -> x44, local copies, waits for them, and re-layouts: 6.48 us -> 6.68 us
  transfers between devices with their start and end apart: 18 -> 18, of which waited for: 8 -> 7; matrix products, arithmetic and copies ran while one was open for 3% -> 3% of each run, Pallas kernels for 9% -> 9%
where the time goes in v4:
time: 115 us; the launch traced here: 114 us
  starting transfers between devices  38.7 us (34%)
  waiting for transfers between devices  36.2 us (31%)
  Pallas kernels  27.5 us (24%)
  local copies, waits for them, and re-layouts  10.2 us (9%)
    ppermute x6, waiting for transfers between devices, swap(): return lax.ppermute(value, ('th', 'tl'), [(i, i ^ by) for i in range(NT)])  27.4 us
    pallas_call x1, Pallas kernels, on_device(): pl.pallas_call(attention_kernel, out_shape=(jax.ShapeDtypeStruct((width,...  12.6 us
    ppermute x1, starting transfers between devices, on_device(): lax.ppermute(send, ('zh', 'core'), [(0, 3), (3, 0), (1, 2), (2, 1)])  7.82 us
    ppermute x6, starting transfers between devices, swap(): return lax.ppermute(value, ('th', 'tl'), [(i, i ^ by) for i in range(NT)])  7.51 us
    ppermute x8, waiting for transfers between devices, shift(): lax.ppermute(value, axis, [(i, (i + by) % count) for i in range(count)])  7.19 us
    all_to_all x1, starting transfers between devices, on_device(): weights = lax.all_to_all(pieces, ('x', 'y'), 0, 0, tiled=True)  6.9 us
    all_to_all x1, starting transfers between devices, on_device(): parts = lax.all_to_all(out_bias, ('x', 'y'), 0, 0, tiled=True)  6.8 us
    unnamed x44, local copies, waits for them, and re-layouts  6.68 us
  transfers between devices with their start and end apart: 18, of which 7 were waited for; matrix products, arithmetic and copies ran while one was open for 3% of the time, Pallas kernels for 9%

profile of v4, /device:TPU:1, one launch (start us, length us, event | category | flops | bytes accessed | tf_op | source)
XLA Modules:
  0.0 114.1 jit_solution(8017993868098606532)
XLA Ops:
  0.6 1.8 %norm.1.normed = bf16[128,768]{1,0:T(8,128)(2,1)} custom-call(bf16[128,768]{1,0:T(8,128)(2,1)} %bitcast.24, f32[768]{0:T(1024)} %gain.3), custom_call_target="tpu_custom_call" | custom-call | tf_op jit(solution)/shard_map/norm/pallas_call | solution.py:283
  2.5 2.5 %collective-permute-start.3 = (bf16[128,768]{1,0:T(8,128)(2,1)}, bf16[128,768]{1,0:T(8,128)(2,1)S(1)}, u32[]{:S(2)}, u32[]{:S(2)}) collective-permute-start(bf16[128,768]{1,0:T(8,128)(2,1)} %norm.1.normed), channel_id=1, source_target_pairs={{0,1},{1,0},{2,3},{3,2},{4,5},{5,4},{6,7},{7,6},{8,9},{9,8},{10,11... | collective-permute-start | bytes 589832 | tf_op jit(solution)/shard_map/ppermute | solution.py:22
  4.9 0.0 collective-permute-start.4
  5.0 0.7 stack.27.pos
  5.6 2.1 %pack.1 = (bf16[12,1536]{1,0:T(8,128)(2,1)}, bf16[12,1536]{1,0:T(8,128)(2,1)}) custom-call(s32[6]{0:T(128)} %stack.27.pos, bf16[12,768]{1,0:T(8,128)(2,1)} %query.1, bf16[12,768]{1,0:T(8,128)(2,1)} %key.1, bf16[12,768]{1,0:T(8,128)(2,1)} %value.1, bf16[12,768]{1,0:T(8,128)(2,1)} %gate.1, bf16[12,768]{1,0:T(8,128)(2,1)} %out.1), custom_call_target="tpu_custom_call" | custom-call | tf_op jit(solution)/shard_map/pack/pallas_call | solution.py:272
  7.7 7.8 %collective-permute-start.2 = (bf16[12,1536]{1,0:T(8,128)(2,1)}, bf16[12,1536]{1,0:T(8,128)(2,1)S(1)}, u32[]{:S(2)}, u32[]{:S(2)}) collective-permute-start(bf16[12,1536]{1,0:T(8,128)(2,1)} %get-tuple-element.15), channel_id=1, source_target_pairs={{0,36},{36,0},{4,32},{32,4},{1,37},{37,1},{5,33},{33,5},{2,38},{38... | collective-permute-start | bytes 110600 | tf_op jit(solution)/shard_map/ppermute | solution.py:281
  15.5 0.2 collective-permute-start.1
  15.7 2.2 %dynamic-slice_bitcast_fusion = (bf16[4,128,512]{2,1,0:T(8,128)(2,1)}, bf16[4,128,512]{2,1,0:T(8,128)(2,1)}) fusion(bf16[4,2,2,128,512]{4,3,2,1,0:T(8,128)(2,1)} %bitcast.26, s32[]{:T(128)S(6)} %select_n.18, s32[]{:T(128)S(6)} %select_n.22, s32[]{:T(128)S(6)} %select_n.20), kind=kLoop, calls=%fused_computation | loop fusion | bytes 2097164 | tf_op jit(solution)/shard_map/jit(dynamic_index_in_dim)/squeeze | solution.py:269
  18.0 5.0 %collective-permute-done.1.above = bf16[12,1536]{1,0:T(8,128)(2,1)S(1)} collective-permute-done((bf16[12,1536]{1,0:T(8,128)(2,1)}, bf16[12,1536]{1,0:T(8,128)(2,1)S(1)}, u32[]{:S(2)}, u32[]{:S(2)}) %collective-permute-start.1) | collective-permute-done | bytes 36896 | tf_op jit(solution)/shard_map/ppermute | solution.py:18
  23.1 0.5 copy-done.18
  23.6 0.0 copy-done.16
  23.6 0.0 copy-done.17
  23.6 0.1 copy-done.14
  23.7 0.1 copy-done.3
  23.8 2.5 %assemble.1 = (bf16[16,48,1152]{2,1,0:T(8,128)(2,1)}, bf16[256,768]{1,0:T(8,128)(2,1)}) custom-call(s32[6]{0:T(128)} %stack.27.pos, bf16[12,1536]{1,0:T(8,128)(2,1)} %get-tuple-element.14.mine, bf16[12,1536]{1,0:T(8,128)(2,1)} %copy-done.17, bf16[12,1536]{1,0:T(8,128)(2,1)} %copy-done.18, bf16[12,1536]{1,0:T(8,128)(2,1)} %copy-done.16, ...), custom_call_target="tpu_custom_call" | custom-call | tf_op jit(solution)/shard_map/assemble/pallas_call | solution.py:293
  26.4 0.0 copy-start.19
  26.4 6.9 %all-to-all-start = ((bf16[16,48,1152]{2,1,0:T(8,128)(2,1)}), bf16[16,48,1152]{2,1,0:T(8,128)(2,1)S(1)}, u32[]{:S(2)}, u32[]{:S(2)}) async-start(bf16[16,48,1152]{2,1,0:T(8,128)(2,1)} %get-tuple-element.17), calls=%async_computation | async-start | bytes 3538944 | tf_op jit(solution)/shard_map/all_to_all | solution.py:305
  33.3 0.9 collective-permute-start.5
  34.2 2.7 %collective-permute-start.10 = (bf16[4,128,512]{2,1,0:T(8,128)(2,1)S(1)}, bf16[4,128,512]{2,1,0:T(8,128)(2,1)S(1)}, u32[]{:S(2)}, u32[]{:S(2)}) collective-permute-start(bf16[4,128,512]{2,1,0:T(8,128)(2,1)S(1)} %copy-done.2), channel_id=1, source_target_pairs={{0,1},{1,0},{2,3},{3,2},{4,5},{5,4},{6,7},{7,6},{8,9},{9,8},{10,11... | collective-permute-start | bytes 1572872 | tf_op jit(solution)/shard_map/ppermute | solution.py:22
  36.9 1.7 %collective-permute-start.6 = (bf16[256,768]{1,0:T(8,128)(2,1)S(1)}, bf16[256,768]{1,0:T(8,128)(2,1)S(1)}, u32[]{:S(2)}, u32[]{:S(2)}) collective-permute-start(bf16[256,768]{1,0:T(8,128)(2,1)S(1)} %copy-done.6), channel_id=1, source_target_pairs={{0,4},{4,0},{1,5},{5,1},{2,6},{6,2},{3,7},{7,3},{8,12},{12,8},{9,1... | collective-permute-start | bytes 1179656 | tf_op jit(solution)/shard_map/ppermute | solution.py:18
  38.6 14.3 %collective-permute-done.5.own_far = bf16[256,768]{1,0:T(8,128)(2,1)S(1)} collective-permute-done((bf16[256,768]{1,0:T(8,128)(2,1)S(1)}, bf16[256,768]{1,0:T(8,128)(2,1)S(1)}, u32[]{:S(2)}, u32[]{:S(2)}) %collective-permute-start.5) | collective-permute-done | bytes 393248 | tf_op jit(solution)/shard_map/ppermute | solution.py:22
  52.9 1.5 %collective-permute-start.7 = (bf16[256,768]{1,0:T(8,128)(2,1)S(1)}, bf16[256,768]{1,0:T(8,128)(2,1)}, u32[]{:S(2)}, u32[]{:S(2)}) collective-permute-start(bf16[256,768]{1,0:T(8,128)(2,1)S(1)} %collective-permute-done.5.own_far), channel_id=1, source_target_pairs={{0,4},{4,0},{1,5},{5,1},{2,6},{6,2},{3,7},{7,3},{8,12},{12,8},{9,1... | collective-permute-start | bytes 1179656 | tf_op jit(solution)/shard_map/ppermute | solution.py:18
  54.4 0.5 collective-permute-start.9
  54.9 0.6 compare_convert_fusion
  55.4 0.9 collective-permute-done.8.cot_oth0
  56.4 0.6 copy-done.12
  57.0 0.1 copy-done.13
  57.1 0.8 copy-done.8
  57.9 1.2 %copy-done = bf16[16,48,1152]{2,1,0:T(8,128)(2,1)} copy-done((bf16[16,48,1152]{2,1,0:T(8,128)(2,1)}, bf16[16,48,1152]{2,1,0:T(8,128)(2,1)S(1)}, u32[]{:S(2)}) %copy-start) | copy-done | bytes 1769496
  59.1 12.6 %attention.1 = (f32[768,128]{1,0:T(8,128)}, f32[768,128]{1,0:T(8,128)}, bf16[2,768,128]{2,1,0:T(8,128)(2,1)}, bf16[2,768,128]{2,1,0:T(8,128)(2,1)}, bf16[2,768,1...) custom-call(s32[6]{0:T(128)} %stack.27.pos, bf16[256,768]{1,0:T(8,128)(2,1)} %get-tuple-element.16.own_near, ...), custom_call_target="tpu_custom_call" | custom-call | tf_op jit(solution)/shard_map/attention/pallas_call | solution.py:313
  71.7 6.8 %all-to-all-start.1 = ((bf16[16,4,2,16,256]{4,3,2,1,0:T(8,128)(2,1)}), bf16[16,4,2,16,256]{4,3,2,1,0:T(8,128)(2,1)S(1)}, u32[]{:S(2)}, u32[]{:S(2)}) async-start(bf16[16,4,2,16,256]{4,3,2,1,0:T(8,128)(2,1)} %get-tuple-element.25), calls=%async_computation.1 | async-start | bytes 2097152 | tf_op jit(solution)/shard_map/all_to_all | solution.py:360
  78.5 0.7 collective-permute-start.12
  79.2 0.1 collective-permute-start.11
  79.3 1.2 %collective-permute-done.12.oth = bf16[2,768,128]{2,1,0:T(8,128)(2,1)S(1)} collective-permute-done((bf16[2,768,128]{2,1,0:T(8,128)(2,1)S(1)}, bf16[2,768,128]{2,1,0:T(8,128)(2,1)S(1)}, u32[]{:S(2)}, u32[]{:S(2)}) %collective-permute-start.12) | collective-permute-done | bytes 393248 | tf_op jit(solution)/shard_map/ppermute | solution.py:18
  80.6 0.7 copy-done.11
  81.3 2.0 %sum_cores.1 = bf16[2,768,128]{2,1,0:T(8,128)(2,1)} custom-call(bf16[2,768,128]{2,1,0:T(8,128)(2,1)} %get-tuple-element.21.own, bf16[2,768,128]{2,1,0:T(8,128)(2,1)} %copy-done.11), custom_call_target="tpu_custom_call" | custom-call | tf_op jit(solution)/shard_map/sum_cores/pallas_call | solution.py:342
  83.3 10.5 %collective-permute-done.13.got = bf16[2,768,128]{2,1,0:T(8,128)(2,1)S(1)} collective-permute-done((bf16[2,768,128]{2,1,0:T(8,128)(2,1)}, bf16[2,768,128]{2,1,0:T(8,128)(2,1)S(1)}, u32[]{:S(2)}, u32[]{:S(2)}) %collective-permute-start.13) | collective-permute-done | bytes 393248 | tf_op jit(solution)/shard_map/ppermute | solution.py:22
  93.8 0.8 copy-done.10
  94.6 2.2 %sum_pair.1 = (f32[768,128]{1,0:T(8,128)}, bf16[768,128]{1,0:T(8,128)(2,1)}) custom-call(f32[768,128]{1,0:T(8,128)} %get-tuple-element.18.own_near, f32[768,128]{1,0:T(8,128)} %get-tuple-element.19.own_far, bf16[2,768,128]{2,1,0:T(8,128)(2,1)} %copy-done.9, bf16[2,768,128]{2,1,0:T(8,128)(2,1)} %copy-done.10), custom_call_target="tpu_custom_call" | custom-call | tf_op jit(solution)/shard_map/sum_pair/pallas_call | solution.py:350
  96.8 1.4 %collective-permute-start.14 = (bf16[768,128]{1,0:T(8,128)(2,1)}, bf16[768,128]{1,0:T(8,128)(2,1)S(1)}, u32[]{:S(2)}, u32[]{:S(2)}) collective-permute-start(bf16[768,128]{1,0:T(8,128)(2,1)} %get-tuple-element.24.after), channel_id=1, source_target_pairs={{0,2},{1,3},{2,0},{3,1},{4,6},{5,7},{6,4},{7,5},{8,10},{9,11},{10,... | collective-permute-start | bytes 589832 | tf_op jit(solution)/shard_map/ppermute | solution.py:22
  98.2 1.0 copy-done.1
  99.2 2.0 %sum_plane.1 = bf16[2,2,2,4,8,128]{5,4,3,2,1,0:T(8,128)(2,1)} custom-call(s32[6]{0:T(128)} %stack.27.pos, bf16[16,4,2,16,256]{4,3,2,1,0:T(8,128)(2,1)} %copy-done.1, bf16[768,128]{1,0:T(8,128)(2,1)} %get-tuple-element.24.after), custom_call_target="tpu_custom_call" | custom-call | tf_op jit(solution)/shard_map/sum_plane/pallas_call | solution.py:361
  101.2 5.0 %all-to-all-start.2 = ((bf16[8,4,8,128]{3,2,1,0:T(8,128)(2,1)}), bf16[8,4,8,128]{3,2,1,0:T(8,128)(2,1)S(1)}, u32[]{:S(2)}, u32[]{:S(2)}) async-start(bf16[8,4,8,128]{3,2,1,0:T(8,128)(2,1)} %bitcast.27), calls=%async_computation.2 | async-start | bytes 131072 | tf_op jit(solution)/shard_map/all_to_all | solution.py:370
  106.3 2.6 %collective-permute-done.14.back = bf16[768,128]{1,0:T(8,128)(2,1)S(1)} collective-permute-done((bf16[768,128]{1,0:T(8,128)(2,1)}, bf16[768,128]{1,0:T(8,128)(2,1)S(1)}, u32[]{:S(2)}, u32[]{:S(2)}) %collective-permute-start.14) | collective-permute-done | bytes 196640 | tf_op jit(solution)/shard_map/ppermute | solution.py:22
  108.9 0.7 copy-done.15
  109.6 2.3 %norm_back.1 = bf16[128,768]{1,0:T(8,128)(2,1)} custom-call(bf16[128,768]{1,0:T(8,128)(2,1)} %bitcast.25, f32[768]{0:T(1024)} %gain.3, f32[768,128]{1,0:T(8,128)} %get-tuple-element.23.near, bf16[768,128]{1,0:T(8,128)(2,1)} %copy-done.15), custom_call_target="tpu_custom_call" | custom-call | tf_op jit(solution)/shard_map/norm_back/pallas_call | solution.py:374
  111.9 1.6 %all-to-all-done.2 = bf16[8,4,8,128]{3,2,1,0:T(8,128)(2,1)S(1)} async-done(((bf16[8,4,8,128]{3,2,1,0:T(8,128)(2,1)}), bf16[8,4,8,128]{3,2,1,0:T(8,128)(2,1)S(1)}, u32[]{:S(2)}, u32[]{:S(2)}) %all-to-all-start.2) | async-done | bytes 65568 | tf_op jit(solution)/shard_map/all_to_all | solution.py:370
  113.4 0.6 copy.18
  (45 shorter events, 0.1 us)
Async XLA Ops:
  2.5 20.6 %collective-permute-start.3 = (bf16[128,768]{1,0:T(8,128)(2,1)}, bf16[128,768]{1,0:T(8,128)(2,1)S(1)}, u32[]{:S(2)}, u32[]{:S(2)}) collective-permute-start(bf16[128,768]{1,0:T(8,128)(2,1)} %norm.1.normed), channel_id=1, source_target_pairs={{0,1},{1,0},{2,3},{3,2},{4,5},{5,4},{6,7},{7,6},{8,9},{9,8},{10,11... | collective-permute-start | bytes 589832 | tf_op jit(solution)/shard_map/ppermute | solution.py:22
  4.9 18.1 %collective-permute-start.4 = (bf16[128,768]{1,0:T(8,128)(2,1)}, bf16[128,768]{1,0:T(8,128)(2,1)S(1)}, u32[]{:S(2)}, u32[]{:S(2)}) collective-permute-start(bf16[128,768]{1,0:T(8,128)(2,1)} %bitcast.30), channel_id=1, source_target_pairs={{0,1},{1,0},{2,3},{3,2},{4,5},{5,4},{6,7},{7,6},{8,9},{9,8},{10,11... | collective-permute-start | bytes 589832 | tf_op jit(solution)/shard_map/ppermute | solution.py:22
  7.7 15.3 %collective-permute-start.2 = (bf16[12,1536]{1,0:T(8,128)(2,1)}, bf16[12,1536]{1,0:T(8,128)(2,1)S(1)}, u32[]{:S(2)}, u32[]{:S(2)}) collective-permute-start(bf16[12,1536]{1,0:T(8,128)(2,1)} %get-tuple-element.15), channel_id=1, source_target_pairs={{0,36},{36,0},{4,32},{32,4},{1,37},{37,1},{5,33},{33,5},{2,38},{38... | collective-permute-start | bytes 110600 | tf_op jit(solution)/shard_map/ppermute | solution.py:281
  15.5 7.5 %collective-permute-start = (bf16[12,1536]{1,0:T(8,128)(2,1)}, bf16[12,1536]{1,0:T(8,128)(2,1)S(1)}, u32[]{:S(2)}, u32[]{:S(2)}) collective-permute-start(bf16[12,1536]{1,0:T(8,128)(2,1)} %get-tuple-element.15), channel_id=1, source_target_pairs={{0,4},{4,0},{1,5},{5,1},{2,6},{6,2},{3,7},{7,3},{8,12},{12,8},{9,1... | collective-permute-start | bytes 110600 | tf_op jit(solution)/shard_map/ppermute | solution.py:18
  15.5 7.5 %collective-permute-start.1 = (bf16[12,1536]{1,0:T(8,128)(2,1)}, bf16[12,1536]{1,0:T(8,128)(2,1)S(1)}, u32[]{:S(2)}, u32[]{:S(2)}) collective-permute-start(bf16[12,1536]{1,0:T(8,128)(2,1)} %get-tuple-element.14.mine), channel_id=1, source_target_pairs={{0,32},{32,0},{1,33},{33,1},{2,34},{34,2},{3,35},{35,3},{4,36},{36... | collective-permute-start | bytes 110600 | tf_op jit(solution)/shard_map/ppermute | solution.py:18
  23.0 0.6 copy-start.18
  23.0 0.6 copy-start.16
  23.0 0.6 copy-start.17
  23.0 0.7 copy-start.14
  23.1 0.8 copy-start.3
  26.3 6.9 %copy-start.6 = (bf16[256,768]{1,0:T(8,128)(2,1)S(1)}, bf16[256,768]{1,0:T(8,128)(2,1)}, u32[]{:S(2)}) copy-start(bf16[256,768]{1,0:T(8,128)(2,1)} %get-tuple-element.16.own_near) | copy-start | bytes 1179652
  26.3 7.9 %copy-start.2 = (bf16[4,128,512]{2,1,0:T(8,128)(2,1)S(1)}, bf16[4,128,512]{2,1,0:T(8,128)(2,1)}, u32[]{:S(2)}) copy-start(bf16[4,128,512]{2,1,0:T(8,128)(2,1)} %get-tuple-element.27.ready) | copy-start | bytes 1572868
  26.4 28.0 %copy-start.4 = (bf16[128,768]{1,0:T(8,128)(2,1)S(1)}, bf16[128,768]{1,0:T(8,128)(2,1)}, u32[]{:S(2)}) copy-start(bf16[128,768]{1,0:T(8,128)(2,1)} %copy-done.3) | copy-start | bytes 589828
  26.4 28.5 %copy-start.19 = (s32[512]{0:T(512)S(1)}, s32[512]{0:T(512)}, u32[]{:S(2)}) copy-start(s32[512]{0:T(512)} %param.19) | copy-start | bytes 6148
  26.4 31.5 %all-to-all-start = ((bf16[16,48,1152]{2,1,0:T(8,128)(2,1)}), bf16[16,48,1152]{2,1,0:T(8,128)(2,1)S(1)}, u32[]{:S(2)}, u32[]{:S(2)}) async-start(bf16[16,48,1152]{2,1,0:T(8,128)(2,1)} %get-tuple-element.17), calls=%async_computation | async-start | bytes 3538944 | tf_op jit(solution)/shard_map/all_to_all | solution.py:305
  33.3 19.6 %collective-permute-start.5 = (bf16[256,768]{1,0:T(8,128)(2,1)S(1)}, bf16[256,768]{1,0:T(8,128)(2,1)S(1)}, u32[]{:S(2)}, u32[]{:S(2)}) collective-permute-start(bf16[256,768]{1,0:T(8,128)(2,1)S(1)} %copy-done.6), channel_id=1, source_target_pairs={{0,2},{1,3},{2,0},{3,1},{4,6},{5,7},{6,4},{7,5},{8,10},{9,11},{10,... | collective-permute-start | bytes 1179656 | tf_op jit(solution)/shard_map/ppermute | solution.py:22
  34.2 22.1 %collective-permute-start.10 = (bf16[4,128,512]{2,1,0:T(8,128)(2,1)S(1)}, bf16[4,128,512]{2,1,0:T(8,128)(2,1)S(1)}, u32[]{:S(2)}, u32[]{:S(2)}) collective-permute-start(bf16[4,128,512]{2,1,0:T(8,128)(2,1)S(1)} %copy-done.2), channel_id=1, source_target_pairs={{0,1},{1,0},{2,3},{3,2},{4,5},{5,4},{6,7},{7,6},{8,9},{9,8},{10,11... | collective-permute-start | bytes 1572872 | tf_op jit(solution)/shard_map/ppermute | solution.py:22
  36.9 19.5 %collective-permute-start.6 = (bf16[256,768]{1,0:T(8,128)(2,1)S(1)}, bf16[256,768]{1,0:T(8,128)(2,1)S(1)}, u32[]{:S(2)}, u32[]{:S(2)}) collective-permute-start(bf16[256,768]{1,0:T(8,128)(2,1)S(1)} %copy-done.6), channel_id=1, source_target_pairs={{0,4},{4,0},{1,5},{5,1},{2,6},{6,2},{3,7},{7,3},{8,12},{12,8},{9,1... | collective-permute-start | bytes 1179656 | tf_op jit(solution)/shard_map/ppermute | solution.py:18
  52.9 3.5 %copy-start.7 = (bf16[256,768]{1,0:T(8,128)(2,1)}, bf16[256,768]{1,0:T(8,128)(2,1)S(1)}, u32[]{:S(2)}) copy-start(bf16[256,768]{1,0:T(8,128)(2,1)S(1)} %collective-permute-done.5.own_far) | copy-start | bytes 1179652
  52.9 5.0 %collective-permute-start.7 = (bf16[256,768]{1,0:T(8,128)(2,1)S(1)}, bf16[256,768]{1,0:T(8,128)(2,1)}, u32[]{:S(2)}, u32[]{:S(2)}) collective-permute-start(bf16[256,768]{1,0:T(8,128)(2,1)S(1)} %collective-permute-done.5.own_far), channel_id=1, source_target_pairs={{0,4},{4,0},{1,5},{5,1},{2,6},{6,2},{3,7},{7,3},{8,12},{12,8},{9,1... | collective-permute-start | bytes 1179656 | tf_op jit(solution)/shard_map/ppermute | solution.py:18
  54.3 2.0 %collective-permute-start.8 = (bf16[128,768]{1,0:T(8,128)(2,1)}, bf16[128,768]{1,0:T(8,128)(2,1)S(1)}, u32[]{:S(2)}, u32[]{:S(2)}) collective-permute-start(bf16[128,768]{1,0:T(8,128)(2,1)} %bitcast.31), channel_id=1, source_target_pairs={{0,4},{4,0},{1,5},{5,1},{2,6},{6,2},{3,7},{7,3},{8,12},{12,8},{9,1... | collective-permute-start | bytes 589832 | tf_op jit(solution)/shard_map/ppermute | solution.py:18
  54.4 2.0 %collective-permute-start.9 = (bf16[128,768]{1,0:T(8,128)(2,1)S(1)}, bf16[128,768]{1,0:T(8,128)(2,1)S(1)}, u32[]{:S(2)}, u32[]{:S(2)}) collective-permute-start(bf16[128,768]{1,0:T(8,128)(2,1)S(1)} %copy-done.4), channel_id=1, source_target_pairs={{0,4},{4,0},{1,5},{5,1},{2,6},{6,2},{3,7},{7,3},{8,12},{12,8},{9,1... | collective-permute-start | bytes 589832 | tf_op jit(solution)/shard_map/ppermute | solution.py:18
  56.3 0.7 copy-start.12
  56.3 0.8 copy-start.13
  56.3 1.5 %copy-start.5 = (bf16[4,128,512]{2,1,0:T(8,128)(2,1)}, bf16[4,128,512]{2,1,0:T(8,128)(2,1)S(1)}, u32[]{:S(2)}) copy-start(bf16[4,128,512]{2,1,0:T(8,128)(2,1)S(1)} %collective-permute-done.10.bias_pair) | copy-start | bytes 1572868
  57.1 0.8 copy-start.8
  57.9 1.2 %copy-start = (bf16[16,48,1152]{2,1,0:T(8,128)(2,1)}, bf16[16,48,1152]{2,1,0:T(8,128)(2,1)S(1)}, u32[]{:S(2)}) copy-start(bf16[16,48,1152]{2,1,0:T(8,128)(2,1)S(1)} %all-to-all-done.weights) | copy-start | bytes 5308420
  71.7 6.8 %copy-start.21 = (bf16[2,768,128]{2,1,0:T(8,128)(2,1)S(1)}, bf16[2,768,128]{2,1,0:T(8,128)(2,1)}, u32[]{:S(2)}) copy-start(bf16[2,768,128]{2,1,0:T(8,128)(2,1)} %get-tuple-element.22) | copy-start | bytes 1179652
  71.7 7.5 %copy-start.20 = (bf16[2,768,128]{2,1,0:T(8,128)(2,1)S(1)}, bf16[2,768,128]{2,1,0:T(8,128)(2,1)}, u32[]{:S(2)}) copy-start(bf16[2,768,128]{2,1,0:T(8,128)(2,1)} %get-tuple-element.20) | copy-start | bytes 1179652
  71.7 26.5 %all-to-all-start.1 = ((bf16[16,4,2,16,256]{4,3,2,1,0:T(8,128)(2,1)}), bf16[16,4,2,16,256]{4,3,2,1,0:T(8,128)(2,1)S(1)}, u32[]{:S(2)}, u32[]{:S(2)}) async-start(bf16[16,4,2,16,256]{4,3,2,1,0:T(8,128)(2,1)} %get-tuple-element.25), calls=%async_computation.1 | async-start | bytes 2097152 | tf_op jit(solution)/shard_map/all_to_all | solution.py:360
  78.5 2.0 %collective-permute-start.12 = (bf16[2,768,128]{2,1,0:T(8,128)(2,1)S(1)}, bf16[2,768,128]{2,1,0:T(8,128)(2,1)S(1)}, u32[]{:S(2)}, u32[]{:S(2)}) collective-permute-start(bf16[2,768,128]{2,1,0:T(8,128)(2,1)S(1)} %copy-done.21), channel_id=1, source_target_pairs={{0,4},{4,0},{1,5},{5,1},{2,6},{6,2},{3,7},{7,3},{8,12},{12,8},{9,1... | collective-permute-start | bytes 1179656 | tf_op jit(solution)/shard_map/ppermute | solution.py:18
  79.2 4.1 %collective-permute-start.11 = (bf16[2,768,128]{2,1,0:T(8,128)(2,1)S(1)}, bf16[2,768,128]{2,1,0:T(8,128)(2,1)S(1)}, u32[]{:S(2)}, u32[]{:S(2)}) collective-permute-start(bf16[2,768,128]{2,1,0:T(8,128)(2,1)S(1)} %copy-done.20), channel_id=1, source_target_pairs={{0,4},{4,0},{1,5},{5,1},{2,6},{6,2},{3,7},{7,3},{8,12},{12,8},{9,1... | collective-permute-start | bytes 1179656 | tf_op jit(solution)/shard_map/ppermute | solution.py:18
  80.6 0.7 copy-start.11
  83.3 10.5 %collective-permute-start.13 = (bf16[2,768,128]{2,1,0:T(8,128)(2,1)}, bf16[2,768,128]{2,1,0:T(8,128)(2,1)S(1)}, u32[]{:S(2)}, u32[]{:S(2)}) collective-permute-start(bf16[2,768,128]{2,1,0:T(8,128)(2,1)} %sum_cores.1), channel_id=1, source_target_pairs={{0,1},{1,0},{2,3},{3,2},{4,5},{5,4},{6,7},{7,6},{8,9},{9,8},{10,11... | collective-permute-start | bytes 1179656 | tf_op jit(solution)/shard_map/ppermute | solution.py:22
  83.3 10.5 %copy-start.9 = (bf16[2,768,128]{2,1,0:T(8,128)(2,1)}, bf16[2,768,128]{2,1,0:T(8,128)(2,1)S(1)}, u32[]{:S(2)}) copy-start(bf16[2,768,128]{2,1,0:T(8,128)(2,1)S(1)} %collective-permute-done.11.oth) | copy-start | bytes 1179652
  93.8 0.8 copy-start.10
  96.8 12.1 %collective-permute-start.14 = (bf16[768,128]{1,0:T(8,128)(2,1)}, bf16[768,128]{1,0:T(8,128)(2,1)S(1)}, u32[]{:S(2)}, u32[]{:S(2)}) collective-permute-start(bf16[768,128]{1,0:T(8,128)(2,1)} %get-tuple-element.24.after), channel_id=1, source_target_pairs={{0,2},{1,3},{2,0},{3,1},{4,6},{5,7},{6,4},{7,5},{8,10},{9,11},{10,... | collective-permute-start | bytes 589832 | tf_op jit(solution)/shard_map/ppermute | solution.py:22
  98.2 1.0 copy-start.1
  101.2 12.2 %all-to-all-start.2 = ((bf16[8,4,8,128]{3,2,1,0:T(8,128)(2,1)}), bf16[8,4,8,128]{3,2,1,0:T(8,128)(2,1)S(1)}, u32[]{:S(2)}, u32[]{:S(2)}) async-start(bf16[8,4,8,128]{3,2,1,0:T(8,128)(2,1)} %bitcast.27), calls=%async_computation.2 | async-start | bytes 131072 | tf_op jit(solution)/shard_map/all_to_all | solution.py:370
  108.9 0.7 copy-start.15

commit v5 on v4

--- a/solution.py
+++ b/solution.py
@@ -261,7 +261,7 @@
     smem = pl.BlockSpec(memory_space=pltpu.SMEM)
     anywhere = pl.BlockSpec(memory_space=pl.ANY)
     gain = layer_norm_scale
-    room = pltpu.CompilerParams(vmem_limit_bytes=58 * 1024 * 1024)
+    room = pltpu.CompilerParams(vmem_limit_bytes=63 * 1024 * 1024)
 
     groups = pair_bias.reshape((heads, NC, 2) + pair_bias.shape[1:])
     groups = lax.dynamic_index_in_dim(groups, core, 1, False)

time: 115 us -> 113 us (0.983)
  local copies, waits for them, and re-layouts: 10.2 us -> 7.97 us
    unnamed x44 -> x42, local copies, waits for them, and re-layouts: 6.68 us -> 4.5 us
  transfers between devices with their start and end apart: 18 -> 18, of which waited for: 7 -> 8; matrix products, arithmetic and copies ran while one was open for 3% -> 3% of each run, Pallas kernels for 9% -> 9%
where the time goes in v5:
time: 113 us
  starting transfers between devices  39.7 us (35%)
  waiting for transfers between devices  36.2 us (32%)
  Pallas kernels  27.5 us (24%)
  local copies, waits for them, and re-layouts  7.97 us (7%)
    ppermute x6, waiting for transfers between devices, swap(): return lax.ppermute(value, ('th', 'tl'), [(i, i ^ by) for i in range(NT)])  28.2 us
    pallas_call x1, Pallas kernels, on_device(): pl.pallas_call(attention_kernel, out_shape=(jax.ShapeDtypeStruct((width,...  12.6 us
    ppermute x1, starting transfers between devices, on_device(): lax.ppermute(send, ('zh', 'core'), [(0, 3), (3, 0), (1, 2), (2, 1)])  7.82 us
    ppermute x6, starting transfers between devices, swap(): return lax.ppermute(value, ('th', 'tl'), [(i, i ^ by) for i in range(NT)])  7.24 us
    ppermute x8, waiting for transfers between devices, shift(): lax.ppermute(value, axis, [(i, (i + by) % count) for i in range(count)])  7.11 us
    all_to_all x1, starting transfers between devices, on_device(): weights = lax.all_to_all(pieces, ('x', 'y'), 0, 0, tiled=True)  6.94 us
    all_to_all x1, starting transfers between devices, on_device(): parts = lax.all_to_all(out_bias, ('x', 'y'), 0, 0, tiled=True)  6.8 us
    all_to_all x1, starting transfers between devices, on_device(): lax.all_to_all(planes.reshape((-1,) + shape[3:]), ('zh', 'core', 'tl'), 0...  5.52 us
  transfers between devices with their start and end apart: 18, of which 8 were waited for; matrix products, arithmetic and copies ran while one was open for 3% of the time, Pallas kernels for 9%

profile of v5, /device:TPU:1, one launch (start us, length us, event | category | flops | bytes accessed | tf_op | source)
XLA Modules:
  0.0 112.7 jit_solution(8064553638152067523)
XLA Ops:
  0.6 1.8 %norm.1.normed = bf16[128,768]{1,0:T(8,128)(2,1)} custom-call(bf16[128,768]{1,0:T(8,128)(2,1)} %bitcast.24, f32[768]{0:T(1024)} %gain.3), custom_call_target="tpu_custom_call" | custom-call | tf_op jit(solution)/shard_map/norm/pallas_call | solution.py:283
  2.5 2.5 %collective-permute-start.3 = (bf16[128,768]{1,0:T(8,128)(2,1)}, bf16[128,768]{1,0:T(8,128)(2,1)S(1)}, u32[]{:S(2)}, u32[]{:S(2)}) collective-permute-start(bf16[128,768]{1,0:T(8,128)(2,1)} %norm.1.normed), channel_id=1, source_target_pairs={{0,1},{1,0},{2,3},{3,2},{4,5},{5,4},{6,7},{7,6},{8,9},{9,8},{10,11... | collective-permute-start | bytes 589832 | tf_op jit(solution)/shard_map/ppermute | solution.py:22
  4.9 0.0 collective-permute-start.4
  5.0 0.6 stack.27.pos
  5.6 2.1 %pack.1 = (bf16[12,1536]{1,0:T(8,128)(2,1)}, bf16[12,1536]{1,0:T(8,128)(2,1)}) custom-call(s32[6]{0:T(128)} %stack.27.pos, bf16[12,768]{1,0:T(8,128)(2,1)} %query.1, bf16[12,768]{1,0:T(8,128)(2,1)} %key.1, bf16[12,768]{1,0:T(8,128)(2,1)} %value.1, bf16[12,768]{1,0:T(8,128)(2,1)} %gate.1, bf16[12,768]{1,0:T(8,128)(2,1)} %out.1), custom_call_target="tpu_custom_call" | custom-call | tf_op jit(solution)/shard_map/pack/pallas_call | solution.py:272
  7.6 7.8 %collective-permute-start.2 = (bf16[12,1536]{1,0:T(8,128)(2,1)}, bf16[12,1536]{1,0:T(8,128)(2,1)S(1)}, u32[]{:S(2)}, u32[]{:S(2)}) collective-permute-start(bf16[12,1536]{1,0:T(8,128)(2,1)} %get-tuple-element.15), channel_id=1, source_target_pairs={{0,36},{36,0},{4,32},{32,4},{1,37},{37,1},{5,33},{33,5},{2,38},{38... | collective-permute-start | bytes 110600 | tf_op jit(solution)/shard_map/ppermute | solution.py:281
  15.5 0.2 collective-permute-start.1
  15.7 2.2 %dynamic-slice_bitcast_fusion = (bf16[4,128,512]{2,1,0:T(8,128)(2,1)}, bf16[4,128,512]{2,1,0:T(8,128)(2,1)}) fusion(bf16[4,2,2,128,512]{4,3,2,1,0:T(8,128)(2,1)} %bitcast.26, s32[]{:T(128)S(6)} %select_n.18, s32[]{:T(128)S(6)} %select_n.22, s32[]{:T(128)S(6)} %select_n.20), kind=kLoop, calls=%fused_computation | loop fusion | bytes 2097164 | tf_op jit(solution)/shard_map/jit(dynamic_index_in_dim)/squeeze | solution.py:269
  17.9 5.0 %collective-permute-done.1.above = bf16[12,1536]{1,0:T(8,128)(2,1)S(1)} collective-permute-done((bf16[12,1536]{1,0:T(8,128)(2,1)}, bf16[12,1536]{1,0:T(8,128)(2,1)S(1)}, u32[]{:S(2)}, u32[]{:S(2)}) %collective-permute-start.1) | collective-permute-done | bytes 36896 | tf_op jit(solution)/shard_map/ppermute | solution.py:18
  23.0 0.6 copy-done.18
  23.5 0.0 copy-done.16
  23.6 0.0 copy-done.17
  23.6 0.1 copy-done.14
  23.7 0.1 copy-done.1
  23.8 2.5 %assemble.1 = (bf16[16,48,1152]{2,1,0:T(8,128)(2,1)}, bf16[256,768]{1,0:T(8,128)(2,1)}) custom-call(s32[6]{0:T(128)} %stack.27.pos, bf16[12,1536]{1,0:T(8,128)(2,1)} %get-tuple-element.14.mine, bf16[12,1536]{1,0:T(8,128)(2,1)} %copy-done.17, bf16[12,1536]{1,0:T(8,128)(2,1)} %copy-done.18, bf16[12,1536]{1,0:T(8,128)(2,1)} %copy-done.16, ...), custom_call_target="tpu_custom_call" | custom-call | tf_op jit(solution)/shard_map/assemble/pallas_call | solution.py:293
  26.3 0.0 copy-start.11
  26.3 0.0 copy-start.19
  26.3 6.9 %all-to-all-start = ((bf16[16,48,1152]{2,1,0:T(8,128)(2,1)}), bf16[16,48,1152]{2,1,0:T(8,128)(2,1)}, u32[]{:S(2)}, u32[]{:S(2)}) async-start(bf16[16,48,1152]{2,1,0:T(8,128)(2,1)} %get-tuple-element.17), calls=%async_computation | async-start | bytes 3538944 | tf_op jit(solution)/shard_map/all_to_all | solution.py:305
  33.3 1.0 collective-permute-start.5
  34.3 2.6 %collective-permute-start.10 = (bf16[4,128,512]{2,1,0:T(8,128)(2,1)S(1)}, bf16[4,128,512]{2,1,0:T(8,128)(2,1)S(1)}, u32[]{:S(2)}, u32[]{:S(2)}) collective-permute-start(bf16[4,128,512]{2,1,0:T(8,128)(2,1)S(1)} %copy-done), channel_id=1, source_target_pairs={{0,1},{1,0},{2,3},{3,2},{4,5},{5,4},{6,7},{7,6},{8,9},{9,8},{10,11... | collective-permute-start | bytes 1572872 | tf_op jit(solution)/shard_map/ppermute | solution.py:22
  36.9 1.7 %collective-permute-start.6 = (bf16[256,768]{1,0:T(8,128)(2,1)S(1)}, bf16[256,768]{1,0:T(8,128)(2,1)S(1)}, u32[]{:S(2)}, u32[]{:S(2)}) collective-permute-start(bf16[256,768]{1,0:T(8,128)(2,1)S(1)} %copy-done.4), channel_id=1, source_target_pairs={{0,4},{4,0},{1,5},{5,1},{2,6},{6,2},{3,7},{7,3},{8,12},{12,8},{9,1... | collective-permute-start | bytes 1179656 | tf_op jit(solution)/shard_map/ppermute | solution.py:18
  38.6 14.2 %collective-permute-done.5.own_far = bf16[256,768]{1,0:T(8,128)(2,1)S(1)} collective-permute-done((bf16[256,768]{1,0:T(8,128)(2,1)S(1)}, bf16[256,768]{1,0:T(8,128)(2,1)S(1)}, u32[]{:S(2)}, u32[]{:S(2)}) %collective-permute-start.5) | collective-permute-done | bytes 393248 | tf_op jit(solution)/shard_map/ppermute | solution.py:22
  52.9 1.5 %collective-permute-start.7 = (bf16[256,768]{1,0:T(8,128)(2,1)S(1)}, bf16[256,768]{1,0:T(8,128)(2,1)S(1)}, u32[]{:S(2)}, u32[]{:S(2)}) collective-permute-start(bf16[256,768]{1,0:T(8,128)(2,1)S(1)} %collective-permute-done.5.own_far), channel_id=1, source_target_pairs={{0,4},{4,0},{1,5},{5,1},{2,6},{6,2},{3,7},{7,3},{8,12},{12,8},{9,1... | collective-permute-start | bytes 1179656 | tf_op jit(solution)/shard_map/ppermute | solution.py:18
  54.4 0.1 collective-permute-start.8
  54.4 0.4 collective-permute-start.9
  54.9 0.6 compare_convert_fusion
  55.5 0.5 collective-permute-done.8.cot_oth0
  56.0 0.3 collective-permute-done.9.cot_oth1
  56.3 0.8 copy-done.6
  57.1 0.7 copy-done.7
  57.8 12.6 %attention.1 = (f32[768,128]{1,0:T(8,128)}, f32[768,128]{1,0:T(8,128)}, bf16[2,768,128]{2,1,0:T(8,128)(2,1)}, bf16[2,768,128]{2,1,0:T(8,128)(2,1)}, bf16[2,768,1...) custom-call(s32[6]{0:T(128)} %stack.27.pos, bf16[256,768]{1,0:T(8,128)(2,1)} %get-tuple-element.16.own_near, ...), custom_call_target="tpu_custom_call" | custom-call | tf_op jit(solution)/shard_map/attention/pallas_call | solution.py:313
  70.4 6.8 %all-to-all-start.1 = ((bf16[16,4,2,16,256]{4,3,2,1,0:T(8,128)(2,1)}), bf16[16,4,2,16,256]{4,3,2,1,0:T(8,128)(2,1)}, u32[]{:S(2)}, u32[]{:S(2)}) async-start(bf16[16,4,2,16,256]{4,3,2,1,0:T(8,128)(2,1)} %get-tuple-element.25), calls=%async_computation.1 | async-start | bytes 2097152 | tf_op jit(solution)/shard_map/all_to_all | solution.py:360
  77.2 1.3 %collective-permute-start.12 = (bf16[2,768,128]{2,1,0:T(8,128)(2,1)S(1)}, bf16[2,768,128]{2,1,0:T(8,128)(2,1)S(1)}, u32[]{:S(2)}, u32[]{:S(2)}) collective-permute-start(bf16[2,768,128]{2,1,0:T(8,128)(2,1)S(1)} %copy-done.20), channel_id=1, source_target_pairs={{0,4},{4,0},{1,5},{5,1},{2,6},{6,2},{3,7},{7,3},{8,12},{12,8},{9,1... | collective-permute-start | bytes 1179656 | tf_op jit(solution)/shard_map/ppermute | solution.py:18
  78.6 0.1 collective-permute-start.11
  78.7 1.2 %collective-permute-done.12.oth = bf16[2,768,128]{2,1,0:T(8,128)(2,1)S(1)} collective-permute-done((bf16[2,768,128]{2,1,0:T(8,128)(2,1)S(1)}, bf16[2,768,128]{2,1,0:T(8,128)(2,1)S(1)}, u32[]{:S(2)}, u32[]{:S(2)}) %collective-permute-start.12) | collective-permute-done | bytes 393248 | tf_op jit(solution)/shard_map/ppermute | solution.py:18
  79.9 0.8 copy-done.10
  80.7 1.9 %sum_cores.1 = bf16[2,768,128]{2,1,0:T(8,128)(2,1)} custom-call(bf16[2,768,128]{2,1,0:T(8,128)(2,1)} %get-tuple-element.21.own, bf16[2,768,128]{2,1,0:T(8,128)(2,1)} %copy-done.10), custom_call_target="tpu_custom_call" | custom-call | tf_op jit(solution)/shard_map/sum_cores/pallas_call | solution.py:342
  82.6 10.6 %collective-permute-done.13.got = bf16[2,768,128]{2,1,0:T(8,128)(2,1)S(1)} collective-permute-done((bf16[2,768,128]{2,1,0:T(8,128)(2,1)}, bf16[2,768,128]{2,1,0:T(8,128)(2,1)S(1)}, u32[]{:S(2)}, u32[]{:S(2)}) %collective-permute-start.13) | collective-permute-done | bytes 393248 | tf_op jit(solution)/shard_map/ppermute | solution.py:22
  93.3 0.8 copy-done.9
  94.0 2.2 %sum_pair.1 = (f32[768,128]{1,0:T(8,128)}, bf16[768,128]{1,0:T(8,128)(2,1)}) custom-call(f32[768,128]{1,0:T(8,128)} %get-tuple-element.18.own_near, f32[768,128]{1,0:T(8,128)} %get-tuple-element.19.own_far, bf16[2,768,128]{2,1,0:T(8,128)(2,1)} %copy-done.8, bf16[2,768,128]{2,1,0:T(8,128)(2,1)} %copy-done.9), custom_call_target="tpu_custom_call" | custom-call | tf_op jit(solution)/shard_map/sum_pair/pallas_call | solution.py:350
  96.2 1.1 %collective-permute-start.14 = (bf16[768,128]{1,0:T(8,128)(2,1)}, bf16[768,128]{1,0:T(8,128)(2,1)S(1)}, u32[]{:S(2)}, u32[]{:S(2)}) collective-permute-start(bf16[768,128]{1,0:T(8,128)(2,1)} %get-tuple-element.24.after), channel_id=1, source_target_pairs={{0,2},{1,3},{2,0},{3,1},{4,6},{5,7},{6,4},{7,5},{8,10},{9,11},{10,... | collective-permute-start | bytes 589832 | tf_op jit(solution)/shard_map/ppermute | solution.py:22
  97.4 2.0 %sum_plane.1 = bf16[2,2,2,4,8,128]{5,4,3,2,1,0:T(8,128)(2,1)} custom-call(s32[6]{0:T(128)} %stack.27.pos, bf16[16,4,2,16,256]{4,3,2,1,0:T(8,128)(2,1)} %all-to-all-done.1.parts, bf16[768,128]{1,0:T(8,128)(2,1)} %get-tuple-element.24.after), custom_call_target="tpu_custom_call" | custom-call | tf_op jit(solution)/shard_map/sum_plane/pallas_call | solution.py:361
  99.4 5.5 %all-to-all-start.2 = ((bf16[8,4,8,128]{3,2,1,0:T(8,128)(2,1)}), bf16[8,4,8,128]{3,2,1,0:T(8,128)(2,1)S(1)}, u32[]{:S(2)}, u32[]{:S(2)}) async-start(bf16[8,4,8,128]{3,2,1,0:T(8,128)(2,1)} %bitcast.27), calls=%async_computation.2 | async-start | bytes 131072 | tf_op jit(solution)/shard_map/all_to_all | solution.py:370
  104.9 3.4 %collective-permute-done.14.back = bf16[768,128]{1,0:T(8,128)(2,1)S(1)} collective-permute-done((bf16[768,128]{1,0:T(8,128)(2,1)}, bf16[768,128]{1,0:T(8,128)(2,1)S(1)}, u32[]{:S(2)}, u32[]{:S(2)}) %collective-permute-start.14) | collective-permute-done | bytes 196640 | tf_op jit(solution)/shard_map/ppermute | solution.py:22
  108.3 0.7 copy-done.15
  109.0 2.3 %norm_back.1 = bf16[128,768]{1,0:T(8,128)(2,1)} custom-call(bf16[128,768]{1,0:T(8,128)(2,1)} %bitcast.25, f32[768]{0:T(1024)} %gain.3, f32[768,128]{1,0:T(8,128)} %get-tuple-element.23.near, bf16[768,128]{1,0:T(8,128)(2,1)} %copy-done.15), custom_call_target="tpu_custom_call" | custom-call | tf_op jit(solution)/shard_map/norm_back/pallas_call | solution.py:374
  111.3 0.8 all-to-all-done.2
  112.1 0.6 copy.18
  (43 shorter events, 0.1 us)
Async XLA Ops:
  2.5 20.5 %collective-permute-start.3 = (bf16[128,768]{1,0:T(8,128)(2,1)}, bf16[128,768]{1,0:T(8,128)(2,1)S(1)}, u32[]{:S(2)}, u32[]{:S(2)}) collective-permute-start(bf16[128,768]{1,0:T(8,128)(2,1)} %norm.1.normed), channel_id=1, source_target_pairs={{0,1},{1,0},{2,3},{3,2},{4,5},{5,4},{6,7},{7,6},{8,9},{9,8},{10,11... | collective-permute-start | bytes 589832 | tf_op jit(solution)/shard_map/ppermute | solution.py:22
  4.9 18.0 %collective-permute-start.4 = (bf16[128,768]{1,0:T(8,128)(2,1)}, bf16[128,768]{1,0:T(8,128)(2,1)S(1)}, u32[]{:S(2)}, u32[]{:S(2)}) collective-permute-start(bf16[128,768]{1,0:T(8,128)(2,1)} %bitcast.30), channel_id=1, source_target_pairs={{0,1},{1,0},{2,3},{3,2},{4,5},{5,4},{6,7},{7,6},{8,9},{9,8},{10,11... | collective-permute-start | bytes 589832 | tf_op jit(solution)/shard_map/ppermute | solution.py:22
  7.6 15.3 %collective-permute-start.2 = (bf16[12,1536]{1,0:T(8,128)(2,1)}, bf16[12,1536]{1,0:T(8,128)(2,1)S(1)}, u32[]{:S(2)}, u32[]{:S(2)}) collective-permute-start(bf16[12,1536]{1,0:T(8,128)(2,1)} %get-tuple-element.15), channel_id=1, source_target_pairs={{0,36},{36,0},{4,32},{32,4},{1,37},{37,1},{5,33},{33,5},{2,38},{38... | collective-permute-start | bytes 110600 | tf_op jit(solution)/shard_map/ppermute | solution.py:281
  15.5 7.5 %collective-permute-start = (bf16[12,1536]{1,0:T(8,128)(2,1)}, bf16[12,1536]{1,0:T(8,128)(2,1)S(1)}, u32[]{:S(2)}, u32[]{:S(2)}) collective-permute-start(bf16[12,1536]{1,0:T(8,128)(2,1)} %get-tuple-element.15), channel_id=1, source_target_pairs={{0,4},{4,0},{1,5},{5,1},{2,6},{6,2},{3,7},{7,3},{8,12},{12,8},{9,1... | collective-permute-start | bytes 110600 | tf_op jit(solution)/shard_map/ppermute | solution.py:18
  15.5 7.5 %collective-permute-start.1 = (bf16[12,1536]{1,0:T(8,128)(2,1)}, bf16[12,1536]{1,0:T(8,128)(2,1)S(1)}, u32[]{:S(2)}, u32[]{:S(2)}) collective-permute-start(bf16[12,1536]{1,0:T(8,128)(2,1)} %get-tuple-element.14.mine), channel_id=1, source_target_pairs={{0,32},{32,0},{1,33},{33,1},{2,34},{34,2},{3,35},{35,3},{4,36},{36... | collective-permute-start | bytes 110600 | tf_op jit(solution)/shard_map/ppermute | solution.py:18
  22.9 0.6 copy-start.18
  22.9 0.6 copy-start.16
  22.9 0.7 copy-start.17
  23.0 0.7 copy-start.14
  23.0 0.8 copy-start.1
  26.3 7.0 %copy-start.4 = (bf16[256,768]{1,0:T(8,128)(2,1)S(1)}, bf16[256,768]{1,0:T(8,128)(2,1)}, u32[]{:S(2)}) copy-start(bf16[256,768]{1,0:T(8,128)(2,1)} %get-tuple-element.16.own_near) | copy-start | bytes 1179652
  26.3 8.0 %copy-start = (bf16[4,128,512]{2,1,0:T(8,128)(2,1)S(1)}, bf16[4,128,512]{2,1,0:T(8,128)(2,1)}, u32[]{:S(2)}) copy-start(bf16[4,128,512]{2,1,0:T(8,128)(2,1)} %get-tuple-element.27.ready) | copy-start | bytes 1572868
  26.3 28.1 %copy-start.11 = (bf16[1,128,768]{2,1,0:T(8,128)(2,1)S(1)}, bf16[1,128,768]{2,1,0:T(8,128)(2,1)}, u32[]{:S(2)}) copy-start(bf16[1,128,768]{2,1,0:T(8,128)(2,1)} %param.11) | copy-start | bytes 589828
  26.3 28.1 %copy-start.2 = (bf16[128,768]{1,0:T(8,128)(2,1)S(1)}, bf16[128,768]{1,0:T(8,128)(2,1)}, u32[]{:S(2)}) copy-start(bf16[128,768]{1,0:T(8,128)(2,1)} %copy-done.1) | copy-start | bytes 589828
  26.3 28.5 %copy-start.19 = (s32[512]{0:T(512)S(1)}, s32[512]{0:T(512)}, u32[]{:S(2)}) copy-start(s32[512]{0:T(512)} %param.19) | copy-start | bytes 6148
  26.3 30.8 %all-to-all-start = ((bf16[16,48,1152]{2,1,0:T(8,128)(2,1)}), bf16[16,48,1152]{2,1,0:T(8,128)(2,1)}, u32[]{:S(2)}, u32[]{:S(2)}) async-start(bf16[16,48,1152]{2,1,0:T(8,128)(2,1)} %get-tuple-element.17), calls=%async_computation | async-start | bytes 3538944 | tf_op jit(solution)/shard_map/all_to_all | solution.py:305
  33.3 19.6 %collective-permute-start.5 = (bf16[256,768]{1,0:T(8,128)(2,1)S(1)}, bf16[256,768]{1,0:T(8,128)(2,1)S(1)}, u32[]{:S(2)}, u32[]{:S(2)}) collective-permute-start(bf16[256,768]{1,0:T(8,128)(2,1)S(1)} %copy-done.4), channel_id=1, source_target_pairs={{0,2},{1,3},{2,0},{3,1},{4,6},{5,7},{6,4},{7,5},{8,10},{9,11},{10,... | collective-permute-start | bytes 1179656 | tf_op jit(solution)/shard_map/ppermute | solution.py:22
  34.3 22.0 %collective-permute-start.10 = (bf16[4,128,512]{2,1,0:T(8,128)(2,1)S(1)}, bf16[4,128,512]{2,1,0:T(8,128)(2,1)S(1)}, u32[]{:S(2)}, u32[]{:S(2)}) collective-permute-start(bf16[4,128,512]{2,1,0:T(8,128)(2,1)S(1)} %copy-done), channel_id=1, source_target_pairs={{0,1},{1,0},{2,3},{3,2},{4,5},{5,4},{6,7},{7,6},{8,9},{9,8},{10,11... | collective-permute-start | bytes 1572872 | tf_op jit(solution)/shard_map/ppermute | solution.py:22
  36.9 19.4 %collective-permute-start.6 = (bf16[256,768]{1,0:T(8,128)(2,1)S(1)}, bf16[256,768]{1,0:T(8,128)(2,1)S(1)}, u32[]{:S(2)}, u32[]{:S(2)}) collective-permute-start(bf16[256,768]{1,0:T(8,128)(2,1)S(1)} %copy-done.4), channel_id=1, source_target_pairs={{0,4},{4,0},{1,5},{5,1},{2,6},{6,2},{3,7},{7,3},{8,12},{12,8},{9,1... | collective-permute-start | bytes 1179656 | tf_op jit(solution)/shard_map/ppermute | solution.py:18
  52.9 3.4 %copy-start.5 = (bf16[256,768]{1,0:T(8,128)(2,1)}, bf16[256,768]{1,0:T(8,128)(2,1)S(1)}, u32[]{:S(2)}) copy-start(bf16[256,768]{1,0:T(8,128)(2,1)S(1)} %collective-permute-done.5.own_far) | copy-start | bytes 1179652
  52.9 3.4 %collective-permute-start.7 = (bf16[256,768]{1,0:T(8,128)(2,1)S(1)}, bf16[256,768]{1,0:T(8,128)(2,1)S(1)}, u32[]{:S(2)}, u32[]{:S(2)}) collective-permute-start(bf16[256,768]{1,0:T(8,128)(2,1)S(1)} %collective-permute-done.5.own_far), channel_id=1, source_target_pairs={{0,4},{4,0},{1,5},{5,1},{2,6},{6,2},{3,7},{7,3},{8,12},{12,8},{9,1... | collective-permute-start | bytes 1179656 | tf_op jit(solution)/shard_map/ppermute | solution.py:18
  54.4 1.6 %collective-permute-start.8 = (bf16[128,768]{1,0:T(8,128)(2,1)S(1)}, bf16[128,768]{1,0:T(8,128)(2,1)S(1)}, u32[]{:S(2)}, u32[]{:S(2)}) collective-permute-start(bf16[128,768]{1,0:T(8,128)(2,1)S(1)} %bitcast.32), channel_id=1, source_target_pairs={{0,4},{4,0},{1,5},{5,1},{2,6},{6,2},{3,7},{7,3},{8,12},{12,8},{9,1... | collective-permute-start | bytes 589832 | tf_op jit(solution)/shard_map/ppermute | solution.py:18
  54.4 1.8 %collective-permute-start.9 = (bf16[128,768]{1,0:T(8,128)(2,1)S(1)}, bf16[128,768]{1,0:T(8,128)(2,1)S(1)}, u32[]{:S(2)}, u32[]{:S(2)}) collective-permute-start(bf16[128,768]{1,0:T(8,128)(2,1)S(1)} %copy-done.2), channel_id=1, source_target_pairs={{0,4},{4,0},{1,5},{5,1},{2,6},{6,2},{3,7},{7,3},{8,12},{12,8},{9,1... | collective-permute-start | bytes 589832 | tf_op jit(solution)/shard_map/ppermute | solution.py:18
  56.0 1.8 %copy-start.12 = (bf16[128,768]{1,0:T(8,128)(2,1)}, bf16[128,768]{1,0:T(8,128)(2,1)S(1)}, u32[]{:S(2)}) copy-start(bf16[128,768]{1,0:T(8,128)(2,1)S(1)} %collective-permute-done.8.cot_oth0) | copy-start | bytes 589828
  56.3 1.5 %copy-start.13 = (bf16[128,768]{1,0:T(8,128)(2,1)}, bf16[128,768]{1,0:T(8,128)(2,1)S(1)}, u32[]{:S(2)}) copy-start(bf16[128,768]{1,0:T(8,128)(2,1)S(1)} %collective-permute-done.9.cot_oth1) | copy-start | bytes 589828
  56.3 1.5 %copy-start.3 = (bf16[4,128,512]{2,1,0:T(8,128)(2,1)}, bf16[4,128,512]{2,1,0:T(8,128)(2,1)S(1)}, u32[]{:S(2)}) copy-start(bf16[4,128,512]{2,1,0:T(8,128)(2,1)S(1)} %collective-permute-done.10.bias_pair) | copy-start | bytes 1572868
  56.3 0.8 copy-start.6
  57.1 0.7 copy-start.7
  70.4 6.8 %copy-start.20 = (bf16[2,768,128]{2,1,0:T(8,128)(2,1)S(1)}, bf16[2,768,128]{2,1,0:T(8,128)(2,1)}, u32[]{:S(2)}) copy-start(bf16[2,768,128]{2,1,0:T(8,128)(2,1)} %get-tuple-element.22) | copy-start | bytes 1179652
  70.4 27.0 %all-to-all-start.1 = ((bf16[16,4,2,16,256]{4,3,2,1,0:T(8,128)(2,1)}), bf16[16,4,2,16,256]{4,3,2,1,0:T(8,128)(2,1)}, u32[]{:S(2)}, u32[]{:S(2)}) async-start(bf16[16,4,2,16,256]{4,3,2,1,0:T(8,128)(2,1)} %get-tuple-element.25), calls=%async_computation.1 | async-start | bytes 2097152 | tf_op jit(solution)/shard_map/all_to_all | solution.py:360
  77.2 2.7 %collective-permute-start.12 = (bf16[2,768,128]{2,1,0:T(8,128)(2,1)S(1)}, bf16[2,768,128]{2,1,0:T(8,128)(2,1)S(1)}, u32[]{:S(2)}, u32[]{:S(2)}) collective-permute-start(bf16[2,768,128]{2,1,0:T(8,128)(2,1)S(1)} %copy-done.20), channel_id=1, source_target_pairs={{0,4},{4,0},{1,5},{5,1},{2,6},{6,2},{3,7},{7,3},{8,12},{12,8},{9,1... | collective-permute-start | bytes 1179656 | tf_op jit(solution)/shard_map/ppermute | solution.py:18
  78.6 4.1 %collective-permute-start.11 = (bf16[2,768,128]{2,1,0:T(8,128)(2,1)}, bf16[2,768,128]{2,1,0:T(8,128)(2,1)S(1)}, u32[]{:S(2)}, u32[]{:S(2)}) collective-permute-start(bf16[2,768,128]{2,1,0:T(8,128)(2,1)} %get-tuple-element.20), channel_id=1, source_target_pairs={{0,4},{4,0},{1,5},{5,1},{2,6},{6,2},{3,7},{7,3},{8,12},{12,8},{9,1... | collective-permute-start | bytes 1179656 | tf_op jit(solution)/shard_map/ppermute | solution.py:18
  79.9 0.8 copy-start.10
  82.6 10.6 %collective-permute-start.13 = (bf16[2,768,128]{2,1,0:T(8,128)(2,1)}, bf16[2,768,128]{2,1,0:T(8,128)(2,1)S(1)}, u32[]{:S(2)}, u32[]{:S(2)}) collective-permute-start(bf16[2,768,128]{2,1,0:T(8,128)(2,1)} %sum_cores.1), channel_id=1, source_target_pairs={{0,1},{1,0},{2,3},{3,2},{4,5},{5,4},{6,7},{7,6},{8,9},{9,8},{10,11... | collective-permute-start | bytes 1179656 | tf_op jit(solution)/shard_map/ppermute | solution.py:22
  82.6 10.6 %copy-start.8 = (bf16[2,768,128]{2,1,0:T(8,128)(2,1)}, bf16[2,768,128]{2,1,0:T(8,128)(2,1)S(1)}, u32[]{:S(2)}) copy-start(bf16[2,768,128]{2,1,0:T(8,128)(2,1)S(1)} %collective-permute-done.11.oth) | copy-start | bytes 1179652
  93.3 0.8 copy-start.9
  96.2 12.0 %collective-permute-start.14 = (bf16[768,128]{1,0:T(8,128)(2,1)}, bf16[768,128]{1,0:T(8,128)(2,1)S(1)}, u32[]{:S(2)}, u32[]{:S(2)}) collective-permute-start(bf16[768,128]{1,0:T(8,128)(2,1)} %get-tuple-element.24.after), channel_id=1, source_target_pairs={{0,2},{1,3},{2,0},{3,1},{4,6},{5,7},{6,4},{7,5},{8,10},{9,11},{10,... | collective-permute-start | bytes 589832 | tf_op jit(solution)/shard_map/ppermute | solution.py:22
  99.4 12.7 %all-to-all-start.2 = ((bf16[8,4,8,128]{3,2,1,0:T(8,128)(2,1)}), bf16[8,4,8,128]{3,2,1,0:T(8,128)(2,1)S(1)}, u32[]{:S(2)}, u32[]{:S(2)}) async-start(bf16[8,4,8,128]{3,2,1,0:T(8,128)(2,1)} %bitcast.27), calls=%async_computation.2 | async-start | bytes 131072 | tf_op jit(solution)/shard_map/all_to_all | solution.py:370
  108.3 0.7 copy-start.15

commit v6 on v5

--- a/solution.py
+++ b/solution.py
@@ -205,15 +205,6 @@
         part[k, :, cols:] = tail
 
 
-def sum_kernel(own, oth, out):
-    out[...] = (own[...].astype(F32) + oth[...].astype(F32)).astype(BF)
-
-
-def halve_kernel(own_near, own_far, oth, got, near, far):
-    near[...] = own_near[...] + oth[0].astype(F32) + got[0].astype(F32)
-    far[...] = (own_far[...] + oth[1].astype(F32) + got[1].astype(F32)).astype(BF)
-
-
 def plane_kernel(pos, parts, after, out):
     rows = out.shape[-1]
     each = out.shape[-2]
@@ -339,22 +330,10 @@
         name="attention",
     )(pos, *operands)
 
-    go = pl.pallas_call(
-        sum_kernel,
-        out_shape=jax.ShapeDtypeStruct((2, width, rows), BF),
-        in_specs=[vmem, vmem],
-        out_specs=vmem,
-        compiler_params=room,
-        name="sum_cores",
-    )(own_go, shift(oth_go, "core", NC, 1))
-    near, far = pl.pallas_call(
-        halve_kernel,
-        out_shape=(jax.ShapeDtypeStruct((width, rows), F32), jax.ShapeDtypeStruct((width, rows), BF)),
-        in_specs=[vmem] * 4,
-        out_specs=(vmem, vmem),
-        compiler_params=room,
-        name="sum_pair",
-    )(own_near_out, own_far_out, shift(oth_keep, "core", NC, 1), swap(go, 1))
+    go = (own_go.astype(F32) + shift(oth_go, "core", NC, 1).astype(F32)).astype(BF)
+    keep, got = shift(oth_keep, "core", NC, 1), swap(go, 1)
+    near = own_near_out + keep[0].astype(F32) + got[0].astype(F32)
+    far = (own_far_out + keep[1].astype(F32) + got[1].astype(F32)).astype(BF)
     back = swap(far, 2)
 
     parts = lax.all_to_all(out_bias, ("x", "y"), 0, 0, tiled=True)

time: 113 us -> 111 us (0.982)
  Pallas kernels: 27.5 us -> 23.3 us
  waiting for transfers between devices: 36.2 us -> 37.8 us
  local copies, waits for them, and re-layouts: 7.97 us -> 6.61 us
    ppermute x6, waiting for transfers between devices: 28.2 us -> 23.9 us  [swap(): return lax.ppermute(value, ('th', 'tl'), [(i, i ^ by) for i in range(NT)])]
    pallas_call x2 -> x0, Pallas kernels: 4.16 us -> none  [the longest x1 2.21 us: on_device(): pl.pallas_call(halve_kernel, out_shape=(jax.ShapeDtypeStruct((width, rows...]
    all_to_all x1, waiting for transfers between devices: 0.83 us -> 4.25 us  [on_device(): lax.all_to_all(planes.reshape((-1,) + shape[3:]), ('zh', 'core', 'tl'), 0...]
    all_to_all x1, waiting for transfers between devices: 0.01 us -> 2.62 us  [on_device(): parts = lax.all_to_all(out_bias, ('x', 'y'), 0, 0, tiled=True)]
    unnamed x42 -> x44, local copies, waits for them, and re-layouts: 4.5 us -> 3.07 us
    all_to_all x1, starting transfers between devices: 6.8 us -> 5.42 us  [on_device(): parts = lax.all_to_all(out_bias, ('x', 'y'), 0, 0, tiled=True)]
    ppermute x8, starting transfers between devices: 5.38 us -> 6.64 us  [shift(): lax.ppermute(value, axis, [(i, (i + by) % count) for i in range(count)])]
  transfers between devices with their start and end apart: 18 -> 18, of which waited for: 8 -> 8; matrix products, arithmetic and copies ran while one was open for 3% -> 4% of each run, Pallas kernels for 9% -> 6%
where the time goes in v6:
time: 111 us
  starting transfers between devices  40.4 us (36%)
  waiting for transfers between devices  37.8 us (34%)
  Pallas kernels  23.3 us (21%)
  local copies, waits for them, and re-layouts  6.61 us (6%)
  other arithmetic  1.56 us (1%)
    ppermute x6, waiting for transfers between devices, swap(): return lax.ppermute(value, ('th', 'tl'), [(i, i ^ by) for i in range(NT)])  23.9 us
    pallas_call x1, Pallas kernels, on_device(): pl.pallas_call(attention_kernel, out_shape=(jax.ShapeDtypeStruct((width,...  12.6 us
    ppermute x1, starting transfers between devices, on_device(): lax.ppermute(send, ('zh', 'core'), [(0, 3), (3, 0), (1, 2), (2, 1)])  7.82 us
    ppermute x6, starting transfers between devices, swap(): return lax.ppermute(value, ('th', 'tl'), [(i, i ^ by) for i in range(NT)])  7.35 us
    ppermute x8, waiting for transfers between devices, shift(): lax.ppermute(value, axis, [(i, (i + by) % count) for i in range(count)])  6.98 us
    all_to_all x1, starting transfers between devices, on_device(): weights = lax.all_to_all(pieces, ('x', 'y'), 0, 0, tiled=True)  6.94 us
    ppermute x8, starting transfers between devices, shift(): lax.ppermute(value, axis, [(i, (i + by) % count) for i in range(count)])  6.64 us
    all_to_all x1, starting transfers between devices, on_device(): lax.all_to_all(planes.reshape((-1,) + shape[3:]), ('zh', 'core', 'tl'), 0...  6.24 us
  transfers between devices with their start and end apart: 18, of which 8 were waited for; matrix products, arithmetic and copies ran while one was open for 4% of the time, Pallas kernels for 6%

profile of v6, /device:TPU:1, one launch (start us, length us, event | category | flops | bytes accessed | tf_op | source)
XLA Modules:
  0.0 110.5 jit_solution(1848800545120026662)
XLA Ops:
  0.6 1.8 %norm.1.normed = bf16[128,768]{1,0:T(8,128)(2,1)} custom-call(bf16[128,768]{1,0:T(8,128)(2,1)} %bitcast.44, f32[768]{0:T(1024)} %gain.3), custom_call_target="tpu_custom_call" | custom-call | tf_op jit(solution)/shard_map/norm/pallas_call | solution.py:274
  2.5 2.5 %collective-permute-start.3 = (bf16[128,768]{1,0:T(8,128)(2,1)}, bf16[128,768]{1,0:T(8,128)(2,1)S(1)}, u32[]{:S(2)}, u32[]{:S(2)}) collective-permute-start(bf16[128,768]{1,0:T(8,128)(2,1)} %norm.1.normed), channel_id=1, source_target_pairs={{0,1},{1,0},{2,3},{3,2},{4,5},{5,4},{6,7},{7,6},{8,9},{9,8},{10,11... | collective-permute-start | bytes 589832 | tf_op jit(solution)/shard_map/ppermute | solution.py:22
  4.9 0.0 collective-permute-start.4
  5.0 0.7 stack.27.pos
  5.6 2.0 %pack.1 = (bf16[12,1536]{1,0:T(8,128)(2,1)}, bf16[12,1536]{1,0:T(8,128)(2,1)}) custom-call(s32[6]{0:T(128)} %stack.27.pos, bf16[12,768]{1,0:T(8,128)(2,1)} %query.1, bf16[12,768]{1,0:T(8,128)(2,1)} %key.1, bf16[12,768]{1,0:T(8,128)(2,1)} %value.1, bf16[12,768]{1,0:T(8,128)(2,1)} %gate.1, bf16[12,768]{1,0:T(8,128)(2,1)} %out.1), custom_call_target="tpu_custom_call" | custom-call | tf_op jit(solution)/shard_map/pack/pallas_call | solution.py:263
  7.7 7.8 %collective-permute-start.2 = (bf16[12,1536]{1,0:T(8,128)(2,1)}, bf16[12,1536]{1,0:T(8,128)(2,1)S(1)}, u32[]{:S(2)}, u32[]{:S(2)}) collective-permute-start(bf16[12,1536]{1,0:T(8,128)(2,1)} %get-tuple-element.13), channel_id=1, source_target_pairs={{0,36},{36,0},{4,32},{32,4},{1,37},{37,1},{5,33},{33,5},{2,38},{38... | collective-permute-start | bytes 110600 | tf_op jit(solution)/shard_map/ppermute | solution.py:272
  15.5 0.0 collective-permute-start
  15.5 0.2 collective-permute-start.1
  15.7 2.2 %dynamic-slice_bitcast_fusion = (bf16[4,128,512]{2,1,0:T(8,128)(2,1)}, bf16[4,128,512]{2,1,0:T(8,128)(2,1)}) fusion(bf16[4,2,2,128,512]{4,3,2,1,0:T(8,128)(2,1)} %bitcast.46, s32[]{:T(128)S(6)} %select_n.18, s32[]{:T(128)S(6)} %select_n.22, s32[]{:T(128)S(6)} %select_n.20), kind=kLoop, calls=%fused_computation.1 | loop fusion | bytes 2097164 | tf_op jit(solution)/shard_map/jit(dynamic_index_in_dim)/squeeze | solution.py:260
  18.0 5.0 %collective-permute-done.1.above = bf16[12,1536]{1,0:T(8,128)(2,1)S(1)} collective-permute-done((bf16[12,1536]{1,0:T(8,128)(2,1)}, bf16[12,1536]{1,0:T(8,128)(2,1)S(1)}, u32[]{:S(2)}, u32[]{:S(2)}) %collective-permute-start.1) | collective-permute-done | bytes 36896 | tf_op jit(solution)/shard_map/ppermute | solution.py:18
  23.0 0.5 copy-done.19
  23.6 0.0 copy-done.17
  23.6 0.0 copy-done.18
  23.6 0.1 copy-done.15
  23.7 0.1 copy-done.1
  23.8 2.5 %assemble.1 = (bf16[16,48,1152]{2,1,0:T(8,128)(2,1)}, bf16[256,768]{1,0:T(8,128)(2,1)}) custom-call(s32[6]{0:T(128)} %stack.27.pos, bf16[12,1536]{1,0:T(8,128)(2,1)} %get-tuple-element.12.mine, bf16[12,1536]{1,0:T(8,128)(2,1)} %copy-done.18, bf16[12,1536]{1,0:T(8,128)(2,1)} %copy-done.19, bf16[12,1536]{1,0:T(8,128)(2,1)} %copy-done.17, ...), custom_call_target="tpu_custom_call" | custom-call | tf_op jit(solution)/shard_map/assemble/pallas_call | solution.py:284
  26.3 0.0 copy-start.12
  26.3 0.0 copy-start.20
  26.4 6.9 %all-to-all-start = ((bf16[16,48,1152]{2,1,0:T(8,128)(2,1)}), bf16[16,48,1152]{2,1,0:T(8,128)(2,1)}, u32[]{:S(2)}, u32[]{:S(2)}) async-start(bf16[16,48,1152]{2,1,0:T(8,128)(2,1)} %get-tuple-element.15), calls=%async_computation | async-start | bytes 3538944 | tf_op jit(solution)/shard_map/all_to_all | solution.py:296
  33.3 0.9 collective-permute-start.5
  34.3 2.7 %collective-permute-start.10 = (bf16[4,128,512]{2,1,0:T(8,128)(2,1)S(1)}, bf16[4,128,512]{2,1,0:T(8,128)(2,1)S(1)}, u32[]{:S(2)}, u32[]{:S(2)}) collective-permute-start(bf16[4,128,512]{2,1,0:T(8,128)(2,1)S(1)} %copy-done), channel_id=1, source_target_pairs={{0,1},{1,0},{2,3},{3,2},{4,5},{5,4},{6,7},{7,6},{8,9},{9,8},{10,11... | collective-permute-start | bytes 1572872 | tf_op jit(solution)/shard_map/ppermute | solution.py:22
  36.9 1.7 %collective-permute-start.6 = (bf16[256,768]{1,0:T(8,128)(2,1)S(1)}, bf16[256,768]{1,0:T(8,128)(2,1)S(1)}, u32[]{:S(2)}, u32[]{:S(2)}) collective-permute-start(bf16[256,768]{1,0:T(8,128)(2,1)S(1)} %copy-done.5), channel_id=1, source_target_pairs={{0,4},{4,0},{1,5},{5,1},{2,6},{6,2},{3,7},{7,3},{8,12},{12,8},{9,1... | collective-permute-start | bytes 1179656 | tf_op jit(solution)/shard_map/ppermute | solution.py:18
  38.6 14.3 %collective-permute-done.5.own_far = bf16[256,768]{1,0:T(8,128)(2,1)S(1)} collective-permute-done((bf16[256,768]{1,0:T(8,128)(2,1)S(1)}, bf16[256,768]{1,0:T(8,128)(2,1)S(1)}, u32[]{:S(2)}, u32[]{:S(2)}) %collective-permute-start.5) | collective-permute-done | bytes 393248 | tf_op jit(solution)/shard_map/ppermute | solution.py:22
  52.9 1.5 %collective-permute-start.7 = (bf16[256,768]{1,0:T(8,128)(2,1)S(1)}, bf16[256,768]{1,0:T(8,128)(2,1)S(1)}, u32[]{:S(2)}, u32[]{:S(2)}) collective-permute-start(bf16[256,768]{1,0:T(8,128)(2,1)S(1)} %collective-permute-done.5.own_far), channel_id=1, source_target_pairs={{0,4},{4,0},{1,5},{5,1},{2,6},{6,2},{3,7},{7,3},{8,12},{12,8},{9,1... | collective-permute-start | bytes 1179656 | tf_op jit(solution)/shard_map/ppermute | solution.py:18
  54.4 0.1 collective-permute-start.8
  54.5 0.4 collective-permute-start.9
  54.9 0.6 compare_convert_fusion
  55.5 0.5 collective-permute-done.8.cot_oth0
  56.0 0.3 collective-permute-done.9.cot_oth1
  56.3 0.8 copy-done.7
  57.2 0.7 copy-done.8
  57.9 12.6 %attention.1 = (f32[768,128]{1,0:T(8,128)}, f32[768,128]{1,0:T(8,128)}, bf16[2,768,128]{2,1,0:T(8,128)(2,1)}, bf16[2,768,128]{2,1,0:T(8,128)(2,1)}, bf16[2,768,1...) custom-call(s32[6]{0:T(128)} %stack.27.pos, bf16[256,768]{1,0:T(8,128)(2,1)} %get-tuple-element.14.own_near, ...), custom_call_target="tpu_custom_call" | custom-call | tf_op jit(solution)/shard_map/attention/pallas_call | solution.py:304
  70.6 2.2 %collective-permute-start.12 = (bf16[2,768,128]{2,1,0:T(8,128)(2,1)}, bf16[2,768,128]{2,1,0:T(8,128)(2,1)S(1)}, u32[]{:S(2)}, u32[]{:S(2)}) collective-permute-start(bf16[2,768,128]{2,1,0:T(8,128)(2,1)} %get-tuple-element.19), channel_id=1, source_target_pairs={{0,4},{4,0},{1,5},{5,1},{2,6},{6,2},{3,7},{7,3},{8,12},{12,8},{9,1... | collective-permute-start | bytes 1179656 | tf_op jit(solution)/shard_map/ppermute | solution.py:18
  72.8 5.4 %all-to-all-start.1 = ((bf16[16,4,2,16,256]{4,3,2,1,0:T(8,128)(2,1)}), bf16[16,4,2,16,256]{4,3,2,1,0:T(8,128)(2,1)}, u32[]{:S(2)}, u32[]{:S(2)}) async-start(bf16[16,4,2,16,256]{4,3,2,1,0:T(8,128)(2,1)} %get-tuple-element.21), calls=%async_computation.1 | async-start | bytes 2097152 | tf_op jit(solution)/shard_map/all_to_all | solution.py:339
  78.2 0.5 collective-permute-start.11
  78.8 0.1 add_convert_fusion
  78.9 0.1 collective-permute-start.13
  79.0 1.1 %collective-permute-done.11 = bf16[2,768,128]{2,1,0:T(8,128)(2,1)S(1)} collective-permute-done((bf16[2,768,128]{2,1,0:T(8,128)(2,1)S(1)}, bf16[2,768,128]{2,1,0:T(8,128)(2,1)S(1)}, u32[]{:S(2)}, u32[]{:S(2)}) %collective-permute-start.11) | collective-permute-done | bytes 393248 | tf_op jit(solution)/shard_map/ppermute | solution.py:18
  80.1 9.6 %collective-permute-done.13 = bf16[2,768,128]{2,1,0:T(8,128)(2,1)S(1)} collective-permute-done((bf16[2,768,128]{2,1,0:T(8,128)(2,1)S(1)}, bf16[2,768,128]{2,1,0:T(8,128)(2,1)S(1)}, u32[]{:S(2)}, u32[]{:S(2)}) %collective-permute-start.13) | collective-permute-done | bytes 393248 | tf_op jit(solution)/shard_map/ppermute | solution.py:22
  89.7 0.9 fusion
  90.6 1.2 %collective-permute-start.14 = (bf16[768,128]{1,0:T(8,128)(2,1)S(1)}, bf16[768,128]{1,0:T(8,128)(2,1)S(1)}, u32[]{:S(2)}, u32[]{:S(2)}) collective-permute-start(bf16[768,128]{1,0:T(8,128)(2,1)S(1)} %get-tuple-element.24.after), channel_id=1, source_target_pairs={{0,2},{1,3},{2,0},{3,1},{4,6},{5,7},{6,4},{7,5},{8,10},{9,11},{10,... | collective-permute-start | bytes 589832 | tf_op jit(solution)/shard_map/ppermute | solution.py:22
  91.8 2.6 %all-to-all-done.1.parts = bf16[16,4,2,16,256]{4,3,2,1,0:T(8,128)(2,1)} async-done(((bf16[16,4,2,16,256]{4,3,2,1,0:T(8,128)(2,1)}), bf16[16,4,2,16,256]{4,3,2,1,0:T(8,128)(2,1)}, u32[]{:S(2)}, u32[]{:S(2)}) %all-to-all-start.1) | async-done | bytes 1048608 | tf_op jit(solution)/shard_map/all_to_all | solution.py:339
  94.4 2.0 %sum_plane.1 = bf16[2,2,2,4,8,128]{5,4,3,2,1,0:T(8,128)(2,1)} custom-call(s32[6]{0:T(128)} %stack.27.pos, bf16[16,4,2,16,256]{4,3,2,1,0:T(8,128)(2,1)} %all-to-all-done.1.parts, bf16[768,128]{1,0:T(8,128)(2,1)} %copy-done.3), custom_call_target="tpu_custom_call" | custom-call | tf_op jit(solution)/shard_map/sum_plane/pallas_call | solution.py:340
  96.4 6.2 %all-to-all-start.2 = ((bf16[8,4,8,128]{3,2,1,0:T(8,128)(2,1)}), bf16[8,4,8,128]{3,2,1,0:T(8,128)(2,1)S(1)}, u32[]{:S(2)}, u32[]{:S(2)}) async-start(bf16[8,4,8,128]{3,2,1,0:T(8,128)(2,1)} %bitcast.47), calls=%async_computation.2 | async-start | bytes 131072 | tf_op jit(solution)/shard_map/all_to_all | solution.py:349
  102.7 0.7 copy-done.16
  103.3 2.3 %norm_back.1 = bf16[128,768]{1,0:T(8,128)(2,1)} custom-call(bf16[128,768]{1,0:T(8,128)(2,1)} %bitcast.45, f32[768]{0:T(1024)} %gain.3, f32[768,128]{1,0:T(8,128)} %get-tuple-element.25.near, bf16[768,128]{1,0:T(8,128)(2,1)} %copy-done.16), custom_call_target="tpu_custom_call" | custom-call | tf_op jit(solution)/shard_map/norm_back/pallas_call | solution.py:353
  105.6 4.2 %all-to-all-done.2 = bf16[8,4,8,128]{3,2,1,0:T(8,128)(2,1)S(1)} async-done(((bf16[8,4,8,128]{3,2,1,0:T(8,128)(2,1)}), bf16[8,4,8,128]{3,2,1,0:T(8,128)(2,1)S(1)}, u32[]{:S(2)}, u32[]{:S(2)}) %all-to-all-start.2) | async-done | bytes 65568 | tf_op jit(solution)/shard_map/all_to_all | solution.py:349
  109.9 0.6 copy.18
  (45 shorter events, 0.1 us)
Async XLA Ops:
  2.5 20.5 %collective-permute-start.3 = (bf16[128,768]{1,0:T(8,128)(2,1)}, bf16[128,768]{1,0:T(8,128)(2,1)S(1)}, u32[]{:S(2)}, u32[]{:S(2)}) collective-permute-start(bf16[128,768]{1,0:T(8,128)(2,1)} %norm.1.normed), channel_id=1, source_target_pairs={{0,1},{1,0},{2,3},{3,2},{4,5},{5,4},{6,7},{7,6},{8,9},{9,8},{10,11... | collective-permute-start | bytes 589832 | tf_op jit(solution)/shard_map/ppermute | solution.py:22
  4.9 18.1 %collective-permute-start.4 = (bf16[128,768]{1,0:T(8,128)(2,1)}, bf16[128,768]{1,0:T(8,128)(2,1)S(1)}, u32[]{:S(2)}, u32[]{:S(2)}) collective-permute-start(bf16[128,768]{1,0:T(8,128)(2,1)} %bitcast.50), channel_id=1, source_target_pairs={{0,1},{1,0},{2,3},{3,2},{4,5},{5,4},{6,7},{7,6},{8,9},{9,8},{10,11... | collective-permute-start | bytes 589832 | tf_op jit(solution)/shard_map/ppermute | solution.py:22
  7.7 15.3 %collective-permute-start.2 = (bf16[12,1536]{1,0:T(8,128)(2,1)}, bf16[12,1536]{1,0:T(8,128)(2,1)S(1)}, u32[]{:S(2)}, u32[]{:S(2)}) collective-permute-start(bf16[12,1536]{1,0:T(8,128)(2,1)} %get-tuple-element.13), channel_id=1, source_target_pairs={{0,36},{36,0},{4,32},{32,4},{1,37},{37,1},{5,33},{33,5},{2,38},{38... | collective-permute-start | bytes 110600 | tf_op jit(solution)/shard_map/ppermute | solution.py:272
  15.5 7.5 %collective-permute-start = (bf16[12,1536]{1,0:T(8,128)(2,1)}, bf16[12,1536]{1,0:T(8,128)(2,1)S(1)}, u32[]{:S(2)}, u32[]{:S(2)}) collective-permute-start(bf16[12,1536]{1,0:T(8,128)(2,1)} %get-tuple-element.13), channel_id=1, source_target_pairs={{0,4},{4,0},{1,5},{5,1},{2,6},{6,2},{3,7},{7,3},{8,12},{12,8},{9,1... | collective-permute-start | bytes 110600 | tf_op jit(solution)/shard_map/ppermute | solution.py:18
  15.5 7.5 %collective-permute-start.1 = (bf16[12,1536]{1,0:T(8,128)(2,1)}, bf16[12,1536]{1,0:T(8,128)(2,1)S(1)}, u32[]{:S(2)}, u32[]{:S(2)}) collective-permute-start(bf16[12,1536]{1,0:T(8,128)(2,1)} %get-tuple-element.12.mine), channel_id=1, source_target_pairs={{0,32},{32,0},{1,33},{33,1},{2,34},{34,2},{3,35},{35,3},{4,36},{36... | collective-permute-start | bytes 110600 | tf_op jit(solution)/shard_map/ppermute | solution.py:18
  23.0 0.6 copy-start.19
  23.0 0.6 copy-start.17
  23.0 0.6 copy-start.18
  23.0 0.7 copy-start.15
  23.0 0.8 copy-start.1
  26.3 7.0 %copy-start.5 = (bf16[256,768]{1,0:T(8,128)(2,1)S(1)}, bf16[256,768]{1,0:T(8,128)(2,1)}, u32[]{:S(2)}) copy-start(bf16[256,768]{1,0:T(8,128)(2,1)} %get-tuple-element.14.own_near) | copy-start | bytes 1179652
  26.3 7.9 %copy-start = (bf16[4,128,512]{2,1,0:T(8,128)(2,1)S(1)}, bf16[4,128,512]{2,1,0:T(8,128)(2,1)}, u32[]{:S(2)}) copy-start(bf16[4,128,512]{2,1,0:T(8,128)(2,1)} %get-tuple-element.23.ready) | copy-start | bytes 1572868
  26.3 28.1 %copy-start.12 = (bf16[1,128,768]{2,1,0:T(8,128)(2,1)S(1)}, bf16[1,128,768]{2,1,0:T(8,128)(2,1)}, u32[]{:S(2)}) copy-start(bf16[1,128,768]{2,1,0:T(8,128)(2,1)} %param.11) | copy-start | bytes 589828
  26.3 28.1 %copy-start.2 = (bf16[128,768]{1,0:T(8,128)(2,1)S(1)}, bf16[128,768]{1,0:T(8,128)(2,1)}, u32[]{:S(2)}) copy-start(bf16[128,768]{1,0:T(8,128)(2,1)} %copy-done.1) | copy-start | bytes 589828
  26.3 28.5 %copy-start.20 = (s32[512]{0:T(512)S(1)}, s32[512]{0:T(512)}, u32[]{:S(2)}) copy-start(s32[512]{0:T(512)} %param.19) | copy-start | bytes 6148
  26.4 30.8 %all-to-all-start = ((bf16[16,48,1152]{2,1,0:T(8,128)(2,1)}), bf16[16,48,1152]{2,1,0:T(8,128)(2,1)}, u32[]{:S(2)}, u32[]{:S(2)}) async-start(bf16[16,48,1152]{2,1,0:T(8,128)(2,1)} %get-tuple-element.15), calls=%async_computation | async-start | bytes 3538944 | tf_op jit(solution)/shard_map/all_to_all | solution.py:296
  33.3 19.6 %collective-permute-start.5 = (bf16[256,768]{1,0:T(8,128)(2,1)S(1)}, bf16[256,768]{1,0:T(8,128)(2,1)S(1)}, u32[]{:S(2)}, u32[]{:S(2)}) collective-permute-start(bf16[256,768]{1,0:T(8,128)(2,1)S(1)} %copy-done.5), channel_id=1, source_target_pairs={{0,2},{1,3},{2,0},{3,1},{4,6},{5,7},{6,4},{7,5},{8,10},{9,11},{10,... | collective-permute-start | bytes 1179656 | tf_op jit(solution)/shard_map/ppermute | solution.py:22
  34.3 22.0 %collective-permute-start.10 = (bf16[4,128,512]{2,1,0:T(8,128)(2,1)S(1)}, bf16[4,128,512]{2,1,0:T(8,128)(2,1)S(1)}, u32[]{:S(2)}, u32[]{:S(2)}) collective-permute-start(bf16[4,128,512]{2,1,0:T(8,128)(2,1)S(1)} %copy-done), channel_id=1, source_target_pairs={{0,1},{1,0},{2,3},{3,2},{4,5},{5,4},{6,7},{7,6},{8,9},{9,8},{10,11... | collective-permute-start | bytes 1572872 | tf_op jit(solution)/shard_map/ppermute | solution.py:22
  36.9 19.4 %collective-permute-start.6 = (bf16[256,768]{1,0:T(8,128)(2,1)S(1)}, bf16[256,768]{1,0:T(8,128)(2,1)S(1)}, u32[]{:S(2)}, u32[]{:S(2)}) collective-permute-start(bf16[256,768]{1,0:T(8,128)(2,1)S(1)} %copy-done.5), channel_id=1, source_target_pairs={{0,4},{4,0},{1,5},{5,1},{2,6},{6,2},{3,7},{7,3},{8,12},{12,8},{9,1... | collective-permute-start | bytes 1179656 | tf_op jit(solution)/shard_map/ppermute | solution.py:18
  52.9 3.4 %copy-start.6 = (bf16[256,768]{1,0:T(8,128)(2,1)}, bf16[256,768]{1,0:T(8,128)(2,1)S(1)}, u32[]{:S(2)}) copy-start(bf16[256,768]{1,0:T(8,128)(2,1)S(1)} %collective-permute-done.5.own_far) | copy-start | bytes 1179652
  52.9 3.4 %collective-permute-start.7 = (bf16[256,768]{1,0:T(8,128)(2,1)S(1)}, bf16[256,768]{1,0:T(8,128)(2,1)S(1)}, u32[]{:S(2)}, u32[]{:S(2)}) collective-permute-start(bf16[256,768]{1,0:T(8,128)(2,1)S(1)} %collective-permute-done.5.own_far), channel_id=1, source_target_pairs={{0,4},{4,0},{1,5},{5,1},{2,6},{6,2},{3,7},{7,3},{8,12},{12,8},{9,1... | collective-permute-start | bytes 1179656 | tf_op jit(solution)/shard_map/ppermute | solution.py:18
  54.4 1.6 %collective-permute-start.8 = (bf16[128,768]{1,0:T(8,128)(2,1)S(1)}, bf16[128,768]{1,0:T(8,128)(2,1)S(1)}, u32[]{:S(2)}, u32[]{:S(2)}) collective-permute-start(bf16[128,768]{1,0:T(8,128)(2,1)S(1)} %bitcast.52), channel_id=1, source_target_pairs={{0,4},{4,0},{1,5},{5,1},{2,6},{6,2},{3,7},{7,3},{8,12},{12,8},{9,1... | collective-permute-start | bytes 589832 | tf_op jit(solution)/shard_map/ppermute | solution.py:18
  54.5 1.8 %collective-permute-start.9 = (bf16[128,768]{1,0:T(8,128)(2,1)S(1)}, bf16[128,768]{1,0:T(8,128)(2,1)S(1)}, u32[]{:S(2)}, u32[]{:S(2)}) collective-permute-start(bf16[128,768]{1,0:T(8,128)(2,1)S(1)} %copy-done.2), channel_id=1, source_target_pairs={{0,4},{4,0},{1,5},{5,1},{2,6},{6,2},{3,7},{7,3},{8,12},{12,8},{9,1... | collective-permute-start | bytes 589832 | tf_op jit(solution)/shard_map/ppermute | solution.py:18
  56.0 1.9 %copy-start.13 = (bf16[128,768]{1,0:T(8,128)(2,1)}, bf16[128,768]{1,0:T(8,128)(2,1)S(1)}, u32[]{:S(2)}) copy-start(bf16[128,768]{1,0:T(8,128)(2,1)S(1)} %collective-permute-done.8.cot_oth0) | copy-start | bytes 589828
  56.3 1.6 %copy-start.14 = (bf16[128,768]{1,0:T(8,128)(2,1)}, bf16[128,768]{1,0:T(8,128)(2,1)S(1)}, u32[]{:S(2)}) copy-start(bf16[128,768]{1,0:T(8,128)(2,1)S(1)} %collective-permute-done.9.cot_oth1) | copy-start | bytes 589828
  56.3 1.6 %copy-start.4 = (bf16[4,128,512]{2,1,0:T(8,128)(2,1)}, bf16[4,128,512]{2,1,0:T(8,128)(2,1)S(1)}, u32[]{:S(2)}) copy-start(bf16[4,128,512]{2,1,0:T(8,128)(2,1)S(1)} %collective-permute-done.10.bias_pair) | copy-start | bytes 1572868
  56.3 0.9 copy-start.7
  57.2 0.7 copy-start.8
  70.5 7.7 %copy-start.21 = (bf16[2,768,128]{2,1,0:T(8,128)(2,1)S(1)}, bf16[2,768,128]{2,1,0:T(8,128)(2,1)}, u32[]{:S(2)}) copy-start(bf16[2,768,128]{2,1,0:T(8,128)(2,1)} %get-tuple-element.17) | copy-start | bytes 1179652
  70.5 8.2 %copy-start.9 = (bf16[2,768,128]{2,1,0:T(8,128)(2,1)S(1)}, bf16[2,768,128]{2,1,0:T(8,128)(2,1)}, u32[]{:S(2)}) copy-start(bf16[2,768,128]{2,1,0:T(8,128)(2,1)} %get-tuple-element.18) | copy-start | bytes 1179652
  70.5 19.2 %copy-start.10 = (f32[768,128]{1,0:T(8,128)S(1)}, f32[768,128]{1,0:T(8,128)}, u32[]{:S(2)}) copy-start(f32[768,128]{1,0:T(8,128)} %get-tuple-element.16) | copy-start | bytes 1179652
  70.6 19.2 %copy-start.11 = (f32[768,128]{1,0:T(8,128)S(1)}, f32[768,128]{1,0:T(8,128)}, u32[]{:S(2)}) copy-start(f32[768,128]{1,0:T(8,128)} %get-tuple-element.20) | copy-start | bytes 1179652
  70.6 8.2 %collective-permute-start.12 = (bf16[2,768,128]{2,1,0:T(8,128)(2,1)}, bf16[2,768,128]{2,1,0:T(8,128)(2,1)S(1)}, u32[]{:S(2)}, u32[]{:S(2)}) collective-permute-start(bf16[2,768,128]{2,1,0:T(8,128)(2,1)} %get-tuple-element.19), channel_id=1, source_target_pairs={{0,4},{4,0},{1,5},{5,1},{2,6},{6,2},{3,7},{7,3},{8,12},{12,8},{9,1... | collective-permute-start | bytes 1179656 | tf_op jit(solution)/shard_map/ppermute | solution.py:18
  72.8 21.6 %all-to-all-start.1 = ((bf16[16,4,2,16,256]{4,3,2,1,0:T(8,128)(2,1)}), bf16[16,4,2,16,256]{4,3,2,1,0:T(8,128)(2,1)}, u32[]{:S(2)}, u32[]{:S(2)}) async-start(bf16[16,4,2,16,256]{4,3,2,1,0:T(8,128)(2,1)} %get-tuple-element.21), calls=%async_computation.1 | async-start | bytes 2097152 | tf_op jit(solution)/shard_map/all_to_all | solution.py:339
  78.2 1.9 %collective-permute-start.11 = (bf16[2,768,128]{2,1,0:T(8,128)(2,1)S(1)}, bf16[2,768,128]{2,1,0:T(8,128)(2,1)S(1)}, u32[]{:S(2)}, u32[]{:S(2)}) collective-permute-start(bf16[2,768,128]{2,1,0:T(8,128)(2,1)S(1)} %copy-done.21), channel_id=1, source_target_pairs={{0,4},{4,0},{1,5},{5,1},{2,6},{6,2},{3,7},{7,3},{8,12},{12,8},{9,1... | collective-permute-start | bytes 1179656 | tf_op jit(solution)/shard_map/ppermute | solution.py:18
  78.9 10.9 %collective-permute-start.13 = (bf16[2,768,128]{2,1,0:T(8,128)(2,1)S(1)}, bf16[2,768,128]{2,1,0:T(8,128)(2,1)S(1)}, u32[]{:S(2)}, u32[]{:S(2)}) collective-permute-start(bf16[2,768,128]{2,1,0:T(8,128)(2,1)S(1)} %add_convert_fusion), channel_id=1, source_target_pairs={{0,1},{1,0},{2,3},{3,2},{4,5},{5,4},{6,7},{7,6},{8,9},{9,8},{10,11... | collective-permute-start | bytes 1179656 | tf_op jit(solution)/shard_map/ppermute | solution.py:22
  90.6 3.8 %copy-start.3 = (bf16[768,128]{1,0:T(8,128)(2,1)}, bf16[768,128]{1,0:T(8,128)(2,1)S(1)}, u32[]{:S(2)}) copy-start(bf16[768,128]{1,0:T(8,128)(2,1)S(1)} %get-tuple-element.24.after) | copy-start | bytes 589828
  90.6 12.0 %collective-permute-start.14 = (bf16[768,128]{1,0:T(8,128)(2,1)S(1)}, bf16[768,128]{1,0:T(8,128)(2,1)S(1)}, u32[]{:S(2)}, u32[]{:S(2)}) collective-permute-start(bf16[768,128]{1,0:T(8,128)(2,1)S(1)} %get-tuple-element.24.after), channel_id=1, source_target_pairs={{0,2},{1,3},{2,0},{3,1},{4,6},{5,7},{6,4},{7,5},{8,10},{9,11},{10,... | collective-permute-start | bytes 589832 | tf_op jit(solution)/shard_map/ppermute | solution.py:22
  96.4 13.5 %all-to-all-start.2 = ((bf16[8,4,8,128]{3,2,1,0:T(8,128)(2,1)}), bf16[8,4,8,128]{3,2,1,0:T(8,128)(2,1)S(1)}, u32[]{:S(2)}, u32[]{:S(2)}) async-start(bf16[8,4,8,128]{3,2,1,0:T(8,128)(2,1)} %bitcast.47), calls=%async_computation.2 | async-start | bytes 131072 | tf_op jit(solution)/shard_map/all_to_all | solution.py:349
  102.6 0.7 copy-start.16

commit v7 on v6

--- a/solution.py
+++ b/solution.py
@@ -265,6 +265,7 @@
         out_shape=(packed, packed),
         in_specs=[smem] + [vmem] * 5,
         out_specs=(vmem, vmem),
+        compiler_params=room,
         name="pack",
     )(pos, query_weight, key_weight, value_weight, gate_weight, out_weight)
     beside = shift(send, "core", NC, 1)
@@ -276,6 +277,7 @@
         out_shape=jax.ShapeDtypeStruct((rows, width), BF),
         in_specs=[vmem, vmem],
         out_specs=vmem,
+        compiler_params=room,
         name="norm",
     )(inputs, gain)
     beyond = swap(normed, 1)

time: 111 us -> 111 us (level)
  no operation moved by 1% of the time
where the time goes in v7:
time: 111 us
  starting transfers between devices  40.4 us (36%)
  waiting for transfers between devices  37.8 us (34%)
  Pallas kernels  23.3 us (21%)
  local copies, waits for them, and re-layouts  6.61 us (6%)
  other arithmetic  1.56 us (1%)
    ppermute x6, waiting for transfers between devices, swap(): return lax.ppermute(value, ('th', 'tl'), [(i, i ^ by) for i in range(NT)])  23.9 us
    pallas_call x1, Pallas kernels, on_device(): pl.pallas_call(attention_kernel, out_shape=(jax.ShapeDtypeStruct((width,...  12.6 us
    ppermute x1, starting transfers between devices, on_device(): lax.ppermute(send, ('zh', 'core'), [(0, 3), (3, 0), (1, 2), (2, 1)])  7.82 us
    ppermute x6, starting transfers between devices, swap(): return lax.ppermute(value, ('th', 'tl'), [(i, i ^ by) for i in range(NT)])  7.35 us
    ppermute x8, waiting for transfers between devices, shift(): lax.ppermute(value, axis, [(i, (i + by) % count) for i in range(count)])  6.98 us
    all_to_all x1, starting transfers between devices, on_device(): weights = lax.all_to_all(pieces, ('x', 'y'), 0, 0, tiled=True)  6.94 us
    ppermute x8, starting transfers between devices, shift(): lax.ppermute(value, axis, [(i, (i + by) % count) for i in range(count)])  6.64 us
    all_to_all x1, starting transfers between devices, on_device(): lax.all_to_all(planes.reshape((-1,) + shape[3:]), ('zh', 'core', 'tl'), 0...  6.24 us
  transfers between devices with their start and end apart: 18, of which 8 were waited for; matrix products, arithmetic and copies ran while one was open for 4% of the time, Pallas kernels for 6%

profile of v7, /device:TPU:1, one launch (start us, length us, event | category | flops | bytes accessed | tf_op | source)
XLA Modules:
  0.0 110.5 jit_solution(8912129695301551430)
XLA Ops:
  0.6 1.8 %norm.1.normed = bf16[128,768]{1,0:T(8,128)(2,1)} custom-call(bf16[128,768]{1,0:T(8,128)(2,1)} %bitcast.44, f32[768]{0:T(1024)} %gain.3), custom_call_target="tpu_custom_call" | custom-call | tf_op jit(solution)/shard_map/norm/pallas_call | solution.py:275
  2.5 2.5 %collective-permute-start.3 = (bf16[128,768]{1,0:T(8,128)(2,1)}, bf16[128,768]{1,0:T(8,128)(2,1)S(1)}, u32[]{:S(2)}, u32[]{:S(2)}) collective-permute-start(bf16[128,768]{1,0:T(8,128)(2,1)} %norm.1.normed), channel_id=1, source_target_pairs={{0,1},{1,0},{2,3},{3,2},{4,5},{5,4},{6,7},{7,6},{8,9},{9,8},{10,11... | collective-permute-start | bytes 589832 | tf_op jit(solution)/shard_map/ppermute | solution.py:22
  4.9 0.0 collective-permute-start.4
  5.0 0.7 stack.27.pos
  5.6 2.0 %pack.1 = (bf16[12,1536]{1,0:T(8,128)(2,1)}, bf16[12,1536]{1,0:T(8,128)(2,1)}) custom-call(s32[6]{0:T(128)} %stack.27.pos, bf16[12,768]{1,0:T(8,128)(2,1)} %query.1, bf16[12,768]{1,0:T(8,128)(2,1)} %key.1, bf16[12,768]{1,0:T(8,128)(2,1)} %value.1, bf16[12,768]{1,0:T(8,128)(2,1)} %gate.1, bf16[12,768]{1,0:T(8,128)(2,1)} %out.1), custom_call_target="tpu_custom_call" | custom-call | tf_op jit(solution)/shard_map/pack/pallas_call | solution.py:263
  7.7 7.8 %collective-permute-start.2 = (bf16[12,1536]{1,0:T(8,128)(2,1)}, bf16[12,1536]{1,0:T(8,128)(2,1)S(1)}, u32[]{:S(2)}, u32[]{:S(2)}) collective-permute-start(bf16[12,1536]{1,0:T(8,128)(2,1)} %get-tuple-element.13), channel_id=1, source_target_pairs={{0,36},{36,0},{4,32},{32,4},{1,37},{37,1},{5,33},{33,5},{2,38},{38... | collective-permute-start | bytes 110600 | tf_op jit(solution)/shard_map/ppermute | solution.py:273
  15.5 0.0 collective-permute-start
  15.5 0.2 collective-permute-start.1
  15.7 2.2 %dynamic-slice_bitcast_fusion = (bf16[4,128,512]{2,1,0:T(8,128)(2,1)}, bf16[4,128,512]{2,1,0:T(8,128)(2,1)}) fusion(bf16[4,2,2,128,512]{4,3,2,1,0:T(8,128)(2,1)} %bitcast.46, s32[]{:T(128)S(6)} %select_n.18, s32[]{:T(128)S(6)} %select_n.22, s32[]{:T(128)S(6)} %select_n.20), kind=kLoop, calls=%fused_computation.1 | loop fusion | bytes 2097164 | tf_op jit(solution)/shard_map/jit(dynamic_index_in_dim)/squeeze | solution.py:260
  18.0 5.0 %collective-permute-done.1.above = bf16[12,1536]{1,0:T(8,128)(2,1)S(1)} collective-permute-done((bf16[12,1536]{1,0:T(8,128)(2,1)}, bf16[12,1536]{1,0:T(8,128)(2,1)S(1)}, u32[]{:S(2)}, u32[]{:S(2)}) %collective-permute-start.1) | collective-permute-done | bytes 36896 | tf_op jit(solution)/shard_map/ppermute | solution.py:18
  23.0 0.5 copy-done.19
  23.6 0.0 copy-done.17
  23.6 0.0 copy-done.18
  23.6 0.1 copy-done.15
  23.7 0.1 copy-done.1
  23.8 2.5 %assemble.1 = (bf16[16,48,1152]{2,1,0:T(8,128)(2,1)}, bf16[256,768]{1,0:T(8,128)(2,1)}) custom-call(s32[6]{0:T(128)} %stack.27.pos, bf16[12,1536]{1,0:T(8,128)(2,1)} %get-tuple-element.12.mine, bf16[12,1536]{1,0:T(8,128)(2,1)} %copy-done.18, bf16[12,1536]{1,0:T(8,128)(2,1)} %copy-done.19, bf16[12,1536]{1,0:T(8,128)(2,1)} %copy-done.17, ...), custom_call_target="tpu_custom_call" | custom-call | tf_op jit(solution)/shard_map/assemble/pallas_call | solution.py:286
  26.3 0.0 copy-start.12
  26.3 0.0 copy-start.20
  26.4 6.9 %all-to-all-start = ((bf16[16,48,1152]{2,1,0:T(8,128)(2,1)}), bf16[16,48,1152]{2,1,0:T(8,128)(2,1)}, u32[]{:S(2)}, u32[]{:S(2)}) async-start(bf16[16,48,1152]{2,1,0:T(8,128)(2,1)} %get-tuple-element.15), calls=%async_computation | async-start | bytes 3538944 | tf_op jit(solution)/shard_map/all_to_all | solution.py:298
  33.3 0.9 collective-permute-start.5
  34.3 2.7 %collective-permute-start.10 = (bf16[4,128,512]{2,1,0:T(8,128)(2,1)S(1)}, bf16[4,128,512]{2,1,0:T(8,128)(2,1)S(1)}, u32[]{:S(2)}, u32[]{:S(2)}) collective-permute-start(bf16[4,128,512]{2,1,0:T(8,128)(2,1)S(1)} %copy-done), channel_id=1, source_target_pairs={{0,1},{1,0},{2,3},{3,2},{4,5},{5,4},{6,7},{7,6},{8,9},{9,8},{10,11... | collective-permute-start | bytes 1572872 | tf_op jit(solution)/shard_map/ppermute | solution.py:22
  36.9 1.7 %collective-permute-start.6 = (bf16[256,768]{1,0:T(8,128)(2,1)S(1)}, bf16[256,768]{1,0:T(8,128)(2,1)S(1)}, u32[]{:S(2)}, u32[]{:S(2)}) collective-permute-start(bf16[256,768]{1,0:T(8,128)(2,1)S(1)} %copy-done.5), channel_id=1, source_target_pairs={{0,4},{4,0},{1,5},{5,1},{2,6},{6,2},{3,7},{7,3},{8,12},{12,8},{9,1... | collective-permute-start | bytes 1179656 | tf_op jit(solution)/shard_map/ppermute | solution.py:18
  38.6 14.3 %collective-permute-done.5.own_far = bf16[256,768]{1,0:T(8,128)(2,1)S(1)} collective-permute-done((bf16[256,768]{1,0:T(8,128)(2,1)S(1)}, bf16[256,768]{1,0:T(8,128)(2,1)S(1)}, u32[]{:S(2)}, u32[]{:S(2)}) %collective-permute-start.5) | collective-permute-done | bytes 393248 | tf_op jit(solution)/shard_map/ppermute | solution.py:22
  52.9 1.5 %collective-permute-start.7 = (bf16[256,768]{1,0:T(8,128)(2,1)S(1)}, bf16[256,768]{1,0:T(8,128)(2,1)S(1)}, u32[]{:S(2)}, u32[]{:S(2)}) collective-permute-start(bf16[256,768]{1,0:T(8,128)(2,1)S(1)} %collective-permute-done.5.own_far), channel_id=1, source_target_pairs={{0,4},{4,0},{1,5},{5,1},{2,6},{6,2},{3,7},{7,3},{8,12},{12,8},{9,1... | collective-permute-start | bytes 1179656 | tf_op jit(solution)/shard_map/ppermute | solution.py:18
  54.4 0.1 collective-permute-start.8
  54.5 0.4 collective-permute-start.9
  54.9 0.6 compare_convert_fusion
  55.5 0.5 collective-permute-done.8.cot_oth0
  56.0 0.3 collective-permute-done.9.cot_oth1
  56.3 0.8 copy-done.7
  57.2 0.7 copy-done.8
  57.9 12.6 %attention.1 = (f32[768,128]{1,0:T(8,128)}, f32[768,128]{1,0:T(8,128)}, bf16[2,768,128]{2,1,0:T(8,128)(2,1)}, bf16[2,768,128]{2,1,0:T(8,128)(2,1)}, bf16[2,768,1...) custom-call(s32[6]{0:T(128)} %stack.27.pos, bf16[256,768]{1,0:T(8,128)(2,1)} %get-tuple-element.14.own_near, ...), custom_call_target="tpu_custom_call" | custom-call | tf_op jit(solution)/shard_map/attention/pallas_call | solution.py:306
  70.6 2.2 %collective-permute-start.12 = (bf16[2,768,128]{2,1,0:T(8,128)(2,1)}, bf16[2,768,128]{2,1,0:T(8,128)(2,1)S(1)}, u32[]{:S(2)}, u32[]{:S(2)}) collective-permute-start(bf16[2,768,128]{2,1,0:T(8,128)(2,1)} %get-tuple-element.19), channel_id=1, source_target_pairs={{0,4},{4,0},{1,5},{5,1},{2,6},{6,2},{3,7},{7,3},{8,12},{12,8},{9,1... | collective-permute-start | bytes 1179656 | tf_op jit(solution)/shard_map/ppermute | solution.py:18
  72.8 5.4 %all-to-all-start.1 = ((bf16[16,4,2,16,256]{4,3,2,1,0:T(8,128)(2,1)}), bf16[16,4,2,16,256]{4,3,2,1,0:T(8,128)(2,1)}, u32[]{:S(2)}, u32[]{:S(2)}) async-start(bf16[16,4,2,16,256]{4,3,2,1,0:T(8,128)(2,1)} %get-tuple-element.21), calls=%async_computation.1 | async-start | bytes 2097152 | tf_op jit(solution)/shard_map/all_to_all | solution.py:341
  78.2 0.5 collective-permute-start.11
  78.8 0.1 add_convert_fusion
  78.9 0.1 collective-permute-start.13
  79.0 1.1 %collective-permute-done.11 = bf16[2,768,128]{2,1,0:T(8,128)(2,1)S(1)} collective-permute-done((bf16[2,768,128]{2,1,0:T(8,128)(2,1)S(1)}, bf16[2,768,128]{2,1,0:T(8,128)(2,1)S(1)}, u32[]{:S(2)}, u32[]{:S(2)}) %collective-permute-start.11) | collective-permute-done | bytes 393248 | tf_op jit(solution)/shard_map/ppermute | solution.py:18
  80.1 9.6 %collective-permute-done.13 = bf16[2,768,128]{2,1,0:T(8,128)(2,1)S(1)} collective-permute-done((bf16[2,768,128]{2,1,0:T(8,128)(2,1)S(1)}, bf16[2,768,128]{2,1,0:T(8,128)(2,1)S(1)}, u32[]{:S(2)}, u32[]{:S(2)}) %collective-permute-start.13) | collective-permute-done | bytes 393248 | tf_op jit(solution)/shard_map/ppermute | solution.py:22
  89.7 0.9 fusion
  90.6 1.2 %collective-permute-start.14 = (bf16[768,128]{1,0:T(8,128)(2,1)S(1)}, bf16[768,128]{1,0:T(8,128)(2,1)S(1)}, u32[]{:S(2)}, u32[]{:S(2)}) collective-permute-start(bf16[768,128]{1,0:T(8,128)(2,1)S(1)} %get-tuple-element.24.after), channel_id=1, source_target_pairs={{0,2},{1,3},{2,0},{3,1},{4,6},{5,7},{6,4},{7,5},{8,10},{9,11},{10,... | collective-permute-start | bytes 589832 | tf_op jit(solution)/shard_map/ppermute | solution.py:22
  91.8 2.6 %all-to-all-done.1.parts = bf16[16,4,2,16,256]{4,3,2,1,0:T(8,128)(2,1)} async-done(((bf16[16,4,2,16,256]{4,3,2,1,0:T(8,128)(2,1)}), bf16[16,4,2,16,256]{4,3,2,1,0:T(8,128)(2,1)}, u32[]{:S(2)}, u32[]{:S(2)}) %all-to-all-start.1) | async-done | bytes 1048608 | tf_op jit(solution)/shard_map/all_to_all | solution.py:341
  94.4 2.0 %sum_plane.1 = bf16[2,2,2,4,8,128]{5,4,3,2,1,0:T(8,128)(2,1)} custom-call(s32[6]{0:T(128)} %stack.27.pos, bf16[16,4,2,16,256]{4,3,2,1,0:T(8,128)(2,1)} %all-to-all-done.1.parts, bf16[768,128]{1,0:T(8,128)(2,1)} %copy-done.3), custom_call_target="tpu_custom_call" | custom-call | tf_op jit(solution)/shard_map/sum_plane/pallas_call | solution.py:342
  96.4 6.2 %all-to-all-start.2 = ((bf16[8,4,8,128]{3,2,1,0:T(8,128)(2,1)}), bf16[8,4,8,128]{3,2,1,0:T(8,128)(2,1)S(1)}, u32[]{:S(2)}, u32[]{:S(2)}) async-start(bf16[8,4,8,128]{3,2,1,0:T(8,128)(2,1)} %bitcast.47), calls=%async_computation.2 | async-start | bytes 131072 | tf_op jit(solution)/shard_map/all_to_all | solution.py:351
  102.7 0.7 copy-done.16
  103.3 2.3 %norm_back.1 = bf16[128,768]{1,0:T(8,128)(2,1)} custom-call(bf16[128,768]{1,0:T(8,128)(2,1)} %bitcast.45, f32[768]{0:T(1024)} %gain.3, f32[768,128]{1,0:T(8,128)} %get-tuple-element.25.near, bf16[768,128]{1,0:T(8,128)(2,1)} %copy-done.16), custom_call_target="tpu_custom_call" | custom-call | tf_op jit(solution)/shard_map/norm_back/pallas_call | solution.py:355
  105.6 4.2 %all-to-all-done.2 = bf16[8,4,8,128]{3,2,1,0:T(8,128)(2,1)S(1)} async-done(((bf16[8,4,8,128]{3,2,1,0:T(8,128)(2,1)}), bf16[8,4,8,128]{3,2,1,0:T(8,128)(2,1)S(1)}, u32[]{:S(2)}, u32[]{:S(2)}) %all-to-all-start.2) | async-done | bytes 65568 | tf_op jit(solution)/shard_map/all_to_all | solution.py:351
  109.9 0.6 copy.18
  (45 shorter events, 0.1 us)
Async XLA Ops:
  2.5 20.5 %collective-permute-start.3 = (bf16[128,768]{1,0:T(8,128)(2,1)}, bf16[128,768]{1,0:T(8,128)(2,1)S(1)}, u32[]{:S(2)}, u32[]{:S(2)}) collective-permute-start(bf16[128,768]{1,0:T(8,128)(2,1)} %norm.1.normed), channel_id=1, source_target_pairs={{0,1},{1,0},{2,3},{3,2},{4,5},{5,4},{6,7},{7,6},{8,9},{9,8},{10,11... | collective-permute-start | bytes 589832 | tf_op jit(solution)/shard_map/ppermute | solution.py:22
  4.9 18.1 %collective-permute-start.4 = (bf16[128,768]{1,0:T(8,128)(2,1)}, bf16[128,768]{1,0:T(8,128)(2,1)S(1)}, u32[]{:S(2)}, u32[]{:S(2)}) collective-permute-start(bf16[128,768]{1,0:T(8,128)(2,1)} %bitcast.50), channel_id=1, source_target_pairs={{0,1},{1,0},{2,3},{3,2},{4,5},{5,4},{6,7},{7,6},{8,9},{9,8},{10,11... | collective-permute-start | bytes 589832 | tf_op jit(solution)/shard_map/ppermute | solution.py:22
  7.7 15.3 %collective-permute-start.2 = (bf16[12,1536]{1,0:T(8,128)(2,1)}, bf16[12,1536]{1,0:T(8,128)(2,1)S(1)}, u32[]{:S(2)}, u32[]{:S(2)}) collective-permute-start(bf16[12,1536]{1,0:T(8,128)(2,1)} %get-tuple-element.13), channel_id=1, source_target_pairs={{0,36},{36,0},{4,32},{32,4},{1,37},{37,1},{5,33},{33,5},{2,38},{38... | collective-permute-start | bytes 110600 | tf_op jit(solution)/shard_map/ppermute | solution.py:273
  15.5 7.5 %collective-permute-start = (bf16[12,1536]{1,0:T(8,128)(2,1)}, bf16[12,1536]{1,0:T(8,128)(2,1)S(1)}, u32[]{:S(2)}, u32[]{:S(2)}) collective-permute-start(bf16[12,1536]{1,0:T(8,128)(2,1)} %get-tuple-element.13), channel_id=1, source_target_pairs={{0,4},{4,0},{1,5},{5,1},{2,6},{6,2},{3,7},{7,3},{8,12},{12,8},{9,1... | collective-permute-start | bytes 110600 | tf_op jit(solution)/shard_map/ppermute | solution.py:18
  15.5 7.5 %collective-permute-start.1 = (bf16[12,1536]{1,0:T(8,128)(2,1)}, bf16[12,1536]{1,0:T(8,128)(2,1)S(1)}, u32[]{:S(2)}, u32[]{:S(2)}) collective-permute-start(bf16[12,1536]{1,0:T(8,128)(2,1)} %get-tuple-element.12.mine), channel_id=1, source_target_pairs={{0,32},{32,0},{1,33},{33,1},{2,34},{34,2},{3,35},{35,3},{4,36},{36... | collective-permute-start | bytes 110600 | tf_op jit(solution)/shard_map/ppermute | solution.py:18
  23.0 0.6 copy-start.19
  23.0 0.6 copy-start.17
  23.0 0.6 copy-start.18
  23.0 0.7 copy-start.15
  23.0 0.8 copy-start.1
  26.3 7.0 %copy-start.5 = (bf16[256,768]{1,0:T(8,128)(2,1)S(1)}, bf16[256,768]{1,0:T(8,128)(2,1)}, u32[]{:S(2)}) copy-start(bf16[256,768]{1,0:T(8,128)(2,1)} %get-tuple-element.14.own_near) | copy-start | bytes 1179652
  26.3 7.9 %copy-start = (bf16[4,128,512]{2,1,0:T(8,128)(2,1)S(1)}, bf16[4,128,512]{2,1,0:T(8,128)(2,1)}, u32[]{:S(2)}) copy-start(bf16[4,128,512]{2,1,0:T(8,128)(2,1)} %get-tuple-element.23.ready) | copy-start | bytes 1572868
  26.3 28.1 %copy-start.12 = (bf16[1,128,768]{2,1,0:T(8,128)(2,1)S(1)}, bf16[1,128,768]{2,1,0:T(8,128)(2,1)}, u32[]{:S(2)}) copy-start(bf16[1,128,768]{2,1,0:T(8,128)(2,1)} %param.11) | copy-start | bytes 589828
  26.3 28.1 %copy-start.2 = (bf16[128,768]{1,0:T(8,128)(2,1)S(1)}, bf16[128,768]{1,0:T(8,128)(2,1)}, u32[]{:S(2)}) copy-start(bf16[128,768]{1,0:T(8,128)(2,1)} %copy-done.1) | copy-start | bytes 589828
  26.3 28.5 %copy-start.20 = (s32[512]{0:T(512)S(1)}, s32[512]{0:T(512)}, u32[]{:S(2)}) copy-start(s32[512]{0:T(512)} %param.19) | copy-start | bytes 6148
  26.4 30.8 %all-to-all-start = ((bf16[16,48,1152]{2,1,0:T(8,128)(2,1)}), bf16[16,48,1152]{2,1,0:T(8,128)(2,1)}, u32[]{:S(2)}, u32[]{:S(2)}) async-start(bf16[16,48,1152]{2,1,0:T(8,128)(2,1)} %get-tuple-element.15), calls=%async_computation | async-start | bytes 3538944 | tf_op jit(solution)/shard_map/all_to_all | solution.py:298
  33.3 19.6 %collective-permute-start.5 = (bf16[256,768]{1,0:T(8,128)(2,1)S(1)}, bf16[256,768]{1,0:T(8,128)(2,1)S(1)}, u32[]{:S(2)}, u32[]{:S(2)}) collective-permute-start(bf16[256,768]{1,0:T(8,128)(2,1)S(1)} %copy-done.5), channel_id=1, source_target_pairs={{0,2},{1,3},{2,0},{3,1},{4,6},{5,7},{6,4},{7,5},{8,10},{9,11},{10,... | collective-permute-start | bytes 1179656 | tf_op jit(solution)/shard_map/ppermute | solution.py:22
  34.3 22.0 %collective-permute-start.10 = (bf16[4,128,512]{2,1,0:T(8,128)(2,1)S(1)}, bf16[4,128,512]{2,1,0:T(8,128)(2,1)S(1)}, u32[]{:S(2)}, u32[]{:S(2)}) collective-permute-start(bf16[4,128,512]{2,1,0:T(8,128)(2,1)S(1)} %copy-done), channel_id=1, source_target_pairs={{0,1},{1,0},{2,3},{3,2},{4,5},{5,4},{6,7},{7,6},{8,9},{9,8},{10,11... | collective-permute-start | bytes 1572872 | tf_op jit(solution)/shard_map/ppermute | solution.py:22
  36.9 19.4 %collective-permute-start.6 = (bf16[256,768]{1,0:T(8,128)(2,1)S(1)}, bf16[256,768]{1,0:T(8,128)(2,1)S(1)}, u32[]{:S(2)}, u32[]{:S(2)}) collective-permute-start(bf16[256,768]{1,0:T(8,128)(2,1)S(1)} %copy-done.5), channel_id=1, source_target_pairs={{0,4},{4,0},{1,5},{5,1},{2,6},{6,2},{3,7},{7,3},{8,12},{12,8},{9,1... | collective-permute-start | bytes 1179656 | tf_op jit(solution)/shard_map/ppermute | solution.py:18
  52.9 3.4 %copy-start.6 = (bf16[256,768]{1,0:T(8,128)(2,1)}, bf16[256,768]{1,0:T(8,128)(2,1)S(1)}, u32[]{:S(2)}) copy-start(bf16[256,768]{1,0:T(8,128)(2,1)S(1)} %collective-permute-done.5.own_far) | copy-start | bytes 1179652
  52.9 3.4 %collective-permute-start.7 = (bf16[256,768]{1,0:T(8,128)(2,1)S(1)}, bf16[256,768]{1,0:T(8,128)(2,1)S(1)}, u32[]{:S(2)}, u32[]{:S(2)}) collective-permute-start(bf16[256,768]{1,0:T(8,128)(2,1)S(1)} %collective-permute-done.5.own_far), channel_id=1, source_target_pairs={{0,4},{4,0},{1,5},{5,1},{2,6},{6,2},{3,7},{7,3},{8,12},{12,8},{9,1... | collective-permute-start | bytes 1179656 | tf_op jit(solution)/shard_map/ppermute | solution.py:18
  54.4 1.6 %collective-permute-start.8 = (bf16[128,768]{1,0:T(8,128)(2,1)S(1)}, bf16[128,768]{1,0:T(8,128)(2,1)S(1)}, u32[]{:S(2)}, u32[]{:S(2)}) collective-permute-start(bf16[128,768]{1,0:T(8,128)(2,1)S(1)} %bitcast.52), channel_id=1, source_target_pairs={{0,4},{4,0},{1,5},{5,1},{2,6},{6,2},{3,7},{7,3},{8,12},{12,8},{9,1... | collective-permute-start | bytes 589832 | tf_op jit(solution)/shard_map/ppermute | solution.py:18
  54.5 1.8 %collective-permute-start.9 = (bf16[128,768]{1,0:T(8,128)(2,1)S(1)}, bf16[128,768]{1,0:T(8,128)(2,1)S(1)}, u32[]{:S(2)}, u32[]{:S(2)}) collective-permute-start(bf16[128,768]{1,0:T(8,128)(2,1)S(1)} %copy-done.2), channel_id=1, source_target_pairs={{0,4},{4,0},{1,5},{5,1},{2,6},{6,2},{3,7},{7,3},{8,12},{12,8},{9,1... | collective-permute-start | bytes 589832 | tf_op jit(solution)/shard_map/ppermute | solution.py:18
  56.0 1.9 %copy-start.13 = (bf16[128,768]{1,0:T(8,128)(2,1)}, bf16[128,768]{1,0:T(8,128)(2,1)S(1)}, u32[]{:S(2)}) copy-start(bf16[128,768]{1,0:T(8,128)(2,1)S(1)} %collective-permute-done.8.cot_oth0) | copy-start | bytes 589828
  56.3 1.6 %copy-start.14 = (bf16[128,768]{1,0:T(8,128)(2,1)}, bf16[128,768]{1,0:T(8,128)(2,1)S(1)}, u32[]{:S(2)}) copy-start(bf16[128,768]{1,0:T(8,128)(2,1)S(1)} %collective-permute-done.9.cot_oth1) | copy-start | bytes 589828
  56.3 1.6 %copy-start.4 = (bf16[4,128,512]{2,1,0:T(8,128)(2,1)}, bf16[4,128,512]{2,1,0:T(8,128)(2,1)S(1)}, u32[]{:S(2)}) copy-start(bf16[4,128,512]{2,1,0:T(8,128)(2,1)S(1)} %collective-permute-done.10.bias_pair) | copy-start | bytes 1572868
  56.3 0.9 copy-start.7
  57.2 0.7 copy-start.8
  70.5 7.7 %copy-start.21 = (bf16[2,768,128]{2,1,0:T(8,128)(2,1)S(1)}, bf16[2,768,128]{2,1,0:T(8,128)(2,1)}, u32[]{:S(2)}) copy-start(bf16[2,768,128]{2,1,0:T(8,128)(2,1)} %get-tuple-element.17) | copy-start | bytes 1179652
  70.5 8.2 %copy-start.9 = (bf16[2,768,128]{2,1,0:T(8,128)(2,1)S(1)}, bf16[2,768,128]{2,1,0:T(8,128)(2,1)}, u32[]{:S(2)}) copy-start(bf16[2,768,128]{2,1,0:T(8,128)(2,1)} %get-tuple-element.18) | copy-start | bytes 1179652
  70.5 19.2 %copy-start.10 = (f32[768,128]{1,0:T(8,128)S(1)}, f32[768,128]{1,0:T(8,128)}, u32[]{:S(2)}) copy-start(f32[768,128]{1,0:T(8,128)} %get-tuple-element.16) | copy-start | bytes 1179652
  70.6 19.2 %copy-start.11 = (f32[768,128]{1,0:T(8,128)S(1)}, f32[768,128]{1,0:T(8,128)}, u32[]{:S(2)}) copy-start(f32[768,128]{1,0:T(8,128)} %get-tuple-element.20) | copy-start | bytes 1179652
  70.6 8.2 %collective-permute-start.12 = (bf16[2,768,128]{2,1,0:T(8,128)(2,1)}, bf16[2,768,128]{2,1,0:T(8,128)(2,1)S(1)}, u32[]{:S(2)}, u32[]{:S(2)}) collective-permute-start(bf16[2,768,128]{2,1,0:T(8,128)(2,1)} %get-tuple-element.19), channel_id=1, source_target_pairs={{0,4},{4,0},{1,5},{5,1},{2,6},{6,2},{3,7},{7,3},{8,12},{12,8},{9,1... | collective-permute-start | bytes 1179656 | tf_op jit(solution)/shard_map/ppermute | solution.py:18
  72.8 21.6 %all-to-all-start.1 = ((bf16[16,4,2,16,256]{4,3,2,1,0:T(8,128)(2,1)}), bf16[16,4,2,16,256]{4,3,2,1,0:T(8,128)(2,1)}, u32[]{:S(2)}, u32[]{:S(2)}) async-start(bf16[16,4,2,16,256]{4,3,2,1,0:T(8,128)(2,1)} %get-tuple-element.21), calls=%async_computation.1 | async-start | bytes 2097152 | tf_op jit(solution)/shard_map/all_to_all | solution.py:341
  78.2 1.9 %collective-permute-start.11 = (bf16[2,768,128]{2,1,0:T(8,128)(2,1)S(1)}, bf16[2,768,128]{2,1,0:T(8,128)(2,1)S(1)}, u32[]{:S(2)}, u32[]{:S(2)}) collective-permute-start(bf16[2,768,128]{2,1,0:T(8,128)(2,1)S(1)} %copy-done.21), channel_id=1, source_target_pairs={{0,4},{4,0},{1,5},{5,1},{2,6},{6,2},{3,7},{7,3},{8,12},{12,8},{9,1... | collective-permute-start | bytes 1179656 | tf_op jit(solution)/shard_map/ppermute | solution.py:18
  78.9 10.9 %collective-permute-start.13 = (bf16[2,768,128]{2,1,0:T(8,128)(2,1)S(1)}, bf16[2,768,128]{2,1,0:T(8,128)(2,1)S(1)}, u32[]{:S(2)}, u32[]{:S(2)}) collective-permute-start(bf16[2,768,128]{2,1,0:T(8,128)(2,1)S(1)} %add_convert_fusion), channel_id=1, source_target_pairs={{0,1},{1,0},{2,3},{3,2},{4,5},{5,4},{6,7},{7,6},{8,9},{9,8},{10,11... | collective-permute-start | bytes 1179656 | tf_op jit(solution)/shard_map/ppermute | solution.py:22
  90.6 3.8 %copy-start.3 = (bf16[768,128]{1,0:T(8,128)(2,1)}, bf16[768,128]{1,0:T(8,128)(2,1)S(1)}, u32[]{:S(2)}) copy-start(bf16[768,128]{1,0:T(8,128)(2,1)S(1)} %get-tuple-element.24.after) | copy-start | bytes 589828
  90.6 12.0 %collective-permute-start.14 = (bf16[768,128]{1,0:T(8,128)(2,1)S(1)}, bf16[768,128]{1,0:T(8,128)(2,1)S(1)}, u32[]{:S(2)}, u32[]{:S(2)}) collective-permute-start(bf16[768,128]{1,0:T(8,128)(2,1)S(1)} %get-tuple-element.24.after), channel_id=1, source_target_pairs={{0,2},{1,3},{2,0},{3,1},{4,6},{5,7},{6,4},{7,5},{8,10},{9,11},{10,... | collective-permute-start | bytes 589832 | tf_op jit(solution)/shard_map/ppermute | solution.py:22
  96.4 13.5 %all-to-all-start.2 = ((bf16[8,4,8,128]{3,2,1,0:T(8,128)(2,1)}), bf16[8,4,8,128]{3,2,1,0:T(8,128)(2,1)S(1)}, u32[]{:S(2)}, u32[]{:S(2)}) async-start(bf16[8,4,8,128]{3,2,1,0:T(8,128)(2,1)} %bitcast.47), calls=%async_computation.2 | async-start | bytes 131072 | tf_op jit(solution)/shard_map/all_to_all | solution.py:351
  102.6 0.7 copy-start.16
